TPU v7x, 128 devices: a whole 4x4x4 slice. The times are simulated.
128 devices in a mesh: row: 8 (over y, core), col: 8 (over z, x_hi), smp: 2 (over x_lo).
Axes of the slice: x: 4 (x_hi: 2, x_lo: 2; x = x_hi * 2 + x_lo), y: 4, z: 4, core: 2. Of those that a mesh axis runs over, the one named last changes fastest.
Arguments:
- token_act: bfloat16 [8, 2048, 768], P('smp', ('row', 'col')), may hold values from -9 to 9
- pair_rep: bfloat16 [2048, 2048, 128], P('row', 'col'), may hold values from -4 to 402
- norm_gain: float32 [768], replicated, may hold values from 0.1 to 1.9
- w_pair: bfloat16 [128, 16], replicated, may hold values from -1 to 1
- w_query: bfloat16 [768, 768], P(None, 'col'), may hold values from -0.21875 to 0.21875
- w_key: bfloat16 [768, 768], P(None, 'col'), may hold values from -0.21875 to 0.21875
- w_value: bfloat16 [768, 768], P(None, 'col'), may hold values from -0.21875 to 0.21875
- w_gate: bfloat16 [768, 768], P(None, 'col'), may hold values from -0.21875 to 0.21875
- w_out: bfloat16 [768, 768], P('col'), may hold values from -0.21875 to 0.21875
- grad_out: bfloat16 [8, 2048, 768], P('smp', ('row', 'col')), may hold values from -6 to 6
Outputs:
- block_out: bfloat16 [8, 2048, 768], P('smp', ('row', 'col'))
- grad_act: bfloat16 [8, 2048, 768], P('smp', ('row', 'col'))
- grad_query: float32 [768, 768], P(None, 'col')
- grad_key: float32 [768, 768], P(None, 'col')
- grad_value: float32 [768, 768], P(None, 'col')
- grad_gate: float32 [768, 768], P(None, 'col')
- grad_wout: float32 [768, 768], P('col')
- grad_wpair: float32 [128, 16], replicated
- grad_gain: float32 [768], replicated
All inputs are finite; a program needn't handle non-finite values.
Results may differ from a plain program's by a relative error of at most 0.019.
Values may be sent and summed in bfloat16 or wider, within the bound.
No kernel may reach another device: no remote copies, remote signals or barrier semaphores. Data moves between devices by JAX's collectives and lax.ppermute only.
A program may use at most 576 MiB of HBM per device.

v0:
```python
import math

import jax
import jax.numpy as jnp
from jax import lax
from jax.sharding import PartitionSpec as P

EPSILON = 1e-05


def normalize(token_act, norm_gain):
    values_f = token_act.astype(jnp.float32)
    centred = values_f - jnp.mean(values_f, axis=-1, keepdims=True)
    inv_std = lax.rsqrt(jnp.mean(centred * centred, axis=-1, keepdims=True) + EPSILON)
    normed = centred * inv_std
    return ((normed * norm_gain).astype(jnp.bfloat16), normed, inv_std)


def normalize_back(grad_norm, normed, inv_std, norm_gain):
    grad_hat = grad_norm * norm_gain
    return inv_std * (
        grad_hat
        - jnp.mean(grad_hat, axis=-1, keepdims=True)
        - normed * jnp.mean(grad_hat * normed, axis=-1, keepdims=True)
    )


def attend(query_s, key_s, value_s, gate_s, bias, score_scale):
    head_count = bias.shape[0]
    row_count = query_s.shape[0]
    key_count = key_s.shape[0]
    head_dim = query_s.shape[1] // head_count
    query_h = query_s.reshape(row_count, head_count, head_dim)
    key_h = key_s.reshape(key_count, head_count, head_dim)
    value_h = value_s.reshape(key_count, head_count, head_dim)
    scores = (
        jnp.einsum("ihd,jhd->hij", query_h, key_h, preferred_element_type=jnp.float32) * score_scale
        + bias
    )
    peak = jnp.max(scores, axis=-1, keepdims=True)
    expo = jnp.exp(scores - peak)
    probs = expo / jnp.sum(expo, axis=-1, keepdims=True)
    probs_bf = probs.astype(jnp.bfloat16)
    attended = jnp.einsum("hij,jhd->ihd", probs_bf, value_h, preferred_element_type=jnp.float32)
    attended = attended.reshape(row_count, head_count * head_dim)
    gate_sig = jax.nn.sigmoid(gate_s.astype(jnp.float32))
    return (probs, probs_bf, attended, gate_sig, query_h, key_h, value_h)


def pair_contract(pair_rows, grad_rows):
    row_count = pair_rows.shape[0]
    block = math.gcd(row_count, 32)
    pair_blocks = pair_rows.reshape(
        row_count // block, block, pair_rows.shape[1], pair_rows.shape[2]
    )
    grad_blocks = jnp.moveaxis(
        grad_rows.reshape(grad_rows.shape[0], row_count // block, block, grad_rows.shape[2]), 1, 0
    )

    def add_block(total, pieces):
        pair_piece, grad_piece = pieces
        return (
            total
            + jnp.einsum(
                "ijc,hij->ch",
                pair_piece.astype(jnp.float32),
                grad_piece,
                precision=lax.Precision.HIGHEST,
            ),
            None,
        )

    start_total = jnp.zeros((pair_rows.shape[2], grad_rows.shape[0]), jnp.float32)
    result, _ = lax.scan(add_block, start_total, (pair_blocks, grad_blocks))
    return result


def on_device(
    token_act, pair_rep, norm_gain, w_pair, w_query, w_key, w_value, w_gate, w_out, grad_out
):
    samples, local_len, width = token_act.shape
    heads = w_pair.shape[1]
    head_dim = width // heads
    score_scale = 1.0 / math.sqrt(head_dim)
    token_norm, normed, inv_std = normalize(token_act, norm_gain)
    bias_tile = jnp.einsum("ijc,ch->hij", pair_rep, w_pair, preferred_element_type=jnp.float32)
    bias = lax.all_to_all(bias_tile, "col", split_axis=0, concat_axis=2, tiled=True)
    rows_in = lax.all_gather(token_norm, "col", axis=1, tiled=True)
    weight_cat = jnp.concatenate([w_query, w_key, w_value, w_gate], axis=1)
    projected = jnp.einsum(
        "stc,cf->stf", rows_in, weight_cat, preferred_element_type=jnp.float32
    ).astype(jnp.bfloat16)
    queries, keys_own, values_own, gates = jnp.split(projected, 4, axis=2)
    keys_all, values_all = (
        lax.all_gather(keys_own, "row", axis=1, tiled=True),
        lax.all_gather(values_own, "row", axis=1, tiled=True),
    )

    def forward_one(inputs):
        query_s, key_s, value_s, gate_s = inputs
        parts = attend(query_s, key_s, value_s, gate_s, bias, score_scale)
        return (parts[3] * parts[2]).astype(jnp.bfloat16)

    gated = lax.map(forward_one, (queries, keys_all, values_all, gates))
    out_part = jnp.einsum("stf,fc->stc", gated, w_out, preferred_element_type=jnp.float32)
    out_sum = lax.psum_scatter(out_part, "col", scatter_dimension=1, tiled=True)
    grad_rows = lax.all_gather(grad_out, "col", axis=1, tiled=True)
    grad_gated = jnp.einsum(
        "stc,fc->stf", grad_rows, w_out, preferred_element_type=jnp.float32
    ).astype(jnp.bfloat16)
    grad_wout = jnp.einsum("stf,stc->fc", gated, grad_rows, preferred_element_type=jnp.float32)
    block_out = (token_act.astype(jnp.float32) + out_sum).astype(jnp.bfloat16)

    def backward_one(grad_bias, inputs):
        query_s, key_s, value_s, gate_s, cot_s = inputs
        probs, probs_bf, attended, gate_sig, query_h, key_h, value_h = attend(
            query_s, key_s, value_s, gate_s, bias, score_scale
        )
        row_count = query_s.shape[0]
        key_count = key_s.shape[0]
        grad_gf = cot_s.astype(jnp.float32)
        grad_att = (grad_gf * gate_sig).astype(jnp.bfloat16)
        grad_gpre = (grad_gf * attended * gate_sig * (1.0 - gate_sig)).astype(jnp.bfloat16)
        grad_ah = grad_att.reshape(query_h.shape)
        grad_probs = jnp.einsum(
            "ihd,jhd->hij", grad_ah, value_h, preferred_element_type=jnp.float32
        )
        row_dot = jnp.sum(probs * grad_probs, axis=-1, keepdims=True)
        grad_scores = (probs * (grad_probs - row_dot)).astype(jnp.bfloat16)
        grad_q = (
            jnp.einsum("hij,jhd->ihd", grad_scores, key_h, preferred_element_type=jnp.float32)
            * score_scale
        )
        grad_q = grad_q.astype(jnp.bfloat16).reshape(row_count, query_s.shape[1])
        grad_k = (
            jnp.einsum("hij,ihd->jhd", grad_scores, query_h, preferred_element_type=jnp.float32)
            * score_scale
        )
        grad_v = jnp.einsum("hij,ihd->jhd", probs_bf, grad_ah, preferred_element_type=jnp.float32)
        outputs = (
            grad_q,
            grad_k.reshape(key_count, key_s.shape[1]),
            grad_v.reshape(key_count, key_s.shape[1]),
            grad_gpre,
        )
        return (grad_bias + grad_scores.astype(jnp.float32), outputs)

    bias_start = jnp.zeros(bias.shape, jnp.float32)
    grad_bias, stacked = lax.scan(
        backward_one, bias_start, (queries, keys_all, values_all, gates, grad_gated)
    )
    grad_q, grad_k_part, grad_v_part, grad_gpre = stacked
    grad_k_sum, grad_v_sum = (
        lax.psum_scatter(grad_k_part, "row", scatter_dimension=1, tiled=True),
        lax.psum_scatter(grad_v_part, "row", scatter_dimension=1, tiled=True),
    )
    grad_k = grad_k_sum.astype(jnp.bfloat16)
    grad_v = grad_v_sum.astype(jnp.bfloat16)
    grad_cat = jnp.concatenate([grad_q, grad_k, grad_v, grad_gpre], axis=2)
    weight_cat_grad = jnp.einsum(
        "stc,stf->cf", rows_in, grad_cat, preferred_element_type=jnp.float32
    )
    query_grad, key_grad, value_grad, gate_grad = jnp.split(weight_cat_grad, 4, axis=1)
    norm_part = jnp.einsum("stf,cf->stc", grad_cat, weight_cat, preferred_element_type=jnp.float32)
    grad_norm = lax.psum_scatter(norm_part, "col", scatter_dimension=1, tiled=True)
    grad_query, grad_key, grad_value, grad_gate, grad_wout = lax.psum(
        (query_grad, key_grad, value_grad, gate_grad, grad_wout), ("row", "smp")
    )
    grad_tile = lax.all_to_all(grad_bias, "col", split_axis=2, concat_axis=0, tiled=True)
    wpair_part = pair_contract(pair_rep, grad_tile)
    gain_part = jnp.sum(grad_norm * normed, axis=(0, 1))
    grad_wpair, grad_gain = lax.psum((wpair_part, gain_part), ("row", "col", "smp"))
    grad_act = (
        grad_out.astype(jnp.float32) + normalize_back(grad_norm, normed, inv_std, norm_gain)
    ).astype(jnp.bfloat16)
    return (
        block_out,
        grad_act,
        grad_query,
        grad_key,
        grad_value,
        grad_gate,
        grad_wout,
        grad_wpair,
        grad_gain,
    )


def solution(mesh):
    placed = (
        P("smp", ("row", "col"), None),
        P("row", "col", None),
        P(),
        P(),
        P(None, "col"),
        P(None, "col"),
        P(None, "col"),
        P(None, "col"),
        P("col", None),
        P("smp", ("row", "col"), None),
    )
    return jax.shard_map(
        on_device,
        mesh=mesh,
        in_specs=placed,
        out_specs=(
            P("smp", ("row", "col"), None),
            P("smp", ("row", "col"), None),
            P(None, "col"),
            P(None, "col"),
            P(None, "col"),
            P(None, "col"),
            P("col", None),
            P(),
            P(),
        ),
        check_vma=False,
    )
```

profile of v0, /device:TPU:1, one launch (start us, length us, event | category | flops | bytes accessed | tf_op | source)
XLA Modules:
  0.0 746.0 jit_solution(12706706181012490678)
XLA Ops:
  17.2 47.2 %all-gather.5.cloned.1.call-done = bf16[4,256,768]{2,1,0:T(8,128)(2,1)} async-done(((bf16[4,32,768]{2,1,0:T(8,128)(2,1)}), bf16[4,256,768]{2,1,0:T(8,128)(2,1)}) %all-gather.5.cloned.1.call-update) | async-done | bytes 1572880 | tf_op jit(solution)/shard_map/all_gather | solution.py:88
  68.1 12.3 %fusion.45 = f32[16,256,256]{2,0,1:T(8,128)} fusion(bf16[256,256,128]{2,1,0:T(8,128)(2,1)} %param.17, bf16[128,16]{0,1:T(8,128)(2,1)S(1)} %copy-done.32), kind=kOutput, calls=%fused_computation.77 | convolution fusion | flops 268435456 | bytes 20975616 | tf_op jit(solution)/shard_map/ijc,ch->hij/dot_general | solution.py:86
  80.4 6.6 copy.42
  94.0 49.7 %all-gather.11.cloned.1.call-done = bf16[4,256,768]{2,1,0:T(8,128)(2,1)} async-done(((bf16[4,32,768]{2,1,0:T(8,128)(2,1)}), bf16[4,256,768]{2,1,0:T(8,128)(2,1)}) %all-gather.11.cloned.1.call-update) | async-done | bytes 1572880 | tf_op jit(solution)/shard_map/all_gather | solution.py:107
  154.6 20.5 %all-gather.9.cloned.1.call-done = bf16[4,2048,96]{2,1,0:T(8,128)(2,1)} async-done(((bf16[4,256,96]{2,1,0:T(8,128)(2,1)}), bf16[4,2048,96]{2,1,0:T(8,128)(2,1)}) %all-gather.9.cloned.1.call-update) | async-done | bytes 1572880 | tf_op jit(solution)/shard_map/all_gather | solution.py:95
  177.9 24.8 %all-gather.7.cloned.1.call-done = bf16[4,2048,96]{2,1,0:T(8,128)(2,1)} async-done(((bf16[4,256,96]{2,1,0:T(8,128)(2,1)}), bf16[4,2048,96]{2,1,0:T(8,128)(2,1)}) %all-gather.7.cloned.1.call-update) | async-done | bytes 1572880 | tf_op jit(solution)/shard_map/all_gather | solution.py:96
  208.0 115.0 %while.41 = (s32[]{:T(128)}, f32[2,256,2048]{2,1,0:T(8,128)}, bf16[4,256,96]{1,2,0:T(8,128)(2,1)}, f32[4,2048,96]{1,2,0:T(8,128)}, f32[4,2048,96]{1,2,0:T(8,128)...) while((s32[]{:T(128)}, f32[2,256,2048]{2,1,0:T(8,128)}, ...), condition=%wide.region_11.12_spmd.clone, body=%wide.region_7.11_spmd.clone.sunk | while | flops 625498624 | bytes 134117688 | solution.py:149
  322.9 4.9 copy.52
  327.9 5.0 copy.53
  333.4 29.3 %reduce-scatter.7.cloned.1.call-done = f32[4,256,96]{2,1,0:T(8,128)} async-done(((f32[4,2048,96]{2,1,0:T(8,128)}), f32[4,256,96]{2,1,0:T(8,128)}) %reduce-scatter.7.cloned.1.call-update) | async-done | bytes 393232 | tf_op jit(solution)/shard_map/reduce_scatter | solution.py:154
  363.8 37.9 %reduce-scatter.9.cloned.1.call-done = f32[4,256,96]{2,1,0:T(8,128)} async-done(((f32[4,2048,96]{2,1,0:T(8,128)}), f32[4,256,96]{2,1,0:T(8,128)}) %reduce-scatter.9.cloned.1.call-update) | async-done | bytes 393232 | tf_op jit(solution)/shard_map/reduce_scatter | solution.py:155
  407.3 53.7 %while.40 = (s32[]{:T(128)}, bf16[4,256,96]{1,2,0:T(8,128)(2,1)S(1)}, bf16[4,256,96]{1,2,0:T(8,128)(2,1)}, bf16[4,2048,96]{1,2,0:T(8,128)(2,1)}, bf16[4,256,96]{...) while((s32[]{:T(128)}, bf16[4,256,96]{1,2,0:T(8,128)(2,1)S(1)}, ...), condition=%wide.region_5.6_spmd, body=%wide.region_2.5_spmd.sunk | while | flops 208818688 | bytes 36360324 | solution.py:104
  415.0 4.9 fusion.115
  428.3 4.9 fusion.115
  441.7 5.1 fusion.115
  455.3 4.9 fusion.115
  463.3 7.3 copy.57
  470.6 6.9 all-to-all-start.1
  478.6 46.7 %all-to-all-done.1 = f32[2,256,2048]{1,0,2:T(2,128)} async-done(((f32[2,256,2048]{1,0,2:T(2,128)}), f32[2,256,2048]{1,0,2:T(2,128)}, u32[]{:S(2)}, u32[]{:S(2)}) %all-to-all-start.1) | async-done | bytes 4194336 | tf_op jit(solution)/shard_map/all_to_all | solution.py:169
  525.3 9.3 %copy.58 = f32[8,2,256,256]{3,1,0,2:T(2,128)} copy(f32[8,2,256,256]{2,1,3,0:T(2,128)} %bitcast.14) | data formatting | bytes 8388608 | tf_op jit(solution)/shard_map/all_to_all | solution.py:169
  534.6 6.2 reshape.100
  543.3 21.6 %while.42 = (s32[]{:T(128)}, f32[128,16]{0,1:T(8,128)S(1)}, bf16[8,32,256,128]{3,2,1,0:T(8,128)(2,1)}, f32[8,16,32,256]{3,1,2,0:T(8,128)}, s32[]{:T(128)}, /*index=5*/s32[]{:T(128)}) while((s32[]{:T(128)}, f32[128,16]{0,1:T(8,128)S(1)}, bf16[8,32,256,128]{3,2,1,0:T(8,128)(2,1)}, f32[8,16,32,256]{3,1,2,0:T(8,128)}, s32[]{:T(128)}, ...), condition=%wide.region_23.24_spmd.clone, body=%wide.region_22.23_spmd.clone.sunk | while | flops 201330688 | bytes 2639446 | solution.py:74
  566.2 72.7 %all-reduce = (f32[128,16]{0,1:T(8,128)}, f32[768]{0:T(1024)}) all-reduce(f32[128,16]{0,1:T(8,128)S(1)} %get-tuple-element.140, f32[768]{0:T(1024)S(1)} %get-tuple-element.233), channel_id=1, replica_groups=mesh['row'=8,'col'=8,'smp'=2] {'row','col','smp'}, use_global_device_ids=true, to_apply=%region_24.25 | all-reduce | flops 2816 | bytes 22528 | tf_op jit(solution)/shard_map/psum | solution.py:172
  641.0 90.0 %all-reduce.4.cloned.1.call-done = (f32[768,96]{0,1:T(8,128)}, f32[768,96]{0,1:T(8,128)}, f32[768,96]{0,1:T(8,128)}, f32[768,96]{0,1:T(8,128)}, f32[96,768]{1,0:T(8,128)}) async-done(((f32[768,96]{0,1:T(8,128)}, f32[768,96]{0,1:T(8,128)}, f32[768,96]{0,1:T(8,128)}, f32[768,96]{0,1:T(8,128)}, f32[96,768]{1,0:T(8,128)}), (f32[768,96]{0,1:T(8,128)}, f32[768,96]{0,1:T(8,128)}, f32[768,96]{0,1:T(8,128)}, ...) | async-done | bytes 1474576 | tf_op jit(solution)/shard_map/psum | solution.py:166
  (251 shorter events, 234.0 us)
Async XLA Ops:
  7.2 136.5 %copy-start = (bf16[96,768]{1,0:T(8,128)(2,1)S(1)}, bf16[96,768]{1,0:T(8,128)(2,1)}, u32[]{:S(2)}) copy-start(bf16[96,768]{1,0:T(8,128)(2,1)} %param.24) | copy-start | bytes 442372
  7.2 57.3 %all-gather.5.cloned.1.call-start = ((), (), s32[]{:S(2)}) async-start(), calls=%async_computation.6 | async-start | bytes 1769472 | tf_op jit(solution)/shard_map/all_gather | solution.py:88
  11.8 131.9 %all-gather.11.cloned.1.call-start = ((), (), s32[]{:S(2)}) async-start(), calls=%async_computation.10 | async-start | bytes 1769472 | tf_op jit(solution)/shard_map/all_gather | solution.py:107
  12.6 162.5 %all-gather.9.cloned.1.call-start = ((), (), s32[]{:S(2)}) async-start(), calls=%async_computation.8 | async-start | bytes 2359296 | tf_op jit(solution)/shard_map/all_gather | solution.py:95
  13.7 50.7 %copy-start.20 = (bf16[768,96]{1,0:T(8,128)(2,1)}, bf16[768,96]{1,0:T(8,128)(2,1)S(1)}, u32[]{:S(2)}) copy-start(bf16[768,96]{1,0:T(8,128)(2,1)S(1)} %copy.38) | copy-start | bytes 442372
  13.7 54.4 %copy-start.32 = (bf16[128,16]{0,1:T(8,128)(2,1)S(1)}, bf16[128,16]{0,1:T(8,128)(2,1)}, u32[]{:S(2)}) copy-start(bf16[128,16]{0,1:T(8,128)(2,1)} %param.19) | copy-start | bytes 12292
  14.9 49.6 %copy-start.22 = (bf16[768,96]{1,0:T(8,128)(2,1)}, bf16[768,96]{1,0:T(8,128)(2,1)S(1)}, u32[]{:S(2)}) copy-start(bf16[768,96]{1,0:T(8,128)(2,1)S(1)} %copy.39) | copy-start | bytes 442372
  16.1 48.4 %copy-start.24 = (bf16[768,96]{1,0:T(8,128)(2,1)}, bf16[768,96]{1,0:T(8,128)(2,1)S(1)}, u32[]{:S(2)}) copy-start(bf16[768,96]{1,0:T(8,128)(2,1)S(1)} %copy.40) | copy-start | bytes 442372
  17.2 63.2 %copy-start.26 = (bf16[768,96]{1,0:T(8,128)(2,1)}, bf16[768,96]{1,0:T(8,128)(2,1)S(1)}, u32[]{:S(2)}) copy-start(bf16[768,96]{1,0:T(8,128)(2,1)S(1)} %copy.41) | copy-start | bytes 442372
  87.0 62.9 %all-to-all-start = ((f32[16,256,256]{2,1,0:T(8,128)}), f32[16,256,256]{2,1,0:T(8,128)}, u32[]{:S(2)}, u32[]{:S(2)}) async-start(f32[16,256,256]{2,1,0:T(8,128)} %copy.42), calls=%async_computation | async-start | bytes 8388608 | tf_op jit(solution)/shard_map/all_to_all | solution.py:87
  91.6 111.1 %all-gather.7.cloned.1.call-start = ((), (), s32[]{:S(2)}) async-start(), calls=%async_computation.7 | async-start | bytes 2359296 | tf_op jit(solution)/shard_map/all_gather | solution.py:96
  92.2 270.6 %reduce-scatter.7.cloned.1.call-start = ((), (), s32[]{:S(2)}) async-start(), calls=%async_computation.11 | async-start | bytes 4718592 | tf_op jit(solution)/shard_map/reduce_scatter | solution.py:154
  327.9 73.9 %reduce-scatter.9.cloned.1.call-start = ((), (), s32[]{:S(2)}) async-start(), calls=%async_computation.12 | async-start | bytes 4718592 | tf_op jit(solution)/shard_map/reduce_scatter | solution.py:155
  332.9 69.9 %copy-start.21 = (bf16[768,96]{1,0:T(8,128)(2,1)S(1)}, bf16[768,96]{1,0:T(8,128)(2,1)}, u32[]{:S(2)}) copy-start(bf16[768,96]{1,0:T(8,128)(2,1)} %copy-done.20) | copy-start | bytes 442372
  332.9 69.9 %copy-start.23 = (bf16[768,96]{1,0:T(8,128)(2,1)S(1)}, bf16[768,96]{1,0:T(8,128)(2,1)}, u32[]{:S(2)}) copy-start(bf16[768,96]{1,0:T(8,128)(2,1)} %copy-done.22) | copy-start | bytes 442372
  332.9 69.9 %copy-start.25 = (bf16[768,96]{1,0:T(8,128)(2,1)S(1)}, bf16[768,96]{1,0:T(8,128)(2,1)}, u32[]{:S(2)}) copy-start(bf16[768,96]{1,0:T(8,128)(2,1)} %copy-done.24) | copy-start | bytes 442372
  333.0 231.9 %reduce-scatter.11.cloned.1.call-start = ((), (), s32[]{:S(2)}) async-start(), calls=%async_computation.13 | async-start | bytes 3538944 | tf_op jit(solution)/shard_map/reduce_scatter | solution.py:165
  333.2 73.8 %copy-start.16 = (bf16[4,256,96]{2,1,0:T(8,128)(2,1)}, bf16[4,256,96]{2,1,0:T(8,128)(2,1)S(1)}, u32[]{:S(2)}) copy-start(bf16[4,256,96]{2,1,0:T(8,128)(2,1)S(1)} %copy.55) | copy-start | bytes 589828
  333.4 73.6 %copy-start.18 = (bf16[4,256,96]{2,1,0:T(8,128)(2,1)}, bf16[4,256,96]{2,1,0:T(8,128)(2,1)S(1)}, u32[]{:S(2)}) copy-start(bf16[4,256,96]{2,1,0:T(8,128)(2,1)S(1)} %copy.54) | copy-start | bytes 589828
  363.8 43.2 %copy-start.12 = (bf16[4,256,96]{2,1,0:T(8,128)(2,1)}, bf16[4,256,96]{2,1,0:T(8,128)(2,1)S(1)}, u32[]{:S(2)}) copy-start(bf16[4,256,96]{2,1,0:T(8,128)(2,1)S(1)} %convert_element_type.85) | copy-start | bytes 589828
  407.0 231.9 %reduce-scatter.5.cloned.1.call-start = ((), (), s32[]{:S(2)}) async-start(), calls=%async_computation.9 | async-start | bytes 3538944 | tf_op jit(solution)/shard_map/reduce_scatter | solution.py:106
  470.6 54.7 %all-to-all-start.1 = ((f32[2,256,2048]{1,0,2:T(2,128)}), f32[2,256,2048]{1,0,2:T(2,128)}, u32[]{:S(2)}, u32[]{:S(2)}) async-start(f32[2,256,2048]{1,0,2:T(2,128)} %copy.57), calls=%async_computation.5 | async-start | bytes 8388608 | tf_op jit(solution)/shard_map/all_to_all | solution.py:169
  477.4 253.5 %all-reduce.4.cloned.1.call-start = ((), (), s32[]{:S(2)}) async-start(), calls=%async_computation.14 | async-start | bytes 2949120 | tf_op jit(solution)/shard_map/psum | solution.py:166
  543.3 95.6 %copy-start.9 = (bf16[4,32,768]{2,1,0:T(8,128)(2,1)S(1)}, bf16[4,32,768]{2,1,0:T(8,128)(2,1)}, u32[]{:S(2)}) copy-start(bf16[4,32,768]{2,1,0:T(8,128)(2,1)} %param.25) | copy-start | bytes 589828
  (39 other events, 236.0 us)
Sparse Core Ops, SparseCore 0:
  12.0 52.4 all-gather.4
  66.8 76.8 all-gather.10
  146.0 29.0 all-gather.8
  177.2 25.4 all-gather.6
  328.0 34.7 reduce-scatter.6
  365.0 36.6 reduce-scatter.8
  407.1 81.8 reduce-scatter.10
  492.9 106.7 reduce-scatter.4
  603.2 127.7 all-reduce.3
where the time goes:
time: 750 us; the launch traced here: 746 us
  waiting for transfers between devices  351 us (47%)
  matrix products  148 us (20%)
  local copies, waits for them, and re-layouts  109 us (15%)
  blocking collectives  72.7 us (10%)
  other arithmetic  38 us (5%)
  between operations  14.4 us (2%)
  starting transfers between devices  12.2 us (2%)
    psum x1, waiting for transfers between devices, on_device(): lax.psum((query_grad, key_grad, value_grad, gate_grad, grad_wout), ('row'...  90 us
    psum x1, blocking collectives, on_device(): lax.psum((wpair_part, gain_part), ('row', 'col', 'smp'))  72.7 us
    all_gather x1, waiting for transfers between devices, on_device(): grad_rows = lax.all_gather(grad_out, 'col', axis=1, tiled=True)  49.7 us
    all_gather x1, waiting for transfers between devices, on_device(): rows_in = lax.all_gather(token_norm, 'col', axis=1, tiled=True)  47.2 us
    all_to_all x1, waiting for transfers between devices, on_device(): lax.all_to_all(grad_bias, 'col', split_axis=2, concat_axis=0, tiled=True)  46.7 us
    dot_general x8, matrix products, attend(): jnp.einsum('hij,jhd->ihd', probs_bf, value_h, preferred_element_type=jnp....  39.2 us
    reduce_scatter x1, waiting for transfers between devices, on_device(): lax.psum_scatter(grad_v_part, 'row', scatter_dimension=1, tiled=True)  37.9 us
    reduce_scatter x1, waiting for transfers between devices, on_device(): lax.psum_scatter(grad_k_part, 'row', scatter_dimension=1, tiled=True)  29.3 us
  transfers between devices with their start and end apart: 11, of which 9 were waited for; matrix products, arithmetic and copies ran while one was open for 19% of the time, Pallas kernels for 0%

commit v1 on v0

v1 whole, which is shorter than its diff:
```python
import functools
import math

import jax
import jax.numpy as jnp
from jax import lax
from jax.experimental import pallas as pl
from jax.experimental.pallas import tpu as pltpu
from jax.sharding import Mesh, PartitionSpec as P

EPSILON = 1e-05
BF = jnp.bfloat16
F32 = jnp.float32
HD = 48
COL = ("z", "xh")
ROW = ("y", "core")
GROUP = ("y", "core", "smp")

NT = (((1,), (1,)), ((), ()))
NN = (((1,), (0,)), ((), ()))
TN = (((0,), (0,)), ((), ()))


def mm(a, b, dims):
    return lax.dot_general(a, b, dims, preferred_element_type=F32)


BIAS_ROWS = 2 * 256 + 16


def bias_kernel(w_ref, pair_ref, out_ref, acc_ref):
    heads, rows, keys = acc_ref.shape
    for block in range(rows // 16):
        piece = jnp.concatenate([pair_ref[block * 16 + k] for k in range(16)], axis=1)
        res = mm(w_ref[...], piece, NT)
        acc_ref[:, block * 16 : (block + 1) * 16, :] = res.reshape(heads, 16, keys)
    row_id = lax.broadcasted_iota(jnp.int32, (16, rows), 0)
    for group in range(heads // 2):
        tops = jnp.zeros((16, rows), F32)
        for half in range(2):
            tile = acc_ref[group * 2 + half].T
            top = jnp.max(tile, axis=0, keepdims=True)
            out_ref[group, half * keys : (half + 1) * keys, :] = (tile - top).astype(BF)
            one = top.astype(BF).astype(F32)
            two = (top - one).astype(BF).astype(F32)
            for k, term in enumerate((one, two, top - one - two)):
                tops = jnp.where(row_id == half * 3 + k, term, tops)
        out_ref[group, 2 * keys :, :] = tops.astype(BF)


def pair_bias(pair, w_pair):
    rows, keys, chans = pair.shape
    heads = w_pair.shape[1]
    eye = jnp.eye(16, dtype=BF)
    spread = (w_pair.T[:, None, None, :] * eye[None, :, :, None]).reshape(heads * 16, 16 * chans)
    step = 128
    return pl.pallas_call(
        bias_kernel,
        grid=(rows // step,),
        in_specs=[
            pl.BlockSpec(spread.shape, lambda i: (0, 0)),
            pl.BlockSpec((step, keys, chans), lambda i: (i, 0, 0)),
        ],
        out_specs=pl.BlockSpec((heads // 2, BIAS_ROWS, step), lambda i: (0, 0, i)),
        out_shape=jax.ShapeDtypeStruct((heads // 2, BIAS_ROWS, rows), BF),
        scratch_shapes=[pltpu.VMEM((heads, step, keys), F32)],
        compiler_params=pltpu.CompilerParams(vmem_limit_bytes=44 * 2**20),
        cost_estimate=pl.CostEstimate(flops=2**32, bytes_accessed=20 * 2**20, transcendentals=0),
        name="pair_bias",
    )(spread, pair)


def project_kernel(rows_ref, wq_ref, wk_ref, wv_ref, wg_ref, q_ref, kv_ref, g_ref):
    rows = rows_ref[:, 0].reshape(256, rows_ref.shape[-1])
    q_ref[0] = mm(wq_ref[...], rows, NT).astype(BF)
    g_ref[0] = mm(wg_ref[...], rows, NT).astype(BF)
    keys = mm(wk_ref[...], rows, NT).astype(BF)
    values = mm(wv_ref[...], rows, NT).astype(BF)
    for h in range(2):
        kv_ref[0, h, :HD, :] = keys[h * HD : (h + 1) * HD, :]
        kv_ref[0, h, HD:, :] = values[h * HD : (h + 1) * HD, :]


def project(rows_in, wq, wk, wv, wg):
    cols, samples, local, width = rows_in.shape
    feat = wq.shape[0]
    tok = cols * local
    wspec = pl.BlockSpec((feat, width), lambda s: (0, 0))
    small = jax.ShapeDtypeStruct((samples, feat, tok), BF)
    small_spec = pl.BlockSpec((1, feat, tok), lambda s: (s, 0, 0))
    return pl.pallas_call(
        project_kernel,
        grid=(samples,),
        in_specs=[pl.BlockSpec((cols, 1, local, width), lambda s: (0, s, 0, 0))] + [wspec] * 4,
        out_specs=[small_spec, pl.BlockSpec((1, 2, feat, tok), lambda s: (s, 0, 0, 0)), small_spec],
        out_shape=[small, jax.ShapeDtypeStruct((samples, 2, feat, tok), BF), small],
        compiler_params=pltpu.CompilerParams(vmem_limit_bytes=24 * 2**20),
        name="project",
    )(rows_in, wq, wk, wv, wg)


def gated_grad_kernel(rows_ref, w_ref, out_ref):
    rows = rows_ref[:, 0].reshape(256, rows_ref.shape[-1])
    out_ref[0] = mm(w_ref[...], rows, NT).astype(BF)


def gated_grad(grad_rows, w_out):
    cols, samples, local, width = grad_rows.shape
    feat = w_out.shape[0]
    tok = cols * local
    return pl.pallas_call(
        gated_grad_kernel,
        grid=(samples,),
        in_specs=[
            pl.BlockSpec((cols, 1, local, width), lambda s: (0, s, 0, 0)),
            pl.BlockSpec((feat, width), lambda s: (0, 0)),
        ],
        out_specs=pl.BlockSpec((1, feat, tok), lambda s: (s, 0, 0)),
        out_shape=jax.ShapeDtypeStruct((samples, feat, tok), BF),
        compiler_params=pltpu.CompilerParams(vmem_limit_bytes=24 * 2**20),
        name="gated_grad",
    )(grad_rows, w_out)


def slot_xor(t):
    return 2 * (t % 4) + t // 4


def attend_kernel(me_ref, bias_ref, q_ref, gate_ref, gg_ref, *refs):
    kv_refs = refs[:8]
    gated_ref, dq_ref, dgate_ref, dkv_own_ref, dkv_far_ref, dbias_ref = refs[8:14]
    s_scr, dp_scr, db_scr = refs[14:]
    head = pl.program_id(0)
    sample = pl.program_id(1)
    me = me_ref[0]
    scale = 1.0 / math.sqrt(HD)
    q = q_ref[0]
    gg = gg_ref[0].astype(F32)
    sig = 1.0 / (1.0 + jnp.exp(-gate_ref[0].astype(F32)))
    gatt = (gg * sig).astype(BF)
    row_id = lax.broadcasted_iota(jnp.int32, (16, 256), 0)
    wanted = (row_id >= head * 3) & (row_id < head * 3 + 3)

    @pl.when(sample == 0)
    def _():
        db_scr[...] = jnp.zeros_like(db_scr)

    peak = None
    for t in range(8):
        block = me ^ slot_xor(t)
        k = kv_refs[t][0, 0, :HD, :]
        tops = bias_ref[block, 512:528, :].astype(F32)
        top = jnp.sum(jnp.where(wanted, tops, 0.0), axis=0, keepdims=True)
        bias = bias_ref[block, pl.ds(pl.multiple_of(head * 256, 256), 256), :].astype(F32) + top
        score = mm(k, q, TN) * scale + bias
        s_scr[t] = score
        high = jnp.max(score, axis=0, keepdims=True)
        peak = high if peak is None else jnp.maximum(peak, high)
    total = jnp.zeros((1, 256), F32)
    dot = jnp.zeros((1, 256), F32)
    for t in range(8):
        v = kv_refs[t][0, 0, HD:, :]
        e = jnp.exp(s_scr[t] - peak)
        s_scr[t] = e
        dp = mm(v, gatt, TN)
        dp_scr[t] = dp
        total = total + jnp.sum(e, axis=0, keepdims=True)
        dot = dot + jnp.sum(e * dp, axis=0, keepdims=True)
    inv = 1.0 / total
    dot = dot * inv
    att = jnp.zeros((HD, 256), F32)
    dq = jnp.zeros((HD, 256), F32)
    for t in range(8):
        block = me ^ slot_xor(t)
        k = kv_refs[t][0, 0, :HD, :]
        v = kv_refs[t][0, 0, HD:, :]
        prob = s_scr[t] * inv
        prob_bf = prob.astype(BF)
        ds = (prob * (dp_scr[t] - dot)).astype(BF)
        db_scr[block] = db_scr[block] + ds.astype(F32)
        att = att + mm(v, prob_bf, NN)
        dq = dq + mm(k, ds, NN)
        out_ref = dkv_own_ref if t < 4 else dkv_far_ref
        out_ref[t % 4, 0, 0, :HD, :] = (mm(q, ds, NT) * scale).astype(BF)
        out_ref[t % 4, 0, 0, HD:, :] = mm(gatt, prob_bf, NT).astype(BF)
    gated_ref[0] = (sig * att).astype(BF)
    dgate_ref[0] = (gg * att * sig * (1.0 - sig)).astype(BF)
    dq_ref[0] = (dq * scale).astype(BF)

    @pl.when(sample == pl.num_programs(1) - 1)
    def _():
        for t in range(8):
            dbias_ref[t, 0] = db_scr[t].astype(BF)


def attend(me, bias, q, gate, gg, kv):
    samples, feat, tok = q.shape
    heads = 2
    half = pl.BlockSpec((1, HD, tok), lambda h, s: (s, h, 0))
    kv_spec = pl.BlockSpec((1, 1, feat, tok), lambda h, s: (s, h, 0, 0))
    small = jax.ShapeDtypeStruct((samples, feat, tok), BF)
    dkv = jax.ShapeDtypeStruct((4, samples, heads, feat, tok), BF)
    dkv_spec = pl.BlockSpec((4, 1, 1, feat, tok), lambda h, s: (0, s, h, 0, 0))
    return pl.pallas_call(
        attend_kernel,
        grid=(heads, samples),
        in_specs=[
            pl.BlockSpec(memory_space=pltpu.SMEM),
            pl.BlockSpec(bias.shape, lambda h, s: (0, 0, 0)),
            half,
            half,
            half,
        ]
        + [kv_spec] * 8,
        out_specs=[
            half,
            half,
            half,
            dkv_spec,
            dkv_spec,
            pl.BlockSpec((8, 1, 256, tok), lambda h, s: (0, h, 0, 0)),
        ],
        out_shape=[small, small, small, dkv, dkv, jax.ShapeDtypeStruct((8, heads, 256, tok), BF)],
        scratch_shapes=[pltpu.VMEM((8, 256, tok), F32)] * 3,
        compiler_params=pltpu.CompilerParams(vmem_limit_bytes=40 * 2**20),
        cost_estimate=pl.CostEstimate(
            flops=2**34, bytes_accessed=20 * 2**20, transcendentals=2**22
        ),
        name="attend",
    )(me, bias, q, gate, gg, *kv)


def output_kernel(gated_ref, rows_ref, w_ref, part_ref, grad_ref):
    gated = gated_ref[0]
    rows = rows_ref[:, 0].reshape(256, rows_ref.shape[-1])
    part = mm(gated, w_ref[...], TN).astype(BF)
    part_ref[:, 0] = part.reshape(part_ref.shape[0], part_ref.shape[2], part_ref.shape[3])
    grad = mm(gated, rows, NN)

    @pl.when(pl.program_id(0) == 0)
    def _():
        grad_ref[...] = grad

    @pl.when(pl.program_id(0) > 0)
    def _():
        grad_ref[...] += grad


def output_part(gated, grad_rows, w_out):
    cols, samples, local, width = grad_rows.shape
    feat = w_out.shape[0]
    row_spec = pl.BlockSpec((cols, 1, local, width), lambda s: (0, s, 0, 0))
    return pl.pallas_call(
        output_kernel,
        grid=(samples,),
        in_specs=[
            pl.BlockSpec((1, feat, cols * local), lambda s: (s, 0, 0)),
            row_spec,
            pl.BlockSpec((feat, width), lambda s: (0, 0)),
        ],
        out_specs=[row_spec, pl.BlockSpec((feat, width), lambda s: (0, 0))],
        out_shape=[
            jax.ShapeDtypeStruct(grad_rows.shape, BF),
            jax.ShapeDtypeStruct((feat, width), F32),
        ],
        compiler_params=pltpu.CompilerParams(vmem_limit_bytes=24 * 2**20),
        name="output_part",
    )(gated, grad_rows, w_out)


def weights_kernel(dq_ref, dg_ref, *refs):
    kv_refs = refs[:4]
    rows_ref, w_ref, gain_ref, part_ref, grad_ref, gain_out_ref = refs[4:]
    dkv = kv_refs[0][0, 0].astype(F32)
    for ref in kv_refs[1:]:
        dkv = dkv + ref[0, 0].astype(F32)
    dkv = dkv.astype(BF)
    dcat = jnp.concatenate(
        [
            dq_ref[0],
            dkv[0, :HD],
            dkv[1, :HD],
            dkv[0, HD:],
            dkv[1, HD:],
            dg_ref[0],
        ],
        axis=0,
    )
    rows = rows_ref[:, 0].reshape(256, rows_ref.shape[-1])
    part = mm(dcat, w_ref[...], TN).astype(BF)
    part_ref[:, 0] = part.reshape(part_ref.shape[0], part_ref.shape[2], part_ref.shape[3])
    grad = mm(dcat, rows, NN)

    @pl.when(pl.program_id(0) == 0)
    def _():
        grad_ref[...] = grad

    @pl.when(pl.program_id(0) > 0)
    def _():
        grad_ref[...] += grad

    @pl.when(pl.program_id(0) == pl.num_programs(0) - 1)
    def _():
        both = jnp.sum(grad_ref[...] * w_ref[...].astype(F32), axis=0, keepdims=True)
        gain_out_ref[...] = both / gain_ref[...]


def weight_part(dq, dg, kv_pieces, rows_in, w_cat, gain):
    cols, samples, local, width = rows_in.shape
    feat = dq.shape[1]
    tok = cols * local
    row_spec = pl.BlockSpec((cols, 1, local, width), lambda s: (0, s, 0, 0))
    half = pl.BlockSpec((1, feat, tok), lambda s: (s, 0, 0))
    kv_spec = pl.BlockSpec((1, 1, 2, feat, tok), lambda s: (0, s, 0, 0, 0))
    full = pl.BlockSpec(w_cat.shape, lambda s: (0, 0))
    line = pl.BlockSpec((1, width), lambda s: (0, 0))
    return pl.pallas_call(
        weights_kernel,
        grid=(samples,),
        in_specs=[half, half] + [kv_spec] * 4 + [row_spec, full, line],
        out_specs=[row_spec, full, line],
        out_shape=[
            jax.ShapeDtypeStruct(rows_in.shape, BF),
            jax.ShapeDtypeStruct(w_cat.shape, F32),
            jax.ShapeDtypeStruct((1, width), F32),
        ],
        compiler_params=pltpu.CompilerParams(vmem_limit_bytes=32 * 2**20),
        name="weight_part",
    )(dq, dg, *kv_pieces, rows_in, w_cat, gain)


def wpair_kernel(db_ref, pair_ref, out_ref, db_scr, acc_ref):
    step = pair_ref.shape[0]
    chans = pair_ref.shape[2]
    heads = db_scr.shape[0]

    @pl.when(pl.program_id(0) == 0)
    def _():
        acc_ref[...] = jnp.zeros_like(acc_ref)

    for h in range(heads):
        db_scr[h] = db_ref[h // 2, h % 2].astype(F32).T.astype(BF)
    for block in range(step // 16):
        left = db_scr[:, block * 16 : (block + 1) * 16, :].reshape(heads * 16, db_scr.shape[2])
        for k in range(0, 16, 2):
            pair = jnp.concatenate(
                [pair_ref[block * 16 + k], pair_ref[block * 16 + k + 1]], axis=1
            )
            at = slice(k * chans, (k + 2) * chans)
            acc_ref[:, at] += mm(left, pair, NN)

    @pl.when(pl.program_id(0) == pl.num_programs(0) - 1)
    def _():
        total = jnp.zeros((heads, chans), F32)
        row_id = lax.broadcasted_iota(jnp.int32, (heads, 16, chans), 1)
        for k in range(16):
            piece = acc_ref[:, k * chans : (k + 1) * chans].reshape(heads, 16, chans)
            total = total + jnp.sum(jnp.where(row_id == k, piece, 0.0), axis=1)
        out_ref[...] = total


def wpair_part(dbias, pair):
    groups, per, keys, rows = dbias.shape
    heads = groups * per
    chans = pair.shape[2]
    step = 128
    return pl.pallas_call(
        wpair_kernel,
        grid=(rows // step,),
        in_specs=[
            pl.BlockSpec((groups, per, keys, step), lambda i: (0, 0, 0, i)),
            pl.BlockSpec((step, keys, chans), lambda i: (i, 0, 0)),
        ],
        out_specs=pl.BlockSpec((heads, chans), lambda i: (0, 0)),
        out_shape=jax.ShapeDtypeStruct((heads, chans), F32),
        scratch_shapes=[
            pltpu.VMEM((heads, step, keys), BF),
            pltpu.VMEM((heads * 16, 16 * chans), F32),
        ],
        compiler_params=pltpu.CompilerParams(vmem_limit_bytes=44 * 2**20),
        cost_estimate=pl.CostEstimate(flops=2**32, bytes_accessed=20 * 2**20, transcendentals=0),
        name="wpair_part",
    )(dbias, pair)


def exchange(x, axes):
    return lax.all_to_all(x, axes, 0, 0, tiled=True)


def gather(x, axes, count):
    return exchange(jnp.broadcast_to(x[None], (count,) + x.shape), axes)


def swap(x, axis, count, k):
    return lax.ppermute(x, axis, [(i, i ^ k) for i in range(count)])


def on_device(
    token_act, pair_rep, norm_gain, w_pair, w_query, w_key, w_value, w_gate, w_out, grad_out
):
    samples, local, width = token_act.shape
    cols = 8
    me = lax.axis_index("y") * 2 + lax.axis_index("core")

    values_f = token_act.astype(F32)
    centred = values_f - jnp.mean(values_f, axis=-1, keepdims=True)
    inv_std = lax.rsqrt(jnp.mean(centred * centred, axis=-1, keepdims=True) + EPSILON)
    normed = centred * inv_std
    token_norm = (normed * norm_gain).astype(BF)

    rows_in = gather(token_norm, COL, cols)
    bias = exchange(pair_bias(pair_rep, w_pair), COL)
    grad_rows = gather(grad_out, COL, cols)

    wq, wk, wv, wg = w_query.T, w_key.T, w_value.T, w_gate.T
    q, kv_own, gate = project(rows_in, wq, wk, wv, wg)
    near = [kv_own] + [swap(kv_own, "y", 4, k) for k in range(1, 4)]
    far = [swap(x, "core", 2, 1) for x in near]
    gg = gated_grad(grad_rows, w_out)

    gated, dq, dgate, dkv_own, dkv_far, dbias = attend(
        jnp.full((1,), me, jnp.int32), bias, q, gate, gg, near + far
    )
    dkv_far = swap(dkv_far, "core", 2, 1)
    dbias = exchange(dbias, COL)
    out_part, grad_wout = output_part(gated, grad_rows, w_out)
    out_recv = exchange(out_part, COL)

    dkv = (dkv_own.astype(F32) + dkv_far.astype(F32)).astype(BF)
    pieces = [dkv[0:1]] + [swap(dkv[k : k + 1], "y", 4, k) for k in range(1, 4)]
    w_cat = jnp.concatenate([wq, wk, wv, wg], axis=0)
    norm_part, grad_cat, gain_part = weight_part(
        dq, dgate, pieces, rows_in, w_cat, norm_gain[None, :]
    )
    norm_recv = exchange(norm_part, COL)

    grads = jnp.concatenate([grad_cat, grad_wout], axis=0).astype(BF)
    grads = exchange(grads.reshape(16, 30, width), GROUP)
    grads = jnp.sum(grads.astype(F32), axis=0).astype(BF)
    grads = gather(grads, GROUP, 16).reshape(480, width).astype(F32)

    wpair = wpair_part(dbias, pair_rep)
    tiny = jnp.concatenate([wpair.reshape(16, 128), gain_part.reshape(6, 128)], axis=0)
    tiny = jnp.sum(gather(tiny, COL, cols), axis=0)
    tiny = jnp.sum(gather(tiny, GROUP, 16), axis=0)
    grad_wpair = tiny[:16].T
    grad_gain = tiny[16:].reshape(width)

    block_out = (values_f + jnp.sum(out_recv.astype(F32), axis=0)).astype(BF)
    grad_norm = jnp.sum(norm_recv.astype(F32), axis=0)
    grad_hat = grad_norm * norm_gain
    grad_act = grad_out.astype(F32) + inv_std * (
        grad_hat
        - jnp.mean(grad_hat, axis=-1, keepdims=True)
        - normed * jnp.mean(grad_hat * normed, axis=-1, keepdims=True)
    )
    feat = w_out.shape[0]
    return (
        block_out,
        grad_act.astype(BF),
        grads[0:feat].T,
        grads[feat : 2 * feat].T,
        grads[2 * feat : 3 * feat].T,
        grads[3 * feat : 4 * feat].T,
        grads[4 * feat :],
        grad_wpair,
        grad_gain,
    )


def solution(mesh):
    fine = Mesh(mesh.devices.reshape(4, 2, 4, 2, 2), ("y", "core", "z", "xh", "smp"))
    tokens = P("smp", ROW + COL, None)
    split_last = P(None, COL)
    return jax.shard_map(
        on_device,
        mesh=fine,
        in_specs=(
            tokens,
            P(ROW, COL, None),
            P(),
            P(),
            split_last,
            split_last,
            split_last,
            split_last,
            P(COL, None),
            tokens,
        ),
        out_specs=(
            tokens,
            tokens,
            split_last,
            split_last,
            split_last,
            split_last,
            P(COL, None),
            P(),
            P(),
        ),
        check_vma=False,
    )
```

time: 750 us -> 296 us (0.39)
  waiting for transfers between devices: 351 us -> 92.3 us
  matrix products: 148 us -> 0 us
  local copies, waits for them, and re-layouts: 109 us -> 25.2 us
  Pallas kernels: 0 us -> 55.7 us
  starting transfers between devices: 12.2 us -> 62.9 us
  other arithmetic: 38 us -> 11.1 us
  blocking collectives: 72.7 us -> 46.8 us
  between operations: 14.4 us -> 1.08 us
    dot_general x47 -> x0, matrix products: 148 us -> none  [the longest x8 39.2 us: attend(): jnp.einsum('hij,jhd->ihd', probs_bf, value_h, preferred_element_type=jnp....]
    all_gather x4 -> x0, waiting for transfers between devices: 142 us -> none  [the longest x1 49.7 us: on_device(): grad_rows = lax.all_gather(grad_out, 'col', axis=1, tiled=True)]
    psum x1 -> x0, waiting for transfers between devices: 90 us -> none  [on_device(): lax.psum((query_grad, key_grad, value_grad, gate_grad, grad_wout), ('row'...]
    psum x1 -> x0, blocking collectives: 72.7 us -> none  [on_device(): lax.psum((wpair_part, gain_part), ('row', 'col', 'smp'))]
    reduce_scatter x4 -> x0, waiting for transfers between devices: 67.3 us -> none  [the longest x1 37.9 us: on_device(): lax.psum_scatter(grad_v_part, 'row', scatter_dimension=1, tiled=True)]
    pallas_call x0 -> x7, Pallas kernels: none -> 55.7 us  [the longest x1 24.2 us: attend(): pl.pallas_call(attend_kernel, grid=(heads, samples), in_specs=[pl.BlockSp...]
    all_to_all x0 -> x2, blocking collectives: none -> 46.8 us  [exchange(): return lax.all_to_all(x, axes, 0, 0, tiled=True)]
    while x57 -> x0, local copies, waits for them, and re-layouts: 40.6 us -> none  [the longest x5 17.5 us: on_device(): lax.scan(backward_one, bias_start, (queries, keys_all, values_all, gates,...]
  transfers between devices with their start and end apart: 11 -> 19, of which waited for: 9 -> 9; matrix products, arithmetic and copies ran while one was open for 19% -> 4% of each run, Pallas kernels for 0% -> 9%
where the time goes in v1:
time: 296 us; the launch traced here: 295 us
  waiting for transfers between devices  92.3 us (31%)
  starting transfers between devices  62.9 us (21%)
  Pallas kernels  55.7 us (19%)
  blocking collectives  46.8 us (16%)
  local copies, waits for them, and re-layouts  25.2 us (9%)
  other arithmetic  11.1 us (4%)
    all_to_all x8, waiting for transfers between devices, exchange(): return lax.all_to_all(x, axes, 0, 0, tiled=True)  86.9 us
    all_to_all x2, blocking collectives, exchange(): return lax.all_to_all(x, axes, 0, 0, tiled=True)  46.8 us
    all_to_all x8, starting transfers between devices, exchange(): return lax.all_to_all(x, axes, 0, 0, tiled=True)  39 us
    pallas_call x1, Pallas kernels, attend(): pl.pallas_call(attend_kernel, grid=(heads, samples), in_specs=[pl.BlockSp...  24.2 us
    ppermute x11, starting transfers between devices, swap(): return lax.ppermute(x, axis, [(i, i ^ k) for i in range(count)])  23.9 us
    unnamed x69, local copies, waits for them, and re-layouts  16.7 us
    pallas_call x1, Pallas kernels, pair_bias(): pl.pallas_call(bias_kernel, grid=(rows // step,), in_specs=[pl.BlockSpec(...  9.58 us
    pallas_call x1, Pallas kernels, wpair_part(): pl.pallas_call(wpair_kernel, grid=(rows // step,), in_specs=[pl.BlockSpec...  9.49 us
  transfers between devices with their start and end apart: 19, of which 9 were waited for; matrix products, arithmetic and copies ran while one was open for 4% of the time, Pallas kernels for 9%

profile of v1, /device:TPU:1, one launch (start us, length us, event | category | flops | bytes accessed | tf_op | source)
XLA Modules:
  0.0 295.0 jit_solution(10756074435632526463)
XLA Ops:
  4.2 30.2 %all_to_all.50.rows_ref.refs_4_ = bf16[8,4,32,768]{3,2,1,0:T(8,128)(2,1)S(1)} all-to-all(bf16[8,4,32,768]{3,2,1,0:T(8,128)(2,1)S(1)} %broadcast_in_dim.15), channel_id=1, replica_groups=mesh['y'=4,'core'=2,'z'=4,'xh'=2,'smp'=2] {'z','xh'}, dimensions={0} | all-to-all | bytes 3145728 | tf_op jit(solution)/shard_map/all_to_all | solution.py:387
  35.7 3.7 %all-to-all-start.2 = ((bf16[8,4,32,768]{3,2,1,0:T(8,128)(2,1)}), bf16[8,4,32,768]{3,2,1,0:T(8,128)(2,1)S(1)}, u32[]{:S(2)}, u32[]{:S(2)}) async-start(bf16[8,4,32,768]{3,2,1,0:T(8,128)(2,1)} %broadcast_in_dim.16), calls=%async_computation.2 | async-start | bytes 3145728 | tf_op jit(solution)/shard_map/all_to_all | solution.py:387
  39.9 9.6 %pair_bias.1 = bf16[8,528,256]{2,1,0:T(8,128)(2,1)S(1)} custom-call(bf16[256,2048]{1,0:T(8,128)(2,1)S(1)} %bitcast.24, bf16[256,256,128]{2,1,0:T(8,128)(2,1)} %pair_ref.3), custom_call_target="tpu_custom_call" | custom-call | flops 4294967296 | bytes 20971520 | tf_op jit(solution)/shard_map/pair_bias/pallas_call | solution.py:57
  50.8 9.2 %all-to-all-done.2.rows_ref = bf16[8,4,32,768]{3,2,1,0:T(8,128)(2,1)S(1)} async-done(((bf16[8,4,32,768]{3,2,1,0:T(8,128)(2,1)}), bf16[8,4,32,768]{3,2,1,0:T(8,128)(2,1)S(1)}, u32[]{:S(2)}, u32[]{:S(2)}) %all-to-all-start.2) | async-done | bytes 1572896 | tf_op jit(solution)/shard_map/all_to_all | solution.py:387
  60.1 4.9 %all-to-all-start = ((bf16[8,528,256]{2,1,0:T(8,128)(2,1)}), bf16[8,528,256]{2,1,0:T(8,128)(2,1)}, u32[]{:S(2)}, u32[]{:S(2)}) async-start(bf16[8,528,256]{2,1,0:T(8,128)(2,1)} %copy-done), calls=%async_computation | async-start | bytes 4325376 | tf_op jit(solution)/shard_map/all_to_all | solution.py:387
  79.7 6.6 %collective-permute-start.4 = (bf16[4,2,96,256]{3,2,1,0:T(8,128)(2,1)}, bf16[4,2,96,256]{3,2,1,0:T(8,128)(2,1)}, u32[]{:S(2)}, u32[]{:S(2)}) collective-permute-start(bf16[4,2,96,256]{3,2,1,0:T(8,128)(2,1)} %collective-permute-done.refs_1_), channel_id=1, source_target_pairs={{0,16},{16,0},{1,17},{17,1},{2,18},{18,2},{3,19},{19,3},{4,20},{20... | collective-permute-start | bytes 1179656 | tf_op jit(solution)/shard_map/ppermute | solution.py:395
  86.3 4.3 %collective-permute-done.1.refs_2_ = bf16[4,2,96,256]{3,2,1,0:T(8,128)(2,1)} collective-permute-done((bf16[4,2,96,256]{3,2,1,0:T(8,128)(2,1)}, bf16[4,2,96,256]{3,2,1,0:T(8,128)(2,1)}, u32[]{:S(2)}, u32[]{:S(2)}) %collective-permute-start.1) | collective-permute-done | bytes 393248 | tf_op jit(solution)/shard_map/ppermute | solution.py:395
  90.6 3.6 %collective-permute-start.5 = (bf16[4,2,96,256]{3,2,1,0:T(8,128)(2,1)}, bf16[4,2,96,256]{3,2,1,0:T(8,128)(2,1)}, u32[]{:S(2)}, u32[]{:S(2)}) collective-permute-start(bf16[4,2,96,256]{3,2,1,0:T(8,128)(2,1)} %collective-permute-done.1.refs_2_), channel_id=1, source_target_pairs={{0,16},{16,0},{1,17},{17,1},{2,18},{18,2},{3,19},{19,3},{4,20},{20... | collective-permute-start | bytes 1179656 | tf_op jit(solution)/shard_map/ppermute | solution.py:395
  102.4 24.2 %attend.1 = (bf16[4,96,256]{2,1,0:T(8,128)(2,1)S(1)}, bf16[4,96,256]{2,1,0:T(8,128)(2,1)S(1)}, bf16[4,96,256]{2,1,0:T(8,128)(2,1)S(1)}, bf16[4,4,2,96,256]{4,3,2...) custom-call(s32[1]{0:T(128)} %bitcast.me_ref, ...), custom_call_target="tpu_custom_call" | custom-call | flops 17179869184 | bytes 20971520 | tf_op jit(solution)/shard_map/attend/pallas_call | solution.py:204
  131.2 6.8 %all-to-all-start.7 = ((bf16[8,2,256,256]{3,2,1,0:T(8,128)(2,1)}), bf16[8,2,256,256]{3,2,1,0:T(8,128)(2,1)}, u32[]{:S(2)}, u32[]{:S(2)}) async-start(bf16[8,2,256,256]{3,2,1,0:T(8,128)(2,1)} %copy-done.2), calls=%async_computation.7 | async-start | bytes 4194304 | tf_op jit(solution)/shard_map/all_to_all | solution.py:387
  143.4 3.8 %collective-permute-start.9 = (bf16[1,4,2,96,256]{4,3,2,1,0:T(8,128)(2,1)}, bf16[1,4,2,96,256]{4,3,2,1,0:T(8,128)(2,1)}, u32[]{:S(2)}, u32[]{:S(2)}) collective-permute-start(bf16[1,4,2,96,256]{4,3,2,1,0:T(8,128)(2,1)} %get-tuple-element.40), channel_id=1, source_target_pairs={{0,64},{32,96},{64,0},{96,32},{1,65},{33,97},{65,1},{97,33},{2,66}... | collective-permute-start | bytes 1179656 | tf_op jit(solution)/shard_map/ppermute | solution.py:395
  147.3 18.6 %all-to-all-done.7.db_ref = bf16[8,2,256,256]{3,2,1,0:T(8,128)(2,1)} async-done(((bf16[8,2,256,256]{3,2,1,0:T(8,128)(2,1)}), bf16[8,2,256,256]{3,2,1,0:T(8,128)(2,1)}, u32[]{:S(2)}, u32[]{:S(2)}) %all-to-all-start.7) | async-done | bytes 2097184 | tf_op jit(solution)/shard_map/all_to_all | solution.py:387
  165.8 9.5 %wpair_part.1 = f32[16,128]{1,0:T(8,128)S(1)} custom-call(bf16[8,2,256,256]{3,2,1,0:T(8,128)(2,1)} %all-to-all-done.7.db_ref, bf16[256,256,128]{2,1,0:T(8,128)(2,1)} %pair_ref.3), custom_call_target="tpu_custom_call" | custom-call | flops 4294967296 | bytes 20971520 | tf_op jit(solution)/shard_map/wpair_part/pallas_call | solution.py:367
  175.4 5.2 %weight_part.1 = (bf16[8,4,32,768]{3,2,1,0:T(8,128)(2,1)}, f32[384,768]{1,0:T(8,128)S(1)}, f32[1,768]{1,0:T(1,128)S(1)}) custom-call(bf16[4,96,256]{2,1,0:T(8,128)(2,1)S(1)} %copy-done.13, bf16[4,96,256]{2,1,0:T(8,128)(2,1)S(1)} %copy-done.15, bf16[1,4,2,96,256]{4,3,2,1,0:T(8,128)(2,1)S(1)} %get-tuple-element.42.refs_0_, ...), custom_call_target="tpu_custom_call" | custom-call | tf_op jit(solution)/shard_map/weight_part/pallas_call | solution.py:317
  182.3 3.6 %all-to-all-start.8 = ((f32[8,22,128]{2,1,0:T(8,128)}), f32[8,22,128]{2,1,0:T(8,128)S(1)}, u32[]{:S(2)}, u32[]{:S(2)}) async-start(f32[8,22,128]{2,1,0:T(8,128)} %broadcast_in_dim.19), calls=%async_computation.8 | async-start | bytes 196608 | tf_op jit(solution)/shard_map/all_to_all | solution.py:387
  192.8 4.5 %all-to-all-start.3 = ((bf16[8,4,32,768]{3,2,1,0:T(8,128)(2,1)}), bf16[8,4,32,768]{3,2,1,0:T(8,128)(2,1)S(1)}, u32[]{:S(2)}, u32[]{:S(2)}) async-start(bf16[8,4,32,768]{3,2,1,0:T(8,128)(2,1)} %get-tuple-element.27), calls=%async_computation.3 | async-start | bytes 3145728 | tf_op jit(solution)/shard_map/all_to_all | solution.py:387
  197.3 20.6 %all-to-all-done.3 = bf16[8,4,32,768]{3,2,1,0:T(8,128)(2,1)S(1)} async-done(((bf16[8,4,32,768]{3,2,1,0:T(8,128)(2,1)}), bf16[8,4,32,768]{3,2,1,0:T(8,128)(2,1)S(1)}, u32[]{:S(2)}, u32[]{:S(2)}) %all-to-all-start.3) | async-done | bytes 1572896 | tf_op jit(solution)/shard_map/all_to_all | solution.py:387
  218.6 6.5 %all-to-all-start.9 = ((f32[16,22,128]{2,1,0:T(8,128)}), f32[16,22,128]{2,1,0:T(8,128)S(1)}, u32[]{:S(2)}, u32[]{:S(2)}) async-start(f32[16,22,128]{2,1,0:T(8,128)} %broadcast_in_dim.20), calls=%async_computation.9 | async-start | bytes 393216 | tf_op jit(solution)/shard_map/all_to_all | solution.py:387
  226.4 5.6 %all-to-all-done.9 = f32[16,22,128]{2,1,0:T(8,128)S(1)} async-done(((f32[16,22,128]{2,1,0:T(8,128)}), f32[16,22,128]{2,1,0:T(8,128)S(1)}, u32[]{:S(2)}, u32[]{:S(2)}) %all-to-all-start.9) | async-done | bytes 180256 | tf_op jit(solution)/shard_map/all_to_all | solution.py:387
  231.9 16.6 %all_to_all.51 = bf16[16,30,768]{2,1,0:T(8,128)(2,1)S(1)} all-to-all(bf16[16,30,768]{2,1,0:T(8,128)(2,1)} %convert_element_type.61), channel_id=1, replica_groups=mesh['y'=4,'core'=2,'z'=4,'xh'=2,'smp'=2] {'y','core','smp'}, dimensions={0} | all-to-all | bytes 1474560 | tf_op jit(solution)/shard_map/all_to_all | solution.py:387
  248.5 4.3 %all-to-all-start.4 = ((bf16[8,4,32,768]{3,2,1,0:T(8,128)(2,1)}), bf16[8,4,32,768]{3,2,1,0:T(8,128)(2,1)}, u32[]{:S(2)}, u32[]{:S(2)}) async-start(bf16[8,4,32,768]{3,2,1,0:T(8,128)(2,1)} %get-tuple-element.32), calls=%async_computation.4 | async-start | bytes 3145728 | tf_op jit(solution)/shard_map/all_to_all | solution.py:387
  254.4 21.0 %all-to-all-done.4 = bf16[8,4,32,768]{3,2,1,0:T(8,128)(2,1)} async-done(((bf16[8,4,32,768]{3,2,1,0:T(8,128)(2,1)}), bf16[8,4,32,768]{3,2,1,0:T(8,128)(2,1)}, u32[]{:S(2)}, u32[]{:S(2)}) %all-to-all-start.4) | async-done | bytes 1572896 | tf_op jit(solution)/shard_map/all_to_all | solution.py:387
  276.5 4.8 %all-to-all-start.6 = ((bf16[16,30,768]{2,1,0:T(8,128)(2,1)}), bf16[16,30,768]{2,1,0:T(8,128)(2,1)S(1)}, u32[]{:S(2)}, u32[]{:S(2)}) async-start(bf16[16,30,768]{2,1,0:T(8,128)(2,1)} %broadcast_in_dim.18), calls=%async_computation.6 | async-start | bytes 1572864 | tf_op jit(solution)/shard_map/all_to_all | solution.py:387
  284.1 9.6 %all-to-all-done.6 = bf16[16,30,768]{2,1,0:T(8,128)(2,1)S(1)} async-done(((bf16[16,30,768]{2,1,0:T(8,128)(2,1)}), bf16[16,30,768]{2,1,0:T(8,128)(2,1)S(1)}, u32[]{:S(2)}, u32[]{:S(2)}) %all-to-all-start.6) | async-done | bytes 737312 | tf_op jit(solution)/shard_map/all_to_all | solution.py:387
  (126 shorter events, 56.8 us)
Async XLA Ops:
  4.2 30.2 %copy-start.25 = (bf16[4,32,768]{2,1,0:T(8,128)(2,1)S(1)}, bf16[4,32,768]{2,1,0:T(8,128)(2,1)}, u32[]{:S(2)}) copy-start(bf16[4,32,768]{2,1,0:T(8,128)(2,1)} %param.19) | copy-start | bytes 589828
  35.7 24.4 %all-to-all-start.2 = ((bf16[8,4,32,768]{3,2,1,0:T(8,128)(2,1)}), bf16[8,4,32,768]{3,2,1,0:T(8,128)(2,1)S(1)}, u32[]{:S(2)}, u32[]{:S(2)}) async-start(bf16[8,4,32,768]{3,2,1,0:T(8,128)(2,1)} %broadcast_in_dim.16), calls=%async_computation.2 | async-start | bytes 3145728 | tf_op jit(solution)/shard_map/all_to_all | solution.py:387
  50.8 14.1 %copy-start.6 = (bf16[768,96]{0,1:T(8,128)(2,1)S(1)}, bf16[768,96]{0,1:T(8,128)(2,1)}, u32[]{:S(2)}) copy-start(bf16[768,96]{0,1:T(8,128)(2,1)} %param.14) | copy-start | bytes 442372
  50.8 14.1 %copy-start.7 = (bf16[768,96]{0,1:T(8,128)(2,1)S(1)}, bf16[768,96]{0,1:T(8,128)(2,1)}, u32[]{:S(2)}) copy-start(bf16[768,96]{0,1:T(8,128)(2,1)} %param.15) | copy-start | bytes 442372
  60.1 39.6 %all-to-all-start = ((bf16[8,528,256]{2,1,0:T(8,128)(2,1)}), bf16[8,528,256]{2,1,0:T(8,128)(2,1)}, u32[]{:S(2)}, u32[]{:S(2)}) async-start(bf16[8,528,256]{2,1,0:T(8,128)(2,1)} %copy-done), calls=%async_computation | async-start | bytes 4325376 | tf_op jit(solution)/shard_map/all_to_all | solution.py:387
  71.4 8.4 %collective-permute-start = (bf16[4,2,96,256]{3,2,1,0:T(8,128)(2,1)}, bf16[4,2,96,256]{3,2,1,0:T(8,128)(2,1)}, u32[]{:S(2)}, u32[]{:S(2)}) collective-permute-start(bf16[4,2,96,256]{3,2,1,0:T(8,128)(2,1)} %get-tuple-element.25.refs_0_), channel_id=1, source_target_pairs={{0,32},{32,0},{64,96},{96,64},{1,33},{33,1},{65,97},{97,65},{2,34}... | collective-permute-start | bytes 1179656 | tf_op jit(solution)/shard_map/ppermute | solution.py:395
  72.7 18.0 %collective-permute-start.1 = (bf16[4,2,96,256]{3,2,1,0:T(8,128)(2,1)}, bf16[4,2,96,256]{3,2,1,0:T(8,128)(2,1)}, u32[]{:S(2)}, u32[]{:S(2)}) collective-permute-start(bf16[4,2,96,256]{3,2,1,0:T(8,128)(2,1)} %get-tuple-element.25.refs_0_), channel_id=1, source_target_pairs={{0,64},{32,96},{64,0},{96,32},{1,65},{33,97},{65,1},{97,33},{2,66}... | collective-permute-start | bytes 1179656 | tf_op jit(solution)/shard_map/ppermute | solution.py:395
  75.3 18.9 %collective-permute-start.2 = (bf16[4,2,96,256]{3,2,1,0:T(8,128)(2,1)}, bf16[4,2,96,256]{3,2,1,0:T(8,128)(2,1)}, u32[]{:S(2)}, u32[]{:S(2)}) collective-permute-start(bf16[4,2,96,256]{3,2,1,0:T(8,128)(2,1)} %get-tuple-element.25.refs_0_), channel_id=1, source_target_pairs={{0,96},{32,64},{64,32},{96,0},{1,97},{33,65},{65,33},{97,1},{2,98}... | collective-permute-start | bytes 1179656 | tf_op jit(solution)/shard_map/ppermute | solution.py:395
  75.3 24.3 %collective-permute-start.3 = (bf16[4,2,96,256]{3,2,1,0:T(8,128)(2,1)}, bf16[4,2,96,256]{3,2,1,0:T(8,128)(2,1)}, u32[]{:S(2)}, u32[]{:S(2)}) collective-permute-start(bf16[4,2,96,256]{3,2,1,0:T(8,128)(2,1)} %get-tuple-element.25.refs_0_), channel_id=1, source_target_pairs={{0,16},{16,0},{1,17},{17,1},{2,18},{18,2},{3,19},{19,3},{4,20},{20... | collective-permute-start | bytes 1179656 | tf_op jit(solution)/shard_map/ppermute | solution.py:395
  79.7 19.9 %collective-permute-start.4 = (bf16[4,2,96,256]{3,2,1,0:T(8,128)(2,1)}, bf16[4,2,96,256]{3,2,1,0:T(8,128)(2,1)}, u32[]{:S(2)}, u32[]{:S(2)}) collective-permute-start(bf16[4,2,96,256]{3,2,1,0:T(8,128)(2,1)} %collective-permute-done.refs_1_), channel_id=1, source_target_pairs={{0,16},{16,0},{1,17},{17,1},{2,18},{18,2},{3,19},{19,3},{4,20},{20... | collective-permute-start | bytes 1179656 | tf_op jit(solution)/shard_map/ppermute | solution.py:395
  90.6 9.0 %collective-permute-start.5 = (bf16[4,2,96,256]{3,2,1,0:T(8,128)(2,1)}, bf16[4,2,96,256]{3,2,1,0:T(8,128)(2,1)}, u32[]{:S(2)}, u32[]{:S(2)}) collective-permute-start(bf16[4,2,96,256]{3,2,1,0:T(8,128)(2,1)} %collective-permute-done.1.refs_2_), channel_id=1, source_target_pairs={{0,16},{16,0},{1,17},{17,1},{2,18},{18,2},{3,19},{19,3},{4,20},{20... | collective-permute-start | bytes 1179656 | tf_op jit(solution)/shard_map/ppermute | solution.py:395
  94.2 5.5 %collective-permute-start.6 = (bf16[4,2,96,256]{3,2,1,0:T(8,128)(2,1)}, bf16[4,2,96,256]{3,2,1,0:T(8,128)(2,1)}, u32[]{:S(2)}, u32[]{:S(2)}) collective-permute-start(bf16[4,2,96,256]{3,2,1,0:T(8,128)(2,1)} %collective-permute-done.2.refs_3_), channel_id=1, source_target_pairs={{0,16},{16,0},{1,17},{17,1},{2,18},{18,2},{3,19},{19,3},{4,20},{20... | collective-permute-start | bytes 1179656 | tf_op jit(solution)/shard_map/ppermute | solution.py:395
  131.2 8.7 %collective-permute-start.7 = (bf16[4,4,2,96,256]{4,3,2,1,0:T(8,128)(2,1)}, bf16[4,4,2,96,256]{4,3,2,1,0:T(8,128)(2,1)}, u32[]{:S(2)}, u32[]{:S(2)}) collective-permute-start(bf16[4,4,2,96,256]{4,3,2,1,0:T(8,128)(2,1)} %get-tuple-element.31), channel_id=1, source_target_pairs={{0,16},{16,0},{1,17},{17,1},{2,18},{18,2},{3,19},{19,3},{4,20},{20... | collective-permute-start | bytes 4718600 | tf_op jit(solution)/shard_map/ppermute | solution.py:395
  131.2 34.6 %all-to-all-start.7 = ((bf16[8,2,256,256]{3,2,1,0:T(8,128)(2,1)}), bf16[8,2,256,256]{3,2,1,0:T(8,128)(2,1)}, u32[]{:S(2)}, u32[]{:S(2)}) async-start(bf16[8,2,256,256]{3,2,1,0:T(8,128)(2,1)} %copy-done.2), calls=%async_computation.7 | async-start | bytes 4194304 | tf_op jit(solution)/shard_map/all_to_all | solution.py:387
  143.4 31.9 %collective-permute-start.10 = (bf16[1,4,2,96,256]{4,3,2,1,0:T(8,128)(2,1)}, bf16[1,4,2,96,256]{4,3,2,1,0:T(8,128)(2,1)}, u32[]{:S(2)}, u32[]{:S(2)}) collective-permute-start(bf16[1,4,2,96,256]{4,3,2,1,0:T(8,128)(2,1)} %get-tuple-element.39), channel_id=1, source_target_pairs={{0,96},{32,64},{64,32},{96,0},{1,97},{33,65},{65,33},{97,1},{2,98}... | collective-permute-start | bytes 1179656 | tf_op jit(solution)/shard_map/ppermute | solution.py:395
  143.4 31.9 %collective-permute-start.8 = (bf16[1,4,2,96,256]{4,3,2,1,0:T(8,128)(2,1)}, bf16[1,4,2,96,256]{4,3,2,1,0:T(8,128)(2,1)}, u32[]{:S(2)}, u32[]{:S(2)}) collective-permute-start(bf16[1,4,2,96,256]{4,3,2,1,0:T(8,128)(2,1)} %get-tuple-element.41), channel_id=1, source_target_pairs={{0,32},{32,0},{64,96},{96,64},{1,33},{33,1},{65,97},{97,65},{2,34}... | collective-permute-start | bytes 1179656 | tf_op jit(solution)/shard_map/ppermute | solution.py:395
  143.4 31.9 %collective-permute-start.9 = (bf16[1,4,2,96,256]{4,3,2,1,0:T(8,128)(2,1)}, bf16[1,4,2,96,256]{4,3,2,1,0:T(8,128)(2,1)}, u32[]{:S(2)}, u32[]{:S(2)}) collective-permute-start(bf16[1,4,2,96,256]{4,3,2,1,0:T(8,128)(2,1)} %get-tuple-element.40), channel_id=1, source_target_pairs={{0,64},{32,96},{64,0},{96,32},{1,65},{33,97},{65,1},{97,33},{2,66}... | collective-permute-start | bytes 1179656 | tf_op jit(solution)/shard_map/ppermute | solution.py:395
  165.8 9.6 %copy-start.15 = (bf16[4,96,256]{2,1,0:T(8,128)(2,1)S(1)}, bf16[4,96,256]{2,1,0:T(8,128)(2,1)}, u32[]{:S(2)}) copy-start(bf16[4,96,256]{2,1,0:T(8,128)(2,1)} %copy-done.14) | copy-start | bytes 589828
  182.3 10.5 %all-to-all-start.8 = ((f32[8,22,128]{2,1,0:T(8,128)}), f32[8,22,128]{2,1,0:T(8,128)S(1)}, u32[]{:S(2)}, u32[]{:S(2)}) async-start(f32[8,22,128]{2,1,0:T(8,128)} %broadcast_in_dim.19), calls=%async_computation.8 | async-start | bytes 196608 | tf_op jit(solution)/shard_map/all_to_all | solution.py:387
  192.8 32.3 %copy-start.5 = (f32[384,768]{1,0:T(8,128)S(1)}, f32[384,768]{1,0:T(8,128)}, u32[]{:S(2)}) copy-start(f32[384,768]{1,0:T(8,128)} %copy-done.4) | copy-start | bytes 3538948
  192.8 25.1 %all-to-all-start.3 = ((bf16[8,4,32,768]{3,2,1,0:T(8,128)(2,1)}), bf16[8,4,32,768]{3,2,1,0:T(8,128)(2,1)S(1)}, u32[]{:S(2)}, u32[]{:S(2)}) async-start(bf16[8,4,32,768]{3,2,1,0:T(8,128)(2,1)} %get-tuple-element.27), calls=%async_computation.3 | async-start | bytes 3145728 | tf_op jit(solution)/shard_map/all_to_all | solution.py:387
  218.6 13.3 %all-to-all-start.9 = ((f32[16,22,128]{2,1,0:T(8,128)}), f32[16,22,128]{2,1,0:T(8,128)S(1)}, u32[]{:S(2)}, u32[]{:S(2)}) async-start(f32[16,22,128]{2,1,0:T(8,128)} %broadcast_in_dim.20), calls=%async_computation.9 | async-start | bytes 393216 | tf_op jit(solution)/shard_map/all_to_all | solution.py:387
  248.5 26.9 %all-to-all-start.4 = ((bf16[8,4,32,768]{3,2,1,0:T(8,128)(2,1)}), bf16[8,4,32,768]{3,2,1,0:T(8,128)(2,1)}, u32[]{:S(2)}, u32[]{:S(2)}) async-start(bf16[8,4,32,768]{3,2,1,0:T(8,128)(2,1)} %get-tuple-element.32), calls=%async_computation.4 | async-start | bytes 3145728 | tf_op jit(solution)/shard_map/all_to_all | solution.py:387
  276.5 17.3 %all-to-all-start.6 = ((bf16[16,30,768]{2,1,0:T(8,128)(2,1)}), bf16[16,30,768]{2,1,0:T(8,128)(2,1)S(1)}, u32[]{:S(2)}, u32[]{:S(2)}) async-start(bf16[16,30,768]{2,1,0:T(8,128)(2,1)} %broadcast_in_dim.18), calls=%async_computation.6 | async-start | bytes 1572864 | tf_op jit(solution)/shard_map/all_to_all | solution.py:387
  (29 other events, 77.4 us)

commit v2 on v1

v2 whole, which is shorter than its diff:
```python
import functools
import math

import jax
import jax.numpy as jnp
from jax import lax
from jax.experimental import pallas as pl
from jax.experimental.pallas import tpu as pltpu
from jax.sharding import Mesh, PartitionSpec as P

EPSILON = 1e-05
BF = jnp.bfloat16
F32 = jnp.float32
HD = 48
VMEM = 56 * 2**20
COL = ("z", "xh")
ROW = ("y", "core")
GROUP = ("y", "core", "smp")

NT = (((1,), (1,)), ((), ()))
NN = (((1,), (0,)), ((), ()))
TN = (((0,), (0,)), ((), ()))


def mm(a, b, dims):
    return lax.dot_general(a, b, dims, preferred_element_type=F32)


GG_ROWS = 64
TOP_AT = GG_ROWS + 2 * 256
BIAS_ROWS = TOP_AT + 16


def bias_kernel(w_ref, pair_ref, out_ref, acc_ref):
    heads, rows, keys = acc_ref.shape
    for block in range(rows // 16):
        piece = jnp.concatenate([pair_ref[block * 16 + k] for k in range(16)], axis=1)
        res = mm(w_ref[...], piece, NT)
        acc_ref[:, block * 16 : (block + 1) * 16, :] = res.reshape(heads, 16, keys)
    row_id = lax.broadcasted_iota(jnp.int32, (16, rows), 0)
    for group in range(heads // 2):
        tops = jnp.zeros((16, rows), F32)
        for half in range(2):
            tile = acc_ref[group * 2 + half].T
            top = jnp.max(tile, axis=0, keepdims=True)
            at = GG_ROWS + half * keys
            out_ref[group, at : at + keys, :] = (tile - top).astype(BF)
            one = top.astype(BF).astype(F32)
            two = (top - one).astype(BF).astype(F32)
            for k, term in enumerate((one, two, top - one - two)):
                tops = jnp.where(row_id == half * 3 + k, term, tops)
        out_ref[group, TOP_AT:, :] = tops.astype(BF)


def pair_bias(pair, w_pair):
    rows, keys, chans = pair.shape
    heads = w_pair.shape[1]
    eye = jnp.eye(16, dtype=BF)
    spread = (w_pair.T[:, None, None, :] * eye[None, :, :, None]).reshape(heads * 16, 16 * chans)
    step = 128
    return pl.pallas_call(
        bias_kernel,
        grid=(rows // step,),
        in_specs=[
            pl.BlockSpec(spread.shape, lambda i: (0, 0)),
            pl.BlockSpec((step, keys, chans), lambda i: (i, 0, 0)),
        ],
        out_specs=pl.BlockSpec((heads // 2, BIAS_ROWS, step), lambda i: (0, 0, i)),
        out_shape=jax.ShapeDtypeStruct((heads // 2, BIAS_ROWS, rows), BF),
        scratch_shapes=[pltpu.VMEM((heads, step, keys), F32)],
        compiler_params=pltpu.CompilerParams(vmem_limit_bytes=VMEM),
        cost_estimate=pl.CostEstimate(flops=2**34, bytes_accessed=2**25, transcendentals=0),
        name="pair_bias",
    )(spread, pair)


def prepare_kernel(core_ref, act_ref, gain_ref, w_ref, out_ref):
    samples, local, width = act_ref.shape
    act = act_ref[...].reshape(samples * local, width).astype(F32)
    centred = act - jnp.mean(act, axis=-1, keepdims=True)
    inv_std = lax.rsqrt(jnp.mean(centred * centred, axis=-1, keepdims=True) + EPSILON)
    norm = (centred * inv_std * gain_ref[...]).astype(BF)
    half = w_ref[pl.ds(pl.multiple_of(core_ref[0] * HD, 16), HD), :]
    for c in range(out_ref.shape[0]):
        out_ref[c, : samples * local, :] = norm
        out_ref[c, samples * local :, :] = half


def prepare(core, token_act, gain, w_out, cols):
    samples, local, width = token_act.shape
    vmem = pl.BlockSpec(memory_space=pltpu.VMEM)
    return pl.pallas_call(
        prepare_kernel,
        in_specs=[pl.BlockSpec(memory_space=pltpu.SMEM), vmem, vmem, vmem],
        out_shape=jax.ShapeDtypeStruct((cols, samples * local + HD, width), BF),
        compiler_params=pltpu.CompilerParams(vmem_limit_bytes=VMEM),
        name="prepare",
    )(core, token_act, gain, w_out)


def project_kernel(rows_ref, wq_ref, wk_ref, wv_ref, wg_ref, q_ref, kv_ref, g_ref):
    rows = rows_ref[...].reshape(256, rows_ref.shape[-1])
    q_ref[0] = mm(wq_ref[...], rows, NT).astype(BF)
    g_ref[0] = mm(wg_ref[...], rows, NT).astype(BF)
    keys = mm(wk_ref[...], rows, NT).astype(BF)
    values = mm(wv_ref[...], rows, NT).astype(BF)
    for h in range(2):
        kv_ref[0, h, :HD, :] = keys[h * HD : (h + 1) * HD, :]
        kv_ref[0, h, HD:, :] = values[h * HD : (h + 1) * HD, :]


def project(rows_in, samples, local, wq, wk, wv, wg):
    cols, _, width = rows_in.shape
    feat = wq.shape[0]
    tok = cols * local
    wspec = pl.BlockSpec((feat, width), lambda s: (0, 0))
    small = jax.ShapeDtypeStruct((samples, feat, tok), BF)
    small_spec = pl.BlockSpec((1, feat, tok), lambda s: (s, 0, 0))
    return pl.pallas_call(
        project_kernel,
        grid=(samples,),
        in_specs=[pl.BlockSpec((cols, local, width), lambda s: (0, s, 0))] + [wspec] * 4,
        out_specs=[small_spec, pl.BlockSpec((1, 2, feat, tok), lambda s: (s, 0, 0, 0)), small_spec],
        out_shape=[small, jax.ShapeDtypeStruct((samples, 2, feat, tok), BF), small],
        compiler_params=pltpu.CompilerParams(vmem_limit_bytes=VMEM),
        name="project",
    )(rows_in, wq, wk, wv, wg)


def whole_w(near, far, core):
    first = jnp.where(core == 0, near, far)
    second = jnp.where(core == 0, far, near)
    return jnp.concatenate([first, second], axis=0)


def gated_grad_kernel(core_ref, cot_ref, near_ref, far_ref, _, out_ref):
    count = cot_ref.shape[0]
    zeros = jnp.zeros((128 - 2 * HD, cot_ref.shape[1]), BF)
    for c in range(out_ref.shape[0]):
        weight = whole_w(near_ref[c], far_ref[c], core_ref[0])
        weight = jnp.concatenate([weight, zeros], axis=0)
        res = mm(cot_ref[...], weight, NT).astype(BF)
        out_ref[c, :, :128] = res[: count // 2]
        out_ref[c, :, 128:] = res[count // 2 :]


def gated_grad(core, cot, near, far, bias):
    cols, _, tok = bias.shape
    whole = lambda x: pl.BlockSpec(x.shape, lambda i: (0,) * x.ndim)
    return pl.pallas_call(
        gated_grad_kernel,
        grid=(1,),
        in_specs=[
            pl.BlockSpec(memory_space=pltpu.SMEM),
            whole(cot),
            whole(near),
            whole(far),
            pl.BlockSpec(memory_space=pl.ANY),
        ],
        out_specs=pl.BlockSpec((cols, GG_ROWS, tok), lambda i: (0, 0, 0)),
        out_shape=jax.ShapeDtypeStruct(bias.shape, BF),
        input_output_aliases={4: 0},
        compiler_params=pltpu.CompilerParams(vmem_limit_bytes=VMEM),
        name="gated_grad",
    )(core, cot, near, far, bias)


def slot_xor(t):
    return 2 * (t % 4) + t // 4


def attend_kernel(me_ref, bias_ref, q_ref, gate_ref, *refs):
    kv_refs = refs[:8]
    gated_ref, dq_ref, dgate_ref, dkv_own_ref, dkv_far_ref, dbias_ref = refs[8:14]
    s_scr, dp_scr = refs[14:]
    samples, _, tok = q_ref.shape
    head = pl.program_id(0)
    me = me_ref[0]
    scale = 1.0 / math.sqrt(HD)
    row_id = lax.broadcasted_iota(jnp.int32, (16, tok), 0)
    wanted = (row_id >= head * 3) & (row_id < head * 3 + 3)
    q = [q_ref[s] for s in range(samples)]
    sig, gg, gatt = [], [], []
    for s in range(samples):
        at = slice((s % 2) * 32, (s % 2) * 32 + 32)
        lanes = slice((s // 2) * 128, (s // 2) * 128 + 128)
        piece = bias_ref[:, at, lanes].astype(F32).reshape(tok, 128).T
        gg.append(jnp.where(head == 0, piece[:HD], piece[HD : 2 * HD]))
        sig.append(1.0 / (1.0 + jnp.exp(-gate_ref[s].astype(F32))))
        gatt.append((gg[s] * sig[s]).astype(BF))

    peak = [None] * samples
    for t in range(8):
        block = me ^ slot_xor(t)
        tops = bias_ref[block, TOP_AT:, :].astype(F32)
        top = jnp.sum(jnp.where(wanted, tops, 0.0), axis=0, keepdims=True)
        at = pl.ds(pl.multiple_of(GG_ROWS + head * 256, 64), 256)
        bias = bias_ref[block, at, :].astype(F32) + top
        for s in range(samples):
            score = mm(kv_refs[t][s, 0, :HD, :], q[s], TN) * scale + bias
            s_scr[s, t] = score
            high = jnp.max(score, axis=0, keepdims=True)
            peak[s] = high if t == 0 else jnp.maximum(peak[s], high)
    inv, dot = [], []
    for s in range(samples):
        total = jnp.zeros((1, tok), F32)
        weighted = jnp.zeros((1, tok), F32)
        for t in range(8):
            e = jnp.exp(s_scr[s, t] - peak[s])
            s_scr[s, t] = e
            dp = mm(kv_refs[t][s, 0, HD:, :], gatt[s], TN)
            dp_scr[s, t] = dp
            total = total + jnp.sum(e, axis=0, keepdims=True)
            weighted = weighted + jnp.sum(e * dp, axis=0, keepdims=True)
        inv.append(1.0 / total)
        dot.append(weighted * inv[s])
    pad = jnp.zeros((HD, tok), F32)
    pad2 = jnp.zeros((32, tok), F32)
    q_nat = [
        jnp.concatenate([q[s].astype(F32) * scale, pad, pad2], axis=0).T.astype(BF)
        for s in range(samples)
    ]
    g_nat = [
        jnp.concatenate([pad, gatt[s].astype(F32), pad2], axis=0).T.astype(BF)
        for s in range(samples)
    ]
    att = [jnp.zeros((HD, tok), F32)] * samples
    dq = [jnp.zeros((HD, tok), F32)] * samples
    for t in range(8):
        block = me ^ slot_xor(t)
        out_ref = dkv_own_ref if t < 4 else dkv_far_ref
        dbias = None
        for s in range(samples):
            prob = s_scr[s, t] * inv[s]
            prob_bf = prob.astype(BF)
            ds = prob * (dp_scr[s, t] - dot[s])
            dbias = ds if s == 0 else dbias + ds
            ds = ds.astype(BF)
            att[s] = att[s] + mm(kv_refs[t][s, 0, HD:, :], prob_bf, NN)
            dq[s] = dq[s] + mm(kv_refs[t][s, 0, :HD, :], ds, NN)
            dkv = mm(ds, q_nat[s], NN) + mm(prob_bf, g_nat[s], NN)
            out_ref[t % 4, s, 0] = dkv.T[: 2 * HD].astype(BF)
        dbias_ref[block, 0] = dbias.astype(BF)
    for s in range(samples):
        gated_ref[s] = (sig[s] * att[s]).astype(BF)
        dgate_ref[s] = (gg[s] * att[s] * sig[s] * (1.0 - sig[s])).astype(BF)
        dq_ref[s] = (dq[s] * scale).astype(BF)


def attend(me, bias, q, gate, kv):
    samples, feat, tok = q.shape
    heads = 2
    half = pl.BlockSpec((samples, HD, tok), lambda h: (0, h, 0))
    kv_spec = pl.BlockSpec((samples, 1, feat, tok), lambda h: (0, h, 0, 0))
    small = jax.ShapeDtypeStruct((samples, feat, tok), BF)
    dkv = jax.ShapeDtypeStruct((4, samples, heads, feat, tok), BF)
    dkv_spec = pl.BlockSpec((4, samples, 1, feat, tok), lambda h: (0, 0, h, 0, 0))
    return pl.pallas_call(
        attend_kernel,
        grid=(heads,),
        in_specs=[
            pl.BlockSpec(memory_space=pltpu.SMEM),
            pl.BlockSpec(bias.shape, lambda h: (0, 0, 0)),
            half,
            half,
        ]
        + [kv_spec] * 8,
        out_specs=[
            half,
            half,
            half,
            dkv_spec,
            dkv_spec,
            pl.BlockSpec((8, 1, 256, tok), lambda h: (0, h, 0, 0)),
        ],
        out_shape=[small, small, small, dkv, dkv, jax.ShapeDtypeStruct((8, heads, 256, tok), BF)],
        scratch_shapes=[pltpu.VMEM((samples, 8, 256, tok), F32)] * 2,
        compiler_params=pltpu.CompilerParams(vmem_limit_bytes=VMEM),
        cost_estimate=pl.CostEstimate(
            flops=2**34, bytes_accessed=20 * 2**20, transcendentals=2**22
        ),
        name="attend",
    )(me, bias, q, gate, *kv)


def fold_kernel(own_ref, far_ref, _, *out_refs):
    for k, out_ref in enumerate(out_refs):
        out_ref[...] = (own_ref[k].astype(F32) + far_ref[k].astype(F32)).astype(BF)


def fold(own, far, after):
    vmem = pl.BlockSpec(memory_space=pltpu.VMEM)
    return pl.pallas_call(
        fold_kernel,
        in_specs=[vmem, vmem, pl.BlockSpec(memory_space=pl.ANY)],
        out_shape=[jax.ShapeDtypeStruct(own.shape[1:], BF)] * own.shape[0],
        compiler_params=pltpu.CompilerParams(vmem_limit_bytes=VMEM),
        name="fold",
    )(own, far, after)


def norm_kernel(gated_ref, dq_ref, dg_ref, *refs):
    kv_refs = refs[:4]
    w_ref, part_ref, dcat_ref = refs[4:]
    dkv = kv_refs[0][0].astype(F32)
    for ref in kv_refs[1:]:
        dkv = dkv + ref[0].astype(F32)
    dkv = dkv.astype(BF)
    dcat = jnp.concatenate(
        [
            dq_ref[0],
            dkv[0, :HD],
            dkv[1, :HD],
            dkv[0, HD:],
            dkv[1, HD:],
            dg_ref[0],
        ],
        axis=0,
    )
    dcat_ref[0] = dcat
    cols, _, local, wide = part_ref.shape
    width = w_ref.shape[1]
    part = mm(dcat, w_ref[...], TN).astype(BF)
    part_ref[:, 0, :, :width] = part.reshape(cols, local, width)
    gated = jnp.concatenate([gated_ref[0], jnp.zeros((32, cols * local), BF)], axis=0)
    part_ref[:, 0, :, width:] = gated.astype(F32).T.astype(BF).reshape(cols, local, 128)


def norm_part(gated, dq, dg, kv_pieces, w_cat, cols):
    samples, feat, tok = dq.shape
    local = tok // cols
    all_feat, width = w_cat.shape
    half = pl.BlockSpec((1, feat, tok), lambda s: (s, 0, 0))
    kv_spec = pl.BlockSpec((1, 2, feat, tok), lambda s: (s, 0, 0, 0))
    return pl.pallas_call(
        norm_kernel,
        grid=(samples,),
        in_specs=[half, half, half]
        + [kv_spec] * 4
        + [pl.BlockSpec(w_cat.shape, lambda s: (0, 0))],
        out_specs=[
            pl.BlockSpec((cols, 1, local, width + 128), lambda s: (0, s, 0, 0)),
            pl.BlockSpec((1, all_feat, tok), lambda s: (s, 0, 0)),
        ],
        out_shape=[
            jax.ShapeDtypeStruct((cols, samples, local, width + 128), BF),
            jax.ShapeDtypeStruct((samples, all_feat, tok), BF),
        ],
        compiler_params=pltpu.CompilerParams(vmem_limit_bytes=VMEM),
        name="norm_part",
    )(gated, dq, dg, *kv_pieces, w_cat)


def weights_kernel(
    place_ref, dcat_ref, gated_ref, rows_ref, cot_ref, w_ref, gain_ref, grad_ref, gain_out_ref, acc
):
    step = pl.program_id(0)
    cols, local, width = rows_ref.shape
    dcat = dcat_ref[0]
    gated = gated_ref[0]
    grad = mm(dcat, rows_ref[...].reshape(cols * local, width), NN)
    grad_out = mm(gated, cot_ref[:, 0].reshape(cols * local, width), NN)
    four = dcat.shape[0]
    five = four + gated.shape[0]

    @pl.when(step == 0)
    def _():
        acc[:four, :] = grad
        acc[four:five, :] = grad_out
        acc[five:, :] = jnp.zeros((512 - five, width), F32)

    @pl.when(step > 0)
    def _():
        acc[:four, :] += grad
        acc[four:five, :] += grad_out

    @pl.when(step == pl.num_programs(0) - 1)
    def _():
        both = jnp.sum(acc[:four, :] * w_ref[...].astype(F32), axis=0, keepdims=True)
        gain_out_ref[...] = both / gain_ref[...]
        for p in range(8):
            grad_ref[p ^ place_ref[0]] = acc[p * 64 : (p + 1) * 64, :].astype(BF)


def weight_part(place, dcat, gated, rows_in, grad_rows, w_cat, gain):
    cols, samples, local, width = grad_rows.shape
    all_feat = w_cat.shape[0]
    feat, tok = gated.shape[1:]
    line = pl.BlockSpec((1, width), lambda s: (0, 0))
    return pl.pallas_call(
        weights_kernel,
        grid=(samples,),
        in_specs=[
            pl.BlockSpec(memory_space=pltpu.SMEM),
            pl.BlockSpec((1, all_feat, tok), lambda s: (s, 0, 0)),
            pl.BlockSpec((1, feat, tok), lambda s: (s, 0, 0)),
            pl.BlockSpec((cols, local, width), lambda s: (0, s, 0)),
            pl.BlockSpec((cols, 1, local, width), lambda s: (0, s, 0, 0)),
            pl.BlockSpec(w_cat.shape, lambda s: (0, 0)),
            line,
        ],
        out_specs=[pl.BlockSpec((8, 64, width), lambda s: (0, 0, 0)), line],
        out_shape=[
            jax.ShapeDtypeStruct((8, 64, width), BF),
            jax.ShapeDtypeStruct((1, width), F32),
        ],
        scratch_shapes=[pltpu.VMEM((512, width), F32)],
        compiler_params=pltpu.CompilerParams(vmem_limit_bytes=VMEM),
        name="weight_part",
    )(place, dcat, gated, rows_in, grad_rows, w_cat, gain)


def finish_kernel(core_ref, recv_ref, near_ref, far_ref, act_ref, cot_ref, gain_ref, out_ref, grad_ref):
    cols, samples, local, wide = recv_ref.shape
    width = act_ref.shape[-1]
    count = samples * local
    act = act_ref[...].reshape(count, width).astype(F32)
    cot = cot_ref[...].reshape(count, width).astype(F32)
    total = act
    grad_norm = jnp.zeros((count, width), F32)
    for c in range(cols):
        gated = recv_ref[c, :, :, width:].reshape(count, wide - width)[:, : 2 * HD]
        total = total + mm(gated, whole_w(near_ref[c], far_ref[c], core_ref[0]), NN)
        grad_norm = grad_norm + recv_ref[c, :, :, :width].reshape(count, width).astype(F32)
    out_ref[...] = total.astype(BF).reshape(samples, local, width)
    centred = act - jnp.mean(act, axis=-1, keepdims=True)
    inv_std = lax.rsqrt(jnp.mean(centred * centred, axis=-1, keepdims=True) + EPSILON)
    normed = centred * inv_std
    hat = grad_norm * gain_ref[...]
    back = inv_std * (
        hat
        - jnp.mean(hat, axis=-1, keepdims=True)
        - normed * jnp.mean(hat * normed, axis=-1, keepdims=True)
    )
    grad_ref[...] = (cot + back).astype(BF).reshape(samples, local, width)


def finish(core, recv, near, far, token_act, grad_out, gain):
    vmem = pl.BlockSpec(memory_space=pltpu.VMEM)
    return pl.pallas_call(
        finish_kernel,
        in_specs=[pl.BlockSpec(memory_space=pltpu.SMEM)] + [vmem] * 6,
        out_shape=[jax.ShapeDtypeStruct(token_act.shape, BF)] * 2,
        compiler_params=pltpu.CompilerParams(vmem_limit_bytes=VMEM),
        name="finish",
    )(core, recv, near, far, token_act, grad_out, gain)


def unpack_kernel(place_ref, near_ref, far_ref, *refs):
    outs, scr = refs[:5], refs[5]
    for p in range(4):
        slot = p ^ (place_ref[0] & 3)
        first = near_ref[slot].astype(F32)
        second = far_ref[slot].astype(F32)
        low = place_ref[0] < 4
        scr[p * 64 : (p + 1) * 64, :] = jnp.where(low, first, second)
        scr[256 + p * 64 : 256 + (p + 1) * 64, :] = jnp.where(low, second, first)
    feat = outs[4].shape[0]
    for k in range(5):
        outs[k][...] = scr[k * feat : (k + 1) * feat, :]


def unpack(place, near, far, feat):
    width = near.shape[-1]
    return pl.pallas_call(
        unpack_kernel,
        in_specs=[
            pl.BlockSpec(memory_space=pltpu.SMEM),
            pl.BlockSpec(memory_space=pltpu.VMEM),
            pl.BlockSpec(memory_space=pltpu.VMEM),
        ],
        out_shape=[jax.ShapeDtypeStruct((feat, width), F32)] * 5,
        scratch_shapes=[pltpu.VMEM((512, width), F32)],
        compiler_params=pltpu.CompilerParams(vmem_limit_bytes=VMEM),
        name="unpack",
    )(place, near, far)


def wpair_kernel(db_ref, pair_ref, out_ref, db_scr, acc_ref):
    step = pair_ref.shape[0]
    chans = pair_ref.shape[2]
    heads = db_scr.shape[0]

    @pl.when(pl.program_id(0) == 0)
    def _():
        acc_ref[...] = jnp.zeros_like(acc_ref)

    for h in range(heads):
        db_scr[h] = db_ref[h // 2, h % 2].astype(F32).T.astype(BF)
    for block in range(step // 16):
        left = db_scr[:, block * 16 : (block + 1) * 16, :].reshape(heads * 16, db_scr.shape[2])
        for k in range(0, 16, 2):
            pair = jnp.concatenate(
                [pair_ref[block * 16 + k], pair_ref[block * 16 + k + 1]], axis=1
            )
            at = slice(k * chans, (k + 2) * chans)
            acc_ref[:, at] += mm(left, pair, NN)

    @pl.when(pl.program_id(0) == pl.num_programs(0) - 1)
    def _():
        total = jnp.zeros((heads, chans), F32)
        row_id = lax.broadcasted_iota(jnp.int32, (heads, 16, chans), 1)
        for k in range(16):
            piece = acc_ref[:, k * chans : (k + 1) * chans].reshape(heads, 16, chans)
            total = total + jnp.sum(jnp.where(row_id == k, piece, 0.0), axis=1)
        out_ref[...] = total


def wpair_part(dbias, pair):
    groups, per, keys, rows = dbias.shape
    heads = groups * per
    chans = pair.shape[2]
    step = 128
    return pl.pallas_call(
        wpair_kernel,
        grid=(rows // step,),
        in_specs=[
            pl.BlockSpec((groups, per, keys, step), lambda i: (0, 0, 0, i)),
            pl.BlockSpec((step, keys, chans), lambda i: (i, 0, 0)),
        ],
        out_specs=pl.BlockSpec((heads, chans), lambda i: (0, 0)),
        out_shape=jax.ShapeDtypeStruct((heads, chans), F32),
        scratch_shapes=[
            pltpu.VMEM((heads, step, keys), BF),
            pltpu.VMEM((heads * 16, 16 * chans), F32),
        ],
        compiler_params=pltpu.CompilerParams(vmem_limit_bytes=VMEM),
        cost_estimate=pl.CostEstimate(flops=2**32, bytes_accessed=20 * 2**20, transcendentals=0),
        name="wpair_part",
    )(dbias, pair)


def exchange(x, axes):
    return lax.all_to_all(x, axes, 0, 0, tiled=True)


def gather(x, axes, count):
    return exchange(jnp.broadcast_to(x[None], (count,) + x.shape), axes)


def swap(x, axis, count, k):
    return lax.ppermute(x, axis, [(i, i ^ k) for i in range(count)])


def add_bf(*terms):
    total = terms[0].astype(F32)
    for term in terms[1:]:
        total = total + term.astype(F32)
    return total.astype(BF)


def add_four(x, axes):
    one, two, three = (swap(x, axes, 4, k) for k in range(1, 4))
    return (x + one) + (two + three)


def on_device(
    token_act, pair_rep, norm_gain, w_pair, w_query, w_key, w_value, w_gate, w_out, grad_out
):
    samples, local, width = token_act.shape
    feat = w_out.shape[0]
    cols = 8
    count = samples * local
    y, core, smp = (lax.axis_index(name) for name in ("y", "core", "smp"))
    me = jnp.full((1,), y * 2 + core, jnp.int32)
    which = jnp.full((1,), core, jnp.int32)
    place = jnp.full((1,), core * 4 + y, jnp.int32)

    load = prepare(which, token_act, norm_gain[None, :], w_out, cols)
    rows_in = exchange(load, COL)
    bias = pair_bias(pair_rep, w_pair)
    rows_in, bias = lax.optimization_barrier((rows_in, bias))
    w_near = rows_in[:, count:]
    w_far = swap(w_near, "core", 2, 1)
    bias = gated_grad(which, grad_out.reshape(count, width), w_near, w_far, bias)
    bias = exchange(bias, COL)

    grad_rows = gather(grad_out, COL, cols)

    wq, wk, wv, wg = w_query.T, w_key.T, w_value.T, w_gate.T
    q, kv_own, gate = project(rows_in, samples, local, wq, wk, wv, wg)
    near = [kv_own] + [swap(kv_own, "y", 4, k) for k in range(1, 4)]
    far = [swap(x, "core", 2, 1) for x in near]

    gated, dq, dgate, dkv_own, dkv_far, dbias = attend(me, bias, q, gate, near + far)
    dbias = exchange(dbias, COL)
    dkv = fold(dkv_own, swap(dkv_far, "core", 2, 1), grad_rows)
    pieces = [dkv[0]] + [swap(dkv[k], "y", 4, k) for k in range(1, 4)]
    w_cat = jnp.concatenate([wq, wk, wv, wg], axis=0)
    part, dcat = norm_part(gated, dq, dgate, pieces, w_cat, cols)
    recv = exchange(part, COL)
    blocks, gain_part = weight_part(
        place, dcat, gated, rows_in, grad_rows, w_cat, norm_gain[None, :]
    )

    blocks = add_bf(blocks[:4], swap(blocks[4:], "core", 2, 1))
    mine = add_bf(blocks[0], *(swap(blocks[k], "y", 4, k) for k in range(1, 4)))
    wpair = wpair_part(dbias, pair_rep)
    tiny = jnp.concatenate([wpair.reshape(16, 128), gain_part.reshape(6, 128)], axis=0)
    tiny = add_four(tiny, "y")
    tiny = tiny + swap(tiny, "core", 2, 1)

    tiny, mine, recv = lax.optimization_barrier((tiny, mine, recv))
    mine = add_bf(mine, swap(mine, "smp", 2, 1))
    tiny = jnp.sum(gather(tiny, COL + ("smp",), 16), axis=0)
    quad = jnp.stack([mine] + [swap(mine, "y", 4, k) for k in range(1, 4)])
    grads = unpack(place, quad, swap(quad, "core", 2, 1), feat)
    grads = [x.T for x in grads[:4]] + [grads[4]]

    block_out, grad_act = finish(
        which, recv, w_near, w_far, token_act, grad_out, norm_gain[None, :]
    )
    return (block_out, grad_act, *grads, tiny[:16].T, tiny[16:].reshape(width))


def solution(mesh):
    fine = Mesh(mesh.devices.reshape(4, 2, 4, 2, 2), ("y", "core", "z", "xh", "smp"))
    tokens = P("smp", ROW + COL, None)
    split_last = P(None, COL)
    return jax.shard_map(
        on_device,
        mesh=fine,
        in_specs=(
            tokens,
            P(ROW, COL, None),
            P(),
            P(),
            split_last,
            split_last,
            split_last,
            split_last,
            P(COL, None),
            tokens,
        ),
        out_specs=(
            tokens,
            tokens,
            split_last,
            split_last,
            split_last,
            split_last,
            P(COL, None),
            P(),
            P(),
        ),
        check_vma=False,
    )
```

time: 296 us -> 215 us (0.73)
  blocking collectives: 46.8 us -> 0 us
  waiting for transfers between devices: 92.3 us -> 58.7 us
  Pallas kernels: 55.7 us -> 70.6 us
  local copies, waits for them, and re-layouts: 25.2 us -> 12.5 us
  other arithmetic: 11.1 us -> 2.06 us
  starting transfers between devices: 62.9 us -> 68.9 us
    all_to_all x8 -> x6, waiting for transfers between devices: 86.9 us -> 19.4 us  [exchange(): return lax.all_to_all(x, axes, 0, 0, tiled=True)]
    all_to_all x2 -> x0, blocking collectives: 46.8 us -> none  [exchange(): return lax.all_to_all(x, axes, 0, 0, tiled=True)]
    ppermute x11 -> x25, waiting for transfers between devices: 5.44 us -> 39.3 us  [swap(): return lax.ppermute(x, axis, [(i, i ^ k) for i in range(count)])]
    pallas_call x4 -> x8, Pallas kernels: 33.4 us -> 45.1 us  [the longest x1 20.5 us: attend(): pl.pallas_call(attend_kernel, grid=(heads,), in_specs=[pl.BlockSpec(memor...]
    unnamed x69 -> x47, local copies, waits for them, and re-layouts: 16.7 us -> 6.62 us
    ppermute x11 -> x25, starting transfers between devices: 23.9 us -> 32.4 us  [swap(): return lax.ppermute(x, axis, [(i, i ^ k) for i in range(count)])]
    reduce_sum x8 -> x1, other arithmetic: 4.48 us -> 0.02 us  [on_device(): tiny = jnp.sum(gather(tiny, COL + ('smp',), 16), axis=0)]
    convert_element_type x3, other arithmetic: 4.44 us -> 0.18 us  [add_bf(): return total.astype(BF)]
  transfers between devices with their start and end apart: 19 -> 31, of which waited for: 9 -> 14; matrix products, arithmetic and copies ran while one was open for 4% -> 4% of each run, Pallas kernels for 9% -> 30%
where the time goes in v2:
time: 215 us; the launch traced here: 214 us
  Pallas kernels  70.6 us (33%)
  starting transfers between devices  68.9 us (32%)
  waiting for transfers between devices  58.7 us (27%)
  local copies, waits for them, and re-layouts  12.5 us (6%)
    ppermute x25, waiting for transfers between devices, swap(): return lax.ppermute(x, axis, [(i, i ^ k) for i in range(count)])  39.3 us
    all_to_all x6, starting transfers between devices, exchange(): return lax.all_to_all(x, axes, 0, 0, tiled=True)  36.4 us
    ppermute x25, starting transfers between devices, swap(): return lax.ppermute(x, axis, [(i, i ^ k) for i in range(count)])  32.4 us
    pallas_call x1, Pallas kernels, attend(): pl.pallas_call(attend_kernel, grid=(heads,), in_specs=[pl.BlockSpec(memor...  20.5 us
    all_to_all x6, waiting for transfers between devices, exchange(): return lax.all_to_all(x, axes, 0, 0, tiled=True)  19.4 us
    pallas_call x1, Pallas kernels, pair_bias(): pl.pallas_call(bias_kernel, grid=(rows // step,), in_specs=[pl.BlockSpec(...  10.5 us
    pallas_call x1, Pallas kernels, wpair_part(): pl.pallas_call(wpair_kernel, grid=(rows // step,), in_specs=[pl.BlockSpec...  10 us
    unnamed x47, local copies, waits for them, and re-layouts  6.62 us
  transfers between devices with their start and end apart: 31, of which 14 were waited for; matrix products, arithmetic and copies ran while one was open for 4% of the time, Pallas kernels for 30%

profile of v2, /device:TPU:1, one launch (start us, length us, event | category | flops | bytes accessed | tf_op | source)
XLA Modules:
  0.0 213.6 jit_solution(15083764102881646733)
XLA Ops:
  1.9 2.7 %prepare.1 = bf16[8,176,768]{2,1,0:T(8,128)(2,1)} custom-call(s32[1]{0:T(128)} %bitcast.core_ref, bf16[4,32,768]{2,1,0:T(8,128)(2,1)} %act_ref.3, f32[1,768]{1,0:T(1,128)} %broadcast_in_dim.14.gain_ref, bf16[96,768]{1,0:T(8,128)(2,1)} %w_ref.1), custom_call_target="tpu_custom_call" | custom-call | tf_op jit(solution)/shard_map/prepare/pallas_call | solution.py:92
  4.6 8.5 %all-to-all-start = ((bf16[8,176,768]{2,1,0:T(8,128)(2,1)}), bf16[8,176,768]{2,1,0:T(8,128)(2,1)S(1)}, u32[]{:S(2)}, u32[]{:S(2)}) async-start(bf16[8,176,768]{2,1,0:T(8,128)(2,1)} %prepare.1), calls=%async_computation | async-start | bytes 4325376 | tf_op jit(solution)/shard_map/all_to_all | solution.py:534
  14.5 10.5 %pair_bias.1._ = bf16[8,592,256]{2,1,0:T(8,128)(2,1)} custom-call(bf16[256,2048]{1,0:T(8,128)(2,1)} %bitcast.40, bf16[256,256,128]{2,1,0:T(8,128)(2,1)} %pair_ref.3), custom_call_target="tpu_custom_call" | custom-call | flops 17179869184 | bytes 33554432 | tf_op jit(solution)/shard_map/pair_bias/pallas_call | solution.py:61
  25.0 16.3 %all-to-all-done.rows_ref = bf16[8,176,768]{2,1,0:T(8,128)(2,1)S(1)} async-done(((bf16[8,176,768]{2,1,0:T(8,128)(2,1)}), bf16[8,176,768]{2,1,0:T(8,128)(2,1)S(1)}, u32[]{:S(2)}, u32[]{:S(2)}) %all-to-all-start) | async-done | bytes 2162720 | tf_op jit(solution)/shard_map/all_to_all | solution.py:534
  45.8 2.6 %gated_grad.1 = bf16[8,592,256]{2,1,0:T(8,128)(2,1)} custom-call(s32[1]{0:T(128)} %bitcast.core_ref, bf16[128,768]{1,0:T(8,128)(2,1)} %bitcast.39, bf16[8,48,768]{2,1,0:T(8,128)(2,1)} %copy-done.3, bf16[8,48,768]{2,1,0:T(8,128)(2,1)} %copy-done.5, bf16[8,592,256]{2,1,0:T(8,128)(2,1)} %pair_bias.1._), custom_call_target="tpu_custom_call", output_to_operand_aliasing={{}: (4, {})} | custom-call | tf_op jit(solution)/shard_map/gated_grad/pallas_call | solution.py:150
  48.4 3.6 %all-to-all-start.1 = ((bf16[8,592,256]{2,1,0:T(8,128)(2,1)}), bf16[8,592,256]{2,1,0:T(8,128)(2,1)S(1)}, u32[]{:S(2)}, u32[]{:S(2)}) async-start(bf16[8,592,256]{2,1,0:T(8,128)(2,1)} %gated_grad.1), calls=%async_computation.1 | async-start | bytes 4849664 | tf_op jit(solution)/shard_map/all_to_all | solution.py:534
  52.0 4.9 %project.1 = (bf16[4,96,256]{2,1,0:T(8,128)(2,1)}, bf16[4,2,96,256]{3,2,1,0:T(8,128)(2,1)}, bf16[4,96,256]{2,1,0:T(8,128)(2,1)}) custom-call(bf16[8,176,768]{2,1,0:T(8,128)(2,1)} %copy-done, bf16[96,768]{1,0:T(8,128)(2,1)} %bitcast.41, bf16[96,768]{1,0:T(8,128)(2,1)} %bitcast.43, bf16[96,768]{1,0:T(8,128)(2,1)} %bitcast.45, bf16[96,768]{1,0:T(8,128)(2,1)} %bitcast.47), custom_call_target="tpu_custom_call" | custom-call | tf_op jit(solution)/shard_map/project/pallas_call | solution.py:119
  58.2 2.6 %collective-permute-start.2 = (bf16[4,2,96,256]{3,2,1,0:T(8,128)(2,1)}, bf16[4,2,96,256]{3,2,1,0:T(8,128)(2,1)S(1)}, u32[]{:S(2)}, u32[]{:S(2)}) collective-permute-start(bf16[4,2,96,256]{3,2,1,0:T(8,128)(2,1)} %get-tuple-element.42.refs_0_), channel_id=1, source_target_pairs={{0,64},{32,96},{64,0},{96,32},{1,65},{33,97},{65,1},{97,33},{2,66}... | collective-permute-start | bytes 1179656 | tf_op jit(solution)/shard_map/ppermute | solution.py:542
  62.0 5.6 %collective-permute-done.1.refs_1_ = bf16[4,2,96,256]{3,2,1,0:T(8,128)(2,1)S(1)} collective-permute-done((bf16[4,2,96,256]{3,2,1,0:T(8,128)(2,1)}, bf16[4,2,96,256]{3,2,1,0:T(8,128)(2,1)S(1)}, u32[]{:S(2)}, u32[]{:S(2)}) %collective-permute-start.1) | collective-permute-done | bytes 393248 | tf_op jit(solution)/shard_map/ppermute | solution.py:542
  69.5 8.9 %collective-permute-done.2.refs_2_ = bf16[4,2,96,256]{3,2,1,0:T(8,128)(2,1)S(1)} collective-permute-done((bf16[4,2,96,256]{3,2,1,0:T(8,128)(2,1)}, bf16[4,2,96,256]{3,2,1,0:T(8,128)(2,1)S(1)}, u32[]{:S(2)}, u32[]{:S(2)}) %collective-permute-start.2) | collective-permute-done | bytes 393248 | tf_op jit(solution)/shard_map/ppermute | solution.py:542
  85.6 5.2 %all-to-all-start.3 = ((bf16[8,4,32,768]{3,2,1,0:T(8,128)(2,1)}), bf16[8,4,32,768]{3,2,1,0:T(8,128)(2,1)S(1)}, u32[]{:S(2)}, u32[]{:S(2)}) async-start(bf16[8,4,32,768]{3,2,1,0:T(8,128)(2,1)} %broadcast_in_dim.32), calls=%async_computation.3 | async-start | bytes 3145728 | tf_op jit(solution)/shard_map/all_to_all | solution.py:534
  90.8 20.5 %attend.1 = (bf16[4,96,256]{2,1,0:T(8,128)(2,1)}, bf16[4,96,256]{2,1,0:T(8,128)(2,1)}, bf16[4,96,256]{2,1,0:T(8,128)(2,1)}, bf16[4,4,2,96,256]{4,3,2,1,0:T(8,128...) custom-call(s32[1]{0:T(128)} %bitcast.1.me_ref, bf16[8,592,256]{2,1,0:T(8,128)(2,1)} %copy-done.4, ...), custom_call_target="tpu_custom_call" | custom-call | flops 17179869184 | bytes 20971520 | tf_op jit(solution)/shard_map/attend/pallas_call | solution.py:258
  114.6 5.1 %all-to-all-start.2 = ((bf16[8,2,256,256]{3,2,1,0:T(8,128)(2,1)}), bf16[8,2,256,256]{3,2,1,0:T(8,128)(2,1)}, u32[]{:S(2)}, u32[]{:S(2)}) async-start(bf16[8,2,256,256]{3,2,1,0:T(8,128)(2,1)} %get-tuple-element.43), calls=%async_computation.2 | async-start | bytes 4194304 | tf_op jit(solution)/shard_map/all_to_all | solution.py:534
  120.9 3.2 %fold.1 = (bf16[4,2,96,256]{3,2,1,0:T(8,128)(2,1)}, bf16[4,2,96,256]{3,2,1,0:T(8,128)(2,1)}, bf16[4,2,96,256]{3,2,1,0:T(8,128)(2,1)}, bf16[4,2,96,256]{3,2,1,0:T(8,128)(2,1)}) custom-call(bf16[4,4,2,96,256]{4,3,2,1,0:T(8,128)(2,1)} %get-tuple-element.47.own_ref, bf16[4,4,2,96,256]{4,3,2,1,0:T(8,128)(2,1)} %copy-done.8, bf16[8,4,32,768]{3,2,1,0:T(8,128)(2,1)} %copy-done.1), custom_call_target="tpu_custom_call" | custom-call | tf_op jit(solution)/shard_map/fold/pallas_call | solution.py:293
  128.0 8.3 %collective-permute-done.10.refs_2_ = bf16[4,2,96,256]{3,2,1,0:T(8,128)(2,1)S(1)} collective-permute-done((bf16[4,2,96,256]{3,2,1,0:T(8,128)(2,1)}, bf16[4,2,96,256]{3,2,1,0:T(8,128)(2,1)S(1)}, u32[]{:S(2)}, u32[]{:S(2)}) %collective-permute-start.10) | collective-permute-done | bytes 393248 | tf_op jit(solution)/shard_map/ppermute | solution.py:542
  136.3 9.1 %collective-permute-done.11.refs_3_ = bf16[4,2,96,256]{3,2,1,0:T(8,128)(2,1)S(1)} collective-permute-done((bf16[4,2,96,256]{3,2,1,0:T(8,128)(2,1)}, bf16[4,2,96,256]{3,2,1,0:T(8,128)(2,1)S(1)}, u32[]{:S(2)}, u32[]{:S(2)}) %collective-permute-start.11) | collective-permute-done | bytes 393248 | tf_op jit(solution)/shard_map/ppermute | solution.py:542
  146.3 5.2 %norm_part.1 = (bf16[8,4,32,896]{3,2,1,0:T(8,128)(2,1)}, bf16[4,384,256]{2,1,0:T(8,128)(2,1)}) custom-call(bf16[4,96,256]{2,1,0:T(8,128)(2,1)} %get-tuple-element.44.gated_ref, bf16[4,96,256]{2,1,0:T(8,128)(2,1)} %get-tuple-element.45.dq_ref, bf16[4,96,256]{2,1,0:T(8,128)(2,1)} %get-tuple-element.46.dg_ref, ...), custom_call_target="tpu_custom_call" | custom-call | tf_op jit(solution)/shard_map/norm_part/pallas_call | solution.py:335
  151.5 6.6 %all-to-all-start.4 = ((bf16[8,4,32,896]{3,2,1,0:T(8,128)(2,1)}), bf16[8,4,32,896]{3,2,1,0:T(8,128)(2,1)S(1)}, u32[]{:S(2)}, u32[]{:S(2)}) async-start(bf16[8,4,32,896]{3,2,1,0:T(8,128)(2,1)} %get-tuple-element.56), calls=%async_computation.4 | async-start | bytes 3670016 | tf_op jit(solution)/shard_map/all_to_all | solution.py:534
  158.0 5.4 %weight_part.1 = (bf16[8,64,768]{2,1,0:T(8,128)(2,1)}, f32[1,768]{1,0:T(1,128)}) custom-call(s32[1]{0:T(128)} %bitcast.8.place_ref, bf16[4,384,256]{2,1,0:T(8,128)(2,1)} %get-tuple-element.53.dcat_ref, bf16[4,96,256]{2,1,0:T(8,128)(2,1)} %get-tuple-element.44.gated_ref, bf16[8,176,768]{2,1,0:T(8,128)(2,1)} %copy-done, bf16[8,4,32,768]{3,2,1,0:T(8,128)(2,1)} %copy-done.1, ...), custom_call_target="tpu_custom_call" | custom-call | tf_op jit(solution)/shard_map/weight_part/pallas_call | solution.py:390
  165.6 10.0 %wpair_part.1 = f32[16,128]{1,0:T(8,128)} custom-call(bf16[8,2,256,256]{3,2,1,0:T(8,128)(2,1)} %all-to-all-done.2.db_ref, bf16[256,256,128]{2,1,0:T(8,128)(2,1)} %pair_ref.3), custom_call_target="tpu_custom_call" | custom-call | flops 4294967296 | bytes 20971520 | tf_op jit(solution)/shard_map/wpair_part/pallas_call | solution.py:514
  177.0 2.6 %collective-permute-start.13 = (f32[22,128]{1,0:T(8,128)S(1)}, f32[22,128]{1,0:T(8,128)S(1)}, u32[]{:S(2)}, u32[]{:S(2)}) collective-permute-start(f32[22,128]{1,0:T(8,128)S(1)} %pad_maximum_fusion.2), channel_id=1, source_target_pairs={{0,64},{32,96},{64,0},{96,32},{1,65},{33,97},{65,1},{97,33},{2,66}... | collective-permute-start | bytes 33800 | tf_op jit(solution)/shard_map/ppermute | solution.py:542
  180.5 3.2 %collective-permute-start.18 = (bf16[64,768]{1,0:T(8,128)(2,1)S(1)}, bf16[64,768]{1,0:T(8,128)(2,1)S(1)}, u32[]{:S(2)}, u32[]{:S(2)}) collective-permute-start(bf16[64,768]{1,0:T(8,128)(2,1)S(1)} %get-tuple-element.69), channel_id=1, source_target_pairs={{0,64},{32,96},{64,0},{96,32},{1,65},{33,97},{65,1},{97,33},{2,66}... | collective-permute-start | bytes 294920 | tf_op jit(solution)/shard_map/ppermute | solution.py:542
  191.3 7.5 %all-to-all-start.5 = ((f32[16,22,128]{2,1,0:T(8,128)}), f32[16,22,128]{2,1,0:T(8,128)S(1)}, u32[]{:S(2)}, u32[]{:S(2)}) async-start(f32[16,22,128]{2,1,0:T(8,128)} %broadcast_in_dim.33), calls=%async_computation.5 | async-start | bytes 393216 | tf_op jit(solution)/shard_map/all_to_all | solution.py:534
  202.8 3.4 %finish.1 = (bf16[4,32,768]{2,1,0:T(8,128)(2,1)}, bf16[4,32,768]{2,1,0:T(8,128)(2,1)}) custom-call(s32[1]{0:T(128)} %bitcast.core_ref, bf16[8,4,32,896]{3,2,1,0:T(8,128)(2,1)} %copy-done.2, bf16[8,48,768]{2,1,0:T(8,128)(2,1)} %copy-done.3, bf16[8,48,768]{2,1,0:T(8,128)(2,1)} %copy-done.5, bf16[4,32,768]{2,1,0:T(8,128)(2,1)} %act_ref.3, ...), custom_call_target="tpu_custom_call" | custom-call | tf_op jit(solution)/shard_map/finish/pallas_call | solution.py:440
  (116 shorter events, 51.4 us)
Async XLA Ops:
  4.6 36.7 %all-to-all-start = ((bf16[8,176,768]{2,1,0:T(8,128)(2,1)}), bf16[8,176,768]{2,1,0:T(8,128)(2,1)S(1)}, u32[]{:S(2)}, u32[]{:S(2)}) async-start(bf16[8,176,768]{2,1,0:T(8,128)(2,1)} %prepare.1), calls=%async_computation | async-start | bytes 4325376 | tf_op jit(solution)/shard_map/all_to_all | solution.py:534
  48.4 35.3 %all-to-all-start.1 = ((bf16[8,592,256]{2,1,0:T(8,128)(2,1)}), bf16[8,592,256]{2,1,0:T(8,128)(2,1)S(1)}, u32[]{:S(2)}, u32[]{:S(2)}) async-start(bf16[8,592,256]{2,1,0:T(8,128)(2,1)} %gated_grad.1), calls=%async_computation.1 | async-start | bytes 4849664 | tf_op jit(solution)/shard_map/all_to_all | solution.py:534
  56.9 10.6 %collective-permute-start.1 = (bf16[4,2,96,256]{3,2,1,0:T(8,128)(2,1)}, bf16[4,2,96,256]{3,2,1,0:T(8,128)(2,1)S(1)}, u32[]{:S(2)}, u32[]{:S(2)}) collective-permute-start(bf16[4,2,96,256]{3,2,1,0:T(8,128)(2,1)} %get-tuple-element.42.refs_0_), channel_id=1, source_target_pairs={{0,32},{32,0},{64,96},{96,64},{1,33},{33,1},{65,97},{97,65},{2,34}... | collective-permute-start | bytes 1179656 | tf_op jit(solution)/shard_map/ppermute | solution.py:542
  58.2 20.2 %collective-permute-start.2 = (bf16[4,2,96,256]{3,2,1,0:T(8,128)(2,1)}, bf16[4,2,96,256]{3,2,1,0:T(8,128)(2,1)S(1)}, u32[]{:S(2)}, u32[]{:S(2)}) collective-permute-start(bf16[4,2,96,256]{3,2,1,0:T(8,128)(2,1)} %get-tuple-element.42.refs_0_), channel_id=1, source_target_pairs={{0,64},{32,96},{64,0},{96,32},{1,65},{33,97},{65,1},{97,33},{2,66}... | collective-permute-start | bytes 1179656 | tf_op jit(solution)/shard_map/ppermute | solution.py:542
  60.9 19.6 %collective-permute-start.3 = (bf16[4,2,96,256]{3,2,1,0:T(8,128)(2,1)}, bf16[4,2,96,256]{3,2,1,0:T(8,128)(2,1)}, u32[]{:S(2)}, u32[]{:S(2)}) collective-permute-start(bf16[4,2,96,256]{3,2,1,0:T(8,128)(2,1)} %get-tuple-element.42.refs_0_), channel_id=1, source_target_pairs={{0,96},{32,64},{64,32},{96,0},{1,97},{33,65},{65,33},{97,1},{2,98}... | collective-permute-start | bytes 1179656 | tf_op jit(solution)/shard_map/ppermute | solution.py:542
  60.9 29.9 %collective-permute-start.4 = (bf16[4,2,96,256]{3,2,1,0:T(8,128)(2,1)}, bf16[4,2,96,256]{3,2,1,0:T(8,128)(2,1)}, u32[]{:S(2)}, u32[]{:S(2)}) collective-permute-start(bf16[4,2,96,256]{3,2,1,0:T(8,128)(2,1)} %get-tuple-element.42.refs_0_), channel_id=1, source_target_pairs={{0,16},{16,0},{1,17},{17,1},{2,18},{18,2},{3,19},{19,3},{4,20},{20... | collective-permute-start | bytes 1179656 | tf_op jit(solution)/shard_map/ppermute | solution.py:542
  67.6 23.2 %collective-permute-start.5 = (bf16[4,2,96,256]{3,2,1,0:T(8,128)(2,1)S(1)}, bf16[4,2,96,256]{3,2,1,0:T(8,128)(2,1)}, u32[]{:S(2)}, u32[]{:S(2)}) collective-permute-start(bf16[4,2,96,256]{3,2,1,0:T(8,128)(2,1)S(1)} %collective-permute-done.1.refs_1_), channel_id=1, source_target_pairs={{0,16},{16,0},{1,17},{17,1},{2,18},{18,2},{3,19},{19,3},{4,20},{20... | collective-permute-start | bytes 1179656 | tf_op jit(solution)/shard_map/ppermute | solution.py:542
  78.4 12.4 %collective-permute-start.6 = (bf16[4,2,96,256]{3,2,1,0:T(8,128)(2,1)S(1)}, bf16[4,2,96,256]{3,2,1,0:T(8,128)(2,1)}, u32[]{:S(2)}, u32[]{:S(2)}) collective-permute-start(bf16[4,2,96,256]{3,2,1,0:T(8,128)(2,1)S(1)} %collective-permute-done.2.refs_2_), channel_id=1, source_target_pairs={{0,16},{16,0},{1,17},{17,1},{2,18},{18,2},{3,19},{19,3},{4,20},{20... | collective-permute-start | bytes 1179656 | tf_op jit(solution)/shard_map/ppermute | solution.py:542
  80.5 10.3 %collective-permute-start.7 = (bf16[4,2,96,256]{3,2,1,0:T(8,128)(2,1)}, bf16[4,2,96,256]{3,2,1,0:T(8,128)(2,1)}, u32[]{:S(2)}, u32[]{:S(2)}) collective-permute-start(bf16[4,2,96,256]{3,2,1,0:T(8,128)(2,1)} %collective-permute-done.3.refs_3_), channel_id=1, source_target_pairs={{0,16},{16,0},{1,17},{17,1},{2,18},{18,2},{3,19},{19,3},{4,20},{20... | collective-permute-start | bytes 1179656 | tf_op jit(solution)/shard_map/ppermute | solution.py:542
  85.6 27.9 %all-to-all-start.3 = ((bf16[8,4,32,768]{3,2,1,0:T(8,128)(2,1)}), bf16[8,4,32,768]{3,2,1,0:T(8,128)(2,1)S(1)}, u32[]{:S(2)}, u32[]{:S(2)}) async-start(bf16[8,4,32,768]{3,2,1,0:T(8,128)(2,1)} %broadcast_in_dim.32), calls=%async_computation.3 | async-start | bytes 3145728 | tf_op jit(solution)/shard_map/all_to_all | solution.py:534
  111.3 8.5 %collective-permute-start.8 = (bf16[4,4,2,96,256]{4,3,2,1,0:T(8,128)(2,1)}, bf16[4,4,2,96,256]{4,3,2,1,0:T(8,128)(2,1)S(1)}, u32[]{:S(2)}, u32[]{:S(2)}) collective-permute-start(bf16[4,4,2,96,256]{4,3,2,1,0:T(8,128)(2,1)} %get-tuple-element.48), channel_id=1, source_target_pairs={{0,16},{16,0},{1,17},{17,1},{2,18},{18,2},{3,19},{19,3},{4,20},{20... | collective-permute-start | bytes 4718600 | tf_op jit(solution)/shard_map/ppermute | solution.py:542
  114.6 36.9 %all-to-all-start.2 = ((bf16[8,2,256,256]{3,2,1,0:T(8,128)(2,1)}), bf16[8,2,256,256]{3,2,1,0:T(8,128)(2,1)}, u32[]{:S(2)}, u32[]{:S(2)}) async-start(bf16[8,2,256,256]{3,2,1,0:T(8,128)(2,1)} %get-tuple-element.43), calls=%async_computation.2 | async-start | bytes 4194304 | tf_op jit(solution)/shard_map/all_to_all | solution.py:534
  124.1 12.2 %collective-permute-start.10 = (bf16[4,2,96,256]{3,2,1,0:T(8,128)(2,1)}, bf16[4,2,96,256]{3,2,1,0:T(8,128)(2,1)S(1)}, u32[]{:S(2)}, u32[]{:S(2)}) collective-permute-start(bf16[4,2,96,256]{3,2,1,0:T(8,128)(2,1)} %get-tuple-element.51), channel_id=1, source_target_pairs={{0,64},{32,96},{64,0},{96,32},{1,65},{33,97},{65,1},{97,33},{2,66}... | collective-permute-start | bytes 1179656 | tf_op jit(solution)/shard_map/ppermute | solution.py:542
  126.3 19.1 %collective-permute-start.11 = (bf16[4,2,96,256]{3,2,1,0:T(8,128)(2,1)}, bf16[4,2,96,256]{3,2,1,0:T(8,128)(2,1)S(1)}, u32[]{:S(2)}, u32[]{:S(2)}) collective-permute-start(bf16[4,2,96,256]{3,2,1,0:T(8,128)(2,1)} %get-tuple-element.52), channel_id=1, source_target_pairs={{0,96},{32,64},{64,32},{96,0},{1,97},{33,65},{65,33},{97,1},{2,98}... | collective-permute-start | bytes 1179656 | tf_op jit(solution)/shard_map/ppermute | solution.py:542
  127.1 18.3 %collective-permute-start.9 = (bf16[4,2,96,256]{3,2,1,0:T(8,128)(2,1)}, bf16[4,2,96,256]{3,2,1,0:T(8,128)(2,1)S(1)}, u32[]{:S(2)}, u32[]{:S(2)}) collective-permute-start(bf16[4,2,96,256]{3,2,1,0:T(8,128)(2,1)} %get-tuple-element.50), channel_id=1, source_target_pairs={{0,32},{32,0},{64,96},{96,64},{1,33},{33,1},{65,97},{97,65},{2,34}... | collective-permute-start | bytes 1179656 | tf_op jit(solution)/shard_map/ppermute | solution.py:542
  151.5 38.6 %all-to-all-start.4 = ((bf16[8,4,32,896]{3,2,1,0:T(8,128)(2,1)}), bf16[8,4,32,896]{3,2,1,0:T(8,128)(2,1)S(1)}, u32[]{:S(2)}, u32[]{:S(2)}) async-start(bf16[8,4,32,896]{3,2,1,0:T(8,128)(2,1)} %get-tuple-element.56), calls=%async_computation.4 | async-start | bytes 3670016 | tf_op jit(solution)/shard_map/all_to_all | solution.py:534
  164.5 15.7 %collective-permute-start.16 = (bf16[4,64,768]{2,1,0:T(8,128)(2,1)S(1)}, bf16[4,64,768]{2,1,0:T(8,128)(2,1)S(1)}, u32[]{:S(2)}, u32[]{:S(2)}) collective-permute-start(bf16[4,64,768]{2,1,0:T(8,128)(2,1)S(1)} %slice.29), channel_id=1, source_target_pairs={{0,16},{16,0},{1,17},{17,1},{2,18},{18,2},{3,19},{19,3},{4,20},{20... | collective-permute-start | bytes 1179656 | tf_op jit(solution)/shard_map/ppermute | solution.py:542
  176.4 7.2 %collective-permute-start.12 = (f32[22,128]{1,0:T(8,128)S(1)}, f32[22,128]{1,0:T(8,128)S(1)}, u32[]{:S(2)}, u32[]{:S(2)}) collective-permute-start(f32[22,128]{1,0:T(8,128)S(1)} %pad_maximum_fusion.2), channel_id=1, source_target_pairs={{0,32},{32,0},{64,96},{96,64},{1,33},{33,1},{65,97},{97,65},{2,34}... | collective-permute-start | bytes 33800 | tf_op jit(solution)/shard_map/ppermute | solution.py:542
  177.0 7.4 %collective-permute-start.13 = (f32[22,128]{1,0:T(8,128)S(1)}, f32[22,128]{1,0:T(8,128)S(1)}, u32[]{:S(2)}, u32[]{:S(2)}) collective-permute-start(f32[22,128]{1,0:T(8,128)S(1)} %pad_maximum_fusion.2), channel_id=1, source_target_pairs={{0,64},{32,96},{64,0},{96,32},{1,65},{33,97},{65,1},{97,33},{2,66}... | collective-permute-start | bytes 33800 | tf_op jit(solution)/shard_map/ppermute | solution.py:542
  180.5 7.0 %collective-permute-start.18 = (bf16[64,768]{1,0:T(8,128)(2,1)S(1)}, bf16[64,768]{1,0:T(8,128)(2,1)S(1)}, u32[]{:S(2)}, u32[]{:S(2)}) collective-permute-start(bf16[64,768]{1,0:T(8,128)(2,1)S(1)} %get-tuple-element.69), channel_id=1, source_target_pairs={{0,64},{32,96},{64,0},{96,32},{1,65},{33,97},{65,1},{97,33},{2,66}... | collective-permute-start | bytes 294920 | tf_op jit(solution)/shard_map/ppermute | solution.py:542
  190.1 8.7 %collective-permute-start.20 = (bf16[64,768]{1,0:T(8,128)(2,1)S(1)}, bf16[64,768]{1,0:T(8,128)(2,1)S(1)}, u32[]{:S(2)}, u32[]{:S(2)}) collective-permute-start(bf16[64,768]{1,0:T(8,128)(2,1)S(1)} %fusion.2), channel_id=1, source_target_pairs={{0,1},{1,0},{2,3},{3,2},{4,5},{5,4},{6,7},{7,6},{8,9},{9,8},{10,11... | collective-permute-start | bytes 294920 | tf_op jit(solution)/shard_map/ppermute | solution.py:542
  191.3 14.8 %all-to-all-start.5 = ((f32[16,22,128]{2,1,0:T(8,128)}), f32[16,22,128]{2,1,0:T(8,128)S(1)}, u32[]{:S(2)}, u32[]{:S(2)}) async-start(f32[16,22,128]{2,1,0:T(8,128)} %broadcast_in_dim.33), calls=%async_computation.5 | async-start | bytes 393216 | tf_op jit(solution)/shard_map/all_to_all | solution.py:534
  198.8 7.3 %collective-permute-start.21 = (bf16[64,768]{1,0:T(8,128)(2,1)S(1)}, bf16[64,768]{1,0:T(8,128)(2,1)S(1)}, u32[]{:S(2)}, u32[]{:S(2)}) collective-permute-start(bf16[64,768]{1,0:T(8,128)(2,1)S(1)} %add_convert_fusion.1), channel_id=1, source_target_pairs={{0,32},{32,0},{64,96},{96,64},{1,33},{33,1},{65,97},{97,65},{2,34}... | collective-permute-start | bytes 294920 | tf_op jit(solution)/shard_map/ppermute | solution.py:542
  198.9 7.3 %collective-permute-start.22 = (bf16[64,768]{1,0:T(8,128)(2,1)S(1)}, bf16[64,768]{1,0:T(8,128)(2,1)S(1)}, u32[]{:S(2)}, u32[]{:S(2)}) collective-permute-start(bf16[64,768]{1,0:T(8,128)(2,1)S(1)} %add_convert_fusion.1), channel_id=1, source_target_pairs={{0,64},{32,96},{64,0},{96,32},{1,65},{33,97},{65,1},{97,33},{2,66}... | collective-permute-start | bytes 294920 | tf_op jit(solution)/shard_map/ppermute | solution.py:542
  (30 other events, 202.4 us)

commit v3 on v2

--- a/solution.py
+++ b/solution.py
@@ -31,8 +31,10 @@
 BIAS_ROWS = TOP_AT + 16
 
 
-def bias_kernel(w_ref, pair_ref, out_ref, acc_ref):
+def bias_kernel(w_ref, pair_ref, cot_ref, out_ref, cot_out_ref, acc_ref):
     heads, rows, keys = acc_ref.shape
+    for c in range(cot_out_ref.shape[0]):
+        cot_out_ref[c] = cot_ref[...]
     for block in range(rows // 16):
         piece = jnp.concatenate([pair_ref[block * 16 + k] for k in range(16)], axis=1)
         res = mm(w_ref[...], piece, NT)
@@ -52,7 +54,7 @@
         out_ref[group, TOP_AT:, :] = tops.astype(BF)
 
 
-def pair_bias(pair, w_pair):
+def pair_bias(pair, w_pair, cot):
     rows, keys, chans = pair.shape
     heads = w_pair.shape[1]
     eye = jnp.eye(16, dtype=BF)
@@ -64,14 +66,21 @@
         in_specs=[
             pl.BlockSpec(spread.shape, lambda i: (0, 0)),
             pl.BlockSpec((step, keys, chans), lambda i: (i, 0, 0)),
-        ],
-        out_specs=pl.BlockSpec((heads // 2, BIAS_ROWS, step), lambda i: (0, 0, i)),
-        out_shape=jax.ShapeDtypeStruct((heads // 2, BIAS_ROWS, rows), BF),
+            pl.BlockSpec(cot.shape, lambda i: (0, 0, 0)),
+        ],
+        out_specs=[
+            pl.BlockSpec((heads // 2, BIAS_ROWS, step), lambda i: (0, 0, i)),
+            pl.BlockSpec((heads * step // 2 // rows,) + cot.shape, lambda i: (i, 0, 0, 0)),
+        ],
+        out_shape=[
+            jax.ShapeDtypeStruct((heads // 2, BIAS_ROWS, rows), BF),
+            jax.ShapeDtypeStruct((heads // 2,) + cot.shape, BF),
+        ],
         scratch_shapes=[pltpu.VMEM((heads, step, keys), F32)],
         compiler_params=pltpu.CompilerParams(vmem_limit_bytes=VMEM),
         cost_estimate=pl.CostEstimate(flops=2**34, bytes_accessed=2**25, transcendentals=0),
         name="pair_bias",
-    )(spread, pair)
+    )(spread, pair, cot)
 
 
 def prepare_kernel(core_ref, act_ref, gain_ref, w_ref, out_ref):
@@ -79,7 +88,8 @@
     act = act_ref[...].reshape(samples * local, width).astype(F32)
     centred = act - jnp.mean(act, axis=-1, keepdims=True)
     inv_std = lax.rsqrt(jnp.mean(centred * centred, axis=-1, keepdims=True) + EPSILON)
-    norm = (centred * inv_std * gain_ref[...]).astype(BF)
+    gain = gain_ref[...].reshape(1, width)
+    norm = (centred * inv_std * gain).astype(BF)
     half = w_ref[pl.ds(pl.multiple_of(core_ref[0] * HD, 16), HD), :]
     for c in range(out_ref.shape[0]):
         out_ref[c, : samples * local, :] = norm
@@ -566,16 +576,16 @@
     which = jnp.full((1,), core, jnp.int32)
     place = jnp.full((1,), core * 4 + y, jnp.int32)
 
-    load = prepare(which, token_act, norm_gain[None, :], w_out, cols)
+    load = prepare(which, token_act, norm_gain, w_out, cols)
     rows_in = exchange(load, COL)
-    bias = pair_bias(pair_rep, w_pair)
+    bias, cot_load = pair_bias(pair_rep, w_pair, grad_out)
     rows_in, bias = lax.optimization_barrier((rows_in, bias))
     w_near = rows_in[:, count:]
     w_far = swap(w_near, "core", 2, 1)
     bias = gated_grad(which, grad_out.reshape(count, width), w_near, w_far, bias)
     bias = exchange(bias, COL)
 
-    grad_rows = gather(grad_out, COL, cols)
+    grad_rows = exchange(cot_load, COL)
 
     wq, wk, wv, wg = w_query.T, w_key.T, w_value.T, w_gate.T
     q, kv_own, gate = project(rows_in, samples, local, wq, wk, wv, wg)

time: 215 us -> 214 us (level)
  transfers between devices with their start and end apart: 31 -> 31, of which waited for: 14 -> 14; matrix products, arithmetic and copies ran while one was open for 4% -> 3% of each run, Pallas kernels for 30% -> 30%
where the time goes in v3:
time: 214 us; the launch traced here: 213 us
  Pallas kernels  70.8 us (33%)
  starting transfers between devices  68.7 us (32%)
  waiting for transfers between devices  58.6 us (27%)
  local copies, waits for them, and re-layouts  11.4 us (5%)
    ppermute x25, waiting for transfers between devices, swap(): return lax.ppermute(x, axis, [(i, i ^ k) for i in range(count)])  39.4 us
    all_to_all x6, starting transfers between devices, exchange(): return lax.all_to_all(x, axes, 0, 0, tiled=True)  36.4 us
    ppermute x25, starting transfers between devices, swap(): return lax.ppermute(x, axis, [(i, i ^ k) for i in range(count)])  32.4 us
    pallas_call x1, Pallas kernels, attend(): pl.pallas_call(attend_kernel, grid=(heads,), in_specs=[pl.BlockSpec(memor...  20.5 us
    all_to_all x6, waiting for transfers between devices, exchange(): return lax.all_to_all(x, axes, 0, 0, tiled=True)  19.2 us
    pallas_call x1, Pallas kernels, pair_bias(): pl.pallas_call(bias_kernel, grid=(rows // step,), in_specs=[pl.BlockSpec(...  10.8 us
    pallas_call x1, Pallas kernels, wpair_part(): pl.pallas_call(wpair_kernel, grid=(rows // step,), in_specs=[pl.BlockSpec...  10 us
    unnamed x47, local copies, waits for them, and re-layouts  7.63 us
  transfers between devices with their start and end apart: 31, of which 14 were waited for; matrix products, arithmetic and copies ran while one was open for 3% of the time, Pallas kernels for 30%

profile of v3, /device:TPU:1, one launch (start us, length us, event | category | flops | bytes accessed | tf_op | source)
XLA Modules:
  0.0 212.5 jit_solution(16864943407475119325)
XLA Ops:
  0.6 2.7 %prepare.1 = bf16[8,176,768]{2,1,0:T(8,128)(2,1)} custom-call(s32[1]{0:T(128)} %bitcast.core_ref, bf16[4,32,768]{2,1,0:T(8,128)(2,1)} %act_ref.3, f32[768]{0:T(1024)} %gain_ref.1, bf16[96,768]{1,0:T(8,128)(2,1)} %w_ref.1), custom_call_target="tpu_custom_call" | custom-call | tf_op jit(solution)/shard_map/prepare/pallas_call | solution.py:102
  3.3 8.5 %all-to-all-start = ((bf16[8,176,768]{2,1,0:T(8,128)(2,1)}), bf16[8,176,768]{2,1,0:T(8,128)(2,1)S(1)}, u32[]{:S(2)}, u32[]{:S(2)}) async-start(bf16[8,176,768]{2,1,0:T(8,128)(2,1)} %prepare.1), calls=%async_computation | async-start | bytes 4325376 | tf_op jit(solution)/shard_map/all_to_all | solution.py:544
  13.2 10.8 %pair_bias.1 = (bf16[8,592,256]{2,1,0:T(8,128)(2,1)}, bf16[8,4,32,768]{3,2,1,0:T(8,128)(2,1)}) custom-call(bf16[256,2048]{1,0:T(8,128)(2,1)} %bitcast.39, bf16[256,256,128]{2,1,0:T(8,128)(2,1)} %pair_ref.3, bf16[4,32,768]{2,1,0:T(8,128)(2,1)} %cot_ref.3), custom_call_target="tpu_custom_call" | custom-call | flops 17179869184 | bytes 33554432 | tf_op jit(solution)/shard_map/pair_bias/pallas_call | solution.py:63
  24.0 16.0 %all-to-all-done.rows_ref = bf16[8,176,768]{2,1,0:T(8,128)(2,1)S(1)} async-done(((bf16[8,176,768]{2,1,0:T(8,128)(2,1)}), bf16[8,176,768]{2,1,0:T(8,128)(2,1)S(1)}, u32[]{:S(2)}, u32[]{:S(2)}) %all-to-all-start) | async-done | bytes 2162720 | tf_op jit(solution)/shard_map/all_to_all | solution.py:544
  44.5 2.6 %gated_grad.1 = bf16[8,592,256]{2,1,0:T(8,128)(2,1)} custom-call(s32[1]{0:T(128)} %bitcast.core_ref, bf16[128,768]{1,0:T(8,128)(2,1)} %bitcast.40, bf16[8,48,768]{2,1,0:T(8,128)(2,1)} %copy-done.3, bf16[8,48,768]{2,1,0:T(8,128)(2,1)} %copy-done.5, bf16[8,592,256]{2,1,0:T(8,128)(2,1)} %get-tuple-element.42._), custom_call_target="tpu_custom_call", output_to_operand_aliasing={{}: (4, {})} | custom-call | tf_op jit(solution)/shard_map/gated_grad/pallas_call | solution.py:160
  47.1 3.6 %all-to-all-start.1 = ((bf16[8,592,256]{2,1,0:T(8,128)(2,1)}), bf16[8,592,256]{2,1,0:T(8,128)(2,1)S(1)}, u32[]{:S(2)}, u32[]{:S(2)}) async-start(bf16[8,592,256]{2,1,0:T(8,128)(2,1)} %gated_grad.1), calls=%async_computation.1 | async-start | bytes 4849664 | tf_op jit(solution)/shard_map/all_to_all | solution.py:544
  50.7 4.8 %project.1 = (bf16[4,96,256]{2,1,0:T(8,128)(2,1)}, bf16[4,2,96,256]{3,2,1,0:T(8,128)(2,1)}, bf16[4,96,256]{2,1,0:T(8,128)(2,1)}) custom-call(bf16[8,176,768]{2,1,0:T(8,128)(2,1)} %copy-done, bf16[96,768]{1,0:T(8,128)(2,1)} %bitcast.41, bf16[96,768]{1,0:T(8,128)(2,1)} %bitcast.43, bf16[96,768]{1,0:T(8,128)(2,1)} %bitcast.45, bf16[96,768]{1,0:T(8,128)(2,1)} %bitcast.47), custom_call_target="tpu_custom_call" | custom-call | tf_op jit(solution)/shard_map/project/pallas_call | solution.py:129
  56.9 2.6 %collective-permute-start.2 = (bf16[4,2,96,256]{3,2,1,0:T(8,128)(2,1)}, bf16[4,2,96,256]{3,2,1,0:T(8,128)(2,1)S(1)}, u32[]{:S(2)}, u32[]{:S(2)}) collective-permute-start(bf16[4,2,96,256]{3,2,1,0:T(8,128)(2,1)} %get-tuple-element.45.refs_0_), channel_id=1, source_target_pairs={{0,64},{32,96},{64,0},{96,32},{1,65},{33,97},{65,1},{97,33},{2,66}... | collective-permute-start | bytes 1179656 | tf_op jit(solution)/shard_map/ppermute | solution.py:552
  60.6 5.6 %collective-permute-done.1.refs_1_ = bf16[4,2,96,256]{3,2,1,0:T(8,128)(2,1)S(1)} collective-permute-done((bf16[4,2,96,256]{3,2,1,0:T(8,128)(2,1)}, bf16[4,2,96,256]{3,2,1,0:T(8,128)(2,1)S(1)}, u32[]{:S(2)}, u32[]{:S(2)}) %collective-permute-start.1) | collective-permute-done | bytes 393248 | tf_op jit(solution)/shard_map/ppermute | solution.py:552
  68.1 8.9 %collective-permute-done.2.refs_2_ = bf16[4,2,96,256]{3,2,1,0:T(8,128)(2,1)S(1)} collective-permute-done((bf16[4,2,96,256]{3,2,1,0:T(8,128)(2,1)}, bf16[4,2,96,256]{3,2,1,0:T(8,128)(2,1)S(1)}, u32[]{:S(2)}, u32[]{:S(2)}) %collective-permute-start.2) | collective-permute-done | bytes 393248 | tf_op jit(solution)/shard_map/ppermute | solution.py:552
  83.8 5.2 %all-to-all-start.3 = ((bf16[8,4,32,768]{3,2,1,0:T(8,128)(2,1)}), bf16[8,4,32,768]{3,2,1,0:T(8,128)(2,1)S(1)}, u32[]{:S(2)}, u32[]{:S(2)}) async-start(bf16[8,4,32,768]{3,2,1,0:T(8,128)(2,1)} %get-tuple-element.52), calls=%async_computation.3 | async-start | bytes 3145728 | tf_op jit(solution)/shard_map/all_to_all | solution.py:544
  89.0 20.5 %attend.1 = (bf16[4,96,256]{2,1,0:T(8,128)(2,1)}, bf16[4,96,256]{2,1,0:T(8,128)(2,1)}, bf16[4,96,256]{2,1,0:T(8,128)(2,1)}, bf16[4,4,2,96,256]{4,3,2,1,0:T(8,128...) custom-call(s32[1]{0:T(128)} %bitcast.1.me_ref, bf16[8,592,256]{2,1,0:T(8,128)(2,1)} %copy-done.4, ...), custom_call_target="tpu_custom_call" | custom-call | flops 17179869184 | bytes 20971520 | tf_op jit(solution)/shard_map/attend/pallas_call | solution.py:268
  112.8 5.1 %all-to-all-start.2 = ((bf16[8,2,256,256]{3,2,1,0:T(8,128)(2,1)}), bf16[8,2,256,256]{3,2,1,0:T(8,128)(2,1)}, u32[]{:S(2)}, u32[]{:S(2)}) async-start(bf16[8,2,256,256]{3,2,1,0:T(8,128)(2,1)} %get-tuple-element.46), calls=%async_computation.2 | async-start | bytes 4194304 | tf_op jit(solution)/shard_map/all_to_all | solution.py:544
  119.2 3.2 %fold.1 = (bf16[4,2,96,256]{3,2,1,0:T(8,128)(2,1)}, bf16[4,2,96,256]{3,2,1,0:T(8,128)(2,1)}, bf16[4,2,96,256]{3,2,1,0:T(8,128)(2,1)}, bf16[4,2,96,256]{3,2,1,0:T(8,128)(2,1)}) custom-call(bf16[4,4,2,96,256]{4,3,2,1,0:T(8,128)(2,1)} %get-tuple-element.50.own_ref, bf16[4,4,2,96,256]{4,3,2,1,0:T(8,128)(2,1)} %copy-done.7, bf16[8,4,32,768]{3,2,1,0:T(8,128)(2,1)} %copy-done.1), custom_call_target="tpu_custom_call" | custom-call | tf_op jit(solution)/shard_map/fold/pallas_call | solution.py:303
  126.2 8.3 %collective-permute-done.10.refs_2_ = bf16[4,2,96,256]{3,2,1,0:T(8,128)(2,1)S(1)} collective-permute-done((bf16[4,2,96,256]{3,2,1,0:T(8,128)(2,1)}, bf16[4,2,96,256]{3,2,1,0:T(8,128)(2,1)S(1)}, u32[]{:S(2)}, u32[]{:S(2)}) %collective-permute-start.10) | collective-permute-done | bytes 393248 | tf_op jit(solution)/shard_map/ppermute | solution.py:552
  134.5 9.1 %collective-permute-done.11.refs_3_ = bf16[4,2,96,256]{3,2,1,0:T(8,128)(2,1)S(1)} collective-permute-done((bf16[4,2,96,256]{3,2,1,0:T(8,128)(2,1)}, bf16[4,2,96,256]{3,2,1,0:T(8,128)(2,1)S(1)}, u32[]{:S(2)}, u32[]{:S(2)}) %collective-permute-start.11) | collective-permute-done | bytes 393248 | tf_op jit(solution)/shard_map/ppermute | solution.py:552
  144.6 5.2 %norm_part.1 = (bf16[8,4,32,896]{3,2,1,0:T(8,128)(2,1)}, bf16[4,384,256]{2,1,0:T(8,128)(2,1)}) custom-call(bf16[4,96,256]{2,1,0:T(8,128)(2,1)} %get-tuple-element.47.gated_ref, bf16[4,96,256]{2,1,0:T(8,128)(2,1)} %get-tuple-element.48.dq_ref, bf16[4,96,256]{2,1,0:T(8,128)(2,1)} %get-tuple-element.49.dg_ref, ...), custom_call_target="tpu_custom_call" | custom-call | tf_op jit(solution)/shard_map/norm_part/pallas_call | solution.py:345
  149.8 6.6 %all-to-all-start.4 = ((bf16[8,4,32,896]{3,2,1,0:T(8,128)(2,1)}), bf16[8,4,32,896]{3,2,1,0:T(8,128)(2,1)S(1)}, u32[]{:S(2)}, u32[]{:S(2)}) async-start(bf16[8,4,32,896]{3,2,1,0:T(8,128)(2,1)} %get-tuple-element.60), calls=%async_computation.4 | async-start | bytes 3670016 | tf_op jit(solution)/shard_map/all_to_all | solution.py:544
  156.9 5.4 %weight_part.1 = (bf16[8,64,768]{2,1,0:T(8,128)(2,1)}, f32[1,768]{1,0:T(1,128)}) custom-call(s32[1]{0:T(128)} %bitcast.8.place_ref, bf16[4,384,256]{2,1,0:T(8,128)(2,1)} %get-tuple-element.57.dcat_ref, bf16[4,96,256]{2,1,0:T(8,128)(2,1)} %get-tuple-element.47.gated_ref, bf16[8,176,768]{2,1,0:T(8,128)(2,1)} %copy-done, bf16[8,4,32,768]{3,2,1,0:T(8,128)(2,1)} %copy-done.1, ...), custom_call_target="tpu_custom_call" | custom-call | tf_op jit(solution)/shard_map/weight_part/pallas_call | solution.py:400
  164.5 10.0 %wpair_part.1 = f32[16,128]{1,0:T(8,128)} custom-call(bf16[8,2,256,256]{3,2,1,0:T(8,128)(2,1)} %all-to-all-done.2.db_ref, bf16[256,256,128]{2,1,0:T(8,128)(2,1)} %pair_ref.3), custom_call_target="tpu_custom_call" | custom-call | flops 4294967296 | bytes 20971520 | tf_op jit(solution)/shard_map/wpair_part/pallas_call | solution.py:524
  175.9 2.6 %collective-permute-start.13 = (f32[22,128]{1,0:T(8,128)S(1)}, f32[22,128]{1,0:T(8,128)S(1)}, u32[]{:S(2)}, u32[]{:S(2)}) collective-permute-start(f32[22,128]{1,0:T(8,128)S(1)} %pad_maximum_fusion.2), channel_id=1, source_target_pairs={{0,64},{32,96},{64,0},{96,32},{1,65},{33,97},{65,1},{97,33},{2,66}... | collective-permute-start | bytes 33800 | tf_op jit(solution)/shard_map/ppermute | solution.py:552
  179.3 3.2 %collective-permute-start.18 = (bf16[64,768]{1,0:T(8,128)(2,1)S(1)}, bf16[64,768]{1,0:T(8,128)(2,1)S(1)}, u32[]{:S(2)}, u32[]{:S(2)}) collective-permute-start(bf16[64,768]{1,0:T(8,128)(2,1)S(1)} %get-tuple-element.73), channel_id=1, source_target_pairs={{0,64},{32,96},{64,0},{96,32},{1,65},{33,97},{65,1},{97,33},{2,66}... | collective-permute-start | bytes 294920 | tf_op jit(solution)/shard_map/ppermute | solution.py:552
  190.2 7.5 %all-to-all-start.5 = ((f32[16,22,128]{2,1,0:T(8,128)}), f32[16,22,128]{2,1,0:T(8,128)S(1)}, u32[]{:S(2)}, u32[]{:S(2)}) async-start(f32[16,22,128]{2,1,0:T(8,128)} %broadcast_in_dim.25), calls=%async_computation.5 | async-start | bytes 393216 | tf_op jit(solution)/shard_map/all_to_all | solution.py:544
  201.7 3.4 %finish.1 = (bf16[4,32,768]{2,1,0:T(8,128)(2,1)}, bf16[4,32,768]{2,1,0:T(8,128)(2,1)}) custom-call(s32[1]{0:T(128)} %bitcast.core_ref, bf16[8,4,32,896]{3,2,1,0:T(8,128)(2,1)} %copy-done.2, bf16[8,48,768]{2,1,0:T(8,128)(2,1)} %copy-done.3, bf16[8,48,768]{2,1,0:T(8,128)(2,1)} %copy-done.5, bf16[4,32,768]{2,1,0:T(8,128)(2,1)} %act_ref.3, ...), custom_call_target="tpu_custom_call" | custom-call | tf_op jit(solution)/shard_map/finish/pallas_call | solution.py:450
  (115 shorter events, 50.4 us)
Async XLA Ops:
  3.3 36.7 %all-to-all-start = ((bf16[8,176,768]{2,1,0:T(8,128)(2,1)}), bf16[8,176,768]{2,1,0:T(8,128)(2,1)S(1)}, u32[]{:S(2)}, u32[]{:S(2)}) async-start(bf16[8,176,768]{2,1,0:T(8,128)(2,1)} %prepare.1), calls=%async_computation | async-start | bytes 4325376 | tf_op jit(solution)/shard_map/all_to_all | solution.py:544
  47.1 35.3 %all-to-all-start.1 = ((bf16[8,592,256]{2,1,0:T(8,128)(2,1)}), bf16[8,592,256]{2,1,0:T(8,128)(2,1)S(1)}, u32[]{:S(2)}, u32[]{:S(2)}) async-start(bf16[8,592,256]{2,1,0:T(8,128)(2,1)} %gated_grad.1), calls=%async_computation.1 | async-start | bytes 4849664 | tf_op jit(solution)/shard_map/all_to_all | solution.py:544
  55.6 10.6 %collective-permute-start.1 = (bf16[4,2,96,256]{3,2,1,0:T(8,128)(2,1)}, bf16[4,2,96,256]{3,2,1,0:T(8,128)(2,1)S(1)}, u32[]{:S(2)}, u32[]{:S(2)}) collective-permute-start(bf16[4,2,96,256]{3,2,1,0:T(8,128)(2,1)} %get-tuple-element.45.refs_0_), channel_id=1, source_target_pairs={{0,32},{32,0},{64,96},{96,64},{1,33},{33,1},{65,97},{97,65},{2,34}... | collective-permute-start | bytes 1179656 | tf_op jit(solution)/shard_map/ppermute | solution.py:552
  56.9 20.2 %collective-permute-start.2 = (bf16[4,2,96,256]{3,2,1,0:T(8,128)(2,1)}, bf16[4,2,96,256]{3,2,1,0:T(8,128)(2,1)S(1)}, u32[]{:S(2)}, u32[]{:S(2)}) collective-permute-start(bf16[4,2,96,256]{3,2,1,0:T(8,128)(2,1)} %get-tuple-element.45.refs_0_), channel_id=1, source_target_pairs={{0,64},{32,96},{64,0},{96,32},{1,65},{33,97},{65,1},{97,33},{2,66}... | collective-permute-start | bytes 1179656 | tf_op jit(solution)/shard_map/ppermute | solution.py:552
  59.5 19.6 %collective-permute-start.3 = (bf16[4,2,96,256]{3,2,1,0:T(8,128)(2,1)}, bf16[4,2,96,256]{3,2,1,0:T(8,128)(2,1)}, u32[]{:S(2)}, u32[]{:S(2)}) collective-permute-start(bf16[4,2,96,256]{3,2,1,0:T(8,128)(2,1)} %get-tuple-element.45.refs_0_), channel_id=1, source_target_pairs={{0,96},{32,64},{64,32},{96,0},{1,97},{33,65},{65,33},{97,1},{2,98}... | collective-permute-start | bytes 1179656 | tf_op jit(solution)/shard_map/ppermute | solution.py:552
  59.5 29.5 %collective-permute-start.4 = (bf16[4,2,96,256]{3,2,1,0:T(8,128)(2,1)}, bf16[4,2,96,256]{3,2,1,0:T(8,128)(2,1)}, u32[]{:S(2)}, u32[]{:S(2)}) collective-permute-start(bf16[4,2,96,256]{3,2,1,0:T(8,128)(2,1)} %get-tuple-element.45.refs_0_), channel_id=1, source_target_pairs={{0,16},{16,0},{1,17},{17,1},{2,18},{18,2},{3,19},{19,3},{4,20},{20... | collective-permute-start | bytes 1179656 | tf_op jit(solution)/shard_map/ppermute | solution.py:552
  66.2 22.8 %collective-permute-start.5 = (bf16[4,2,96,256]{3,2,1,0:T(8,128)(2,1)S(1)}, bf16[4,2,96,256]{3,2,1,0:T(8,128)(2,1)}, u32[]{:S(2)}, u32[]{:S(2)}) collective-permute-start(bf16[4,2,96,256]{3,2,1,0:T(8,128)(2,1)S(1)} %collective-permute-done.1.refs_1_), channel_id=1, source_target_pairs={{0,16},{16,0},{1,17},{17,1},{2,18},{18,2},{3,19},{19,3},{4,20},{20... | collective-permute-start | bytes 1179656 | tf_op jit(solution)/shard_map/ppermute | solution.py:552
  77.0 12.0 %collective-permute-start.6 = (bf16[4,2,96,256]{3,2,1,0:T(8,128)(2,1)S(1)}, bf16[4,2,96,256]{3,2,1,0:T(8,128)(2,1)}, u32[]{:S(2)}, u32[]{:S(2)}) collective-permute-start(bf16[4,2,96,256]{3,2,1,0:T(8,128)(2,1)S(1)} %collective-permute-done.2.refs_2_), channel_id=1, source_target_pairs={{0,16},{16,0},{1,17},{17,1},{2,18},{18,2},{3,19},{19,3},{4,20},{20... | collective-permute-start | bytes 1179656 | tf_op jit(solution)/shard_map/ppermute | solution.py:552
  79.1 9.9 %collective-permute-start.7 = (bf16[4,2,96,256]{3,2,1,0:T(8,128)(2,1)}, bf16[4,2,96,256]{3,2,1,0:T(8,128)(2,1)}, u32[]{:S(2)}, u32[]{:S(2)}) collective-permute-start(bf16[4,2,96,256]{3,2,1,0:T(8,128)(2,1)} %collective-permute-done.3.refs_3_), channel_id=1, source_target_pairs={{0,16},{16,0},{1,17},{17,1},{2,18},{18,2},{3,19},{19,3},{4,20},{20... | collective-permute-start | bytes 1179656 | tf_op jit(solution)/shard_map/ppermute | solution.py:552
  83.8 27.8 %all-to-all-start.3 = ((bf16[8,4,32,768]{3,2,1,0:T(8,128)(2,1)}), bf16[8,4,32,768]{3,2,1,0:T(8,128)(2,1)S(1)}, u32[]{:S(2)}, u32[]{:S(2)}) async-start(bf16[8,4,32,768]{3,2,1,0:T(8,128)(2,1)} %get-tuple-element.52), calls=%async_computation.3 | async-start | bytes 3145728 | tf_op jit(solution)/shard_map/all_to_all | solution.py:544
  109.5 8.5 %collective-permute-start.8 = (bf16[4,4,2,96,256]{4,3,2,1,0:T(8,128)(2,1)}, bf16[4,4,2,96,256]{4,3,2,1,0:T(8,128)(2,1)S(1)}, u32[]{:S(2)}, u32[]{:S(2)}) collective-permute-start(bf16[4,4,2,96,256]{4,3,2,1,0:T(8,128)(2,1)} %get-tuple-element.51), channel_id=1, source_target_pairs={{0,16},{16,0},{1,17},{17,1},{2,18},{18,2},{3,19},{19,3},{4,20},{20... | collective-permute-start | bytes 4718600 | tf_op jit(solution)/shard_map/ppermute | solution.py:552
  112.8 37.0 %all-to-all-start.2 = ((bf16[8,2,256,256]{3,2,1,0:T(8,128)(2,1)}), bf16[8,2,256,256]{3,2,1,0:T(8,128)(2,1)}, u32[]{:S(2)}, u32[]{:S(2)}) async-start(bf16[8,2,256,256]{3,2,1,0:T(8,128)(2,1)} %get-tuple-element.46), calls=%async_computation.2 | async-start | bytes 4194304 | tf_op jit(solution)/shard_map/all_to_all | solution.py:544
  122.4 12.2 %collective-permute-start.10 = (bf16[4,2,96,256]{3,2,1,0:T(8,128)(2,1)}, bf16[4,2,96,256]{3,2,1,0:T(8,128)(2,1)S(1)}, u32[]{:S(2)}, u32[]{:S(2)}) collective-permute-start(bf16[4,2,96,256]{3,2,1,0:T(8,128)(2,1)} %get-tuple-element.55), channel_id=1, source_target_pairs={{0,64},{32,96},{64,0},{96,32},{1,65},{33,97},{65,1},{97,33},{2,66}... | collective-permute-start | bytes 1179656 | tf_op jit(solution)/shard_map/ppermute | solution.py:552
  124.6 19.1 %collective-permute-start.11 = (bf16[4,2,96,256]{3,2,1,0:T(8,128)(2,1)}, bf16[4,2,96,256]{3,2,1,0:T(8,128)(2,1)S(1)}, u32[]{:S(2)}, u32[]{:S(2)}) collective-permute-start(bf16[4,2,96,256]{3,2,1,0:T(8,128)(2,1)} %get-tuple-element.56), channel_id=1, source_target_pairs={{0,96},{32,64},{64,32},{96,0},{1,97},{33,65},{65,33},{97,1},{2,98}... | collective-permute-start | bytes 1179656 | tf_op jit(solution)/shard_map/ppermute | solution.py:552
  125.4 18.3 %collective-permute-start.9 = (bf16[4,2,96,256]{3,2,1,0:T(8,128)(2,1)}, bf16[4,2,96,256]{3,2,1,0:T(8,128)(2,1)S(1)}, u32[]{:S(2)}, u32[]{:S(2)}) collective-permute-start(bf16[4,2,96,256]{3,2,1,0:T(8,128)(2,1)} %get-tuple-element.54), channel_id=1, source_target_pairs={{0,32},{32,0},{64,96},{96,64},{1,33},{33,1},{65,97},{97,65},{2,34}... | collective-permute-start | bytes 1179656 | tf_op jit(solution)/shard_map/ppermute | solution.py:552
  149.8 39.2 %all-to-all-start.4 = ((bf16[8,4,32,896]{3,2,1,0:T(8,128)(2,1)}), bf16[8,4,32,896]{3,2,1,0:T(8,128)(2,1)S(1)}, u32[]{:S(2)}, u32[]{:S(2)}) async-start(bf16[8,4,32,896]{3,2,1,0:T(8,128)(2,1)} %get-tuple-element.60), calls=%async_computation.4 | async-start | bytes 3670016 | tf_op jit(solution)/shard_map/all_to_all | solution.py:544
  163.4 15.7 %collective-permute-start.16 = (bf16[4,64,768]{2,1,0:T(8,128)(2,1)S(1)}, bf16[4,64,768]{2,1,0:T(8,128)(2,1)S(1)}, u32[]{:S(2)}, u32[]{:S(2)}) collective-permute-start(bf16[4,64,768]{2,1,0:T(8,128)(2,1)S(1)} %slice.29), channel_id=1, source_target_pairs={{0,16},{16,0},{1,17},{17,1},{2,18},{18,2},{3,19},{19,3},{4,20},{20... | collective-permute-start | bytes 1179656 | tf_op jit(solution)/shard_map/ppermute | solution.py:552
  175.2 7.3 %collective-permute-start.12 = (f32[22,128]{1,0:T(8,128)S(1)}, f32[22,128]{1,0:T(8,128)S(1)}, u32[]{:S(2)}, u32[]{:S(2)}) collective-permute-start(f32[22,128]{1,0:T(8,128)S(1)} %pad_maximum_fusion.2), channel_id=1, source_target_pairs={{0,32},{32,0},{64,96},{96,64},{1,33},{33,1},{65,97},{97,65},{2,34}... | collective-permute-start | bytes 33800 | tf_op jit(solution)/shard_map/ppermute | solution.py:552
  175.9 7.3 %collective-permute-start.13 = (f32[22,128]{1,0:T(8,128)S(1)}, f32[22,128]{1,0:T(8,128)S(1)}, u32[]{:S(2)}, u32[]{:S(2)}) collective-permute-start(f32[22,128]{1,0:T(8,128)S(1)} %pad_maximum_fusion.2), channel_id=1, source_target_pairs={{0,64},{32,96},{64,0},{96,32},{1,65},{33,97},{65,1},{97,33},{2,66}... | collective-permute-start | bytes 33800 | tf_op jit(solution)/shard_map/ppermute | solution.py:552
  179.3 7.0 %collective-permute-start.18 = (bf16[64,768]{1,0:T(8,128)(2,1)S(1)}, bf16[64,768]{1,0:T(8,128)(2,1)S(1)}, u32[]{:S(2)}, u32[]{:S(2)}) collective-permute-start(bf16[64,768]{1,0:T(8,128)(2,1)S(1)} %get-tuple-element.73), channel_id=1, source_target_pairs={{0,64},{32,96},{64,0},{96,32},{1,65},{33,97},{65,1},{97,33},{2,66}... | collective-permute-start | bytes 294920 | tf_op jit(solution)/shard_map/ppermute | solution.py:552
  189.0 8.7 %collective-permute-start.20 = (bf16[64,768]{1,0:T(8,128)(2,1)S(1)}, bf16[64,768]{1,0:T(8,128)(2,1)S(1)}, u32[]{:S(2)}, u32[]{:S(2)}) collective-permute-start(bf16[64,768]{1,0:T(8,128)(2,1)S(1)} %fusion.2), channel_id=1, source_target_pairs={{0,1},{1,0},{2,3},{3,2},{4,5},{5,4},{6,7},{7,6},{8,9},{9,8},{10,11... | collective-permute-start | bytes 294920 | tf_op jit(solution)/shard_map/ppermute | solution.py:552
  190.2 14.8 %all-to-all-start.5 = ((f32[16,22,128]{2,1,0:T(8,128)}), f32[16,22,128]{2,1,0:T(8,128)S(1)}, u32[]{:S(2)}, u32[]{:S(2)}) async-start(f32[16,22,128]{2,1,0:T(8,128)} %broadcast_in_dim.25), calls=%async_computation.5 | async-start | bytes 393216 | tf_op jit(solution)/shard_map/all_to_all | solution.py:544
  197.8 7.3 %collective-permute-start.21 = (bf16[64,768]{1,0:T(8,128)(2,1)S(1)}, bf16[64,768]{1,0:T(8,128)(2,1)S(1)}, u32[]{:S(2)}, u32[]{:S(2)}) collective-permute-start(bf16[64,768]{1,0:T(8,128)(2,1)S(1)} %add_convert_fusion.1), channel_id=1, source_target_pairs={{0,32},{32,0},{64,96},{96,64},{1,33},{33,1},{65,97},{97,65},{2,34}... | collective-permute-start | bytes 294920 | tf_op jit(solution)/shard_map/ppermute | solution.py:552
  197.8 7.3 %collective-permute-start.22 = (bf16[64,768]{1,0:T(8,128)(2,1)S(1)}, bf16[64,768]{1,0:T(8,128)(2,1)S(1)}, u32[]{:S(2)}, u32[]{:S(2)}) collective-permute-start(bf16[64,768]{1,0:T(8,128)(2,1)S(1)} %add_convert_fusion.1), channel_id=1, source_target_pairs={{0,64},{32,96},{64,0},{96,32},{1,65},{33,97},{65,1},{97,33},{2,66}... | collective-permute-start | bytes 294920 | tf_op jit(solution)/shard_map/ppermute | solution.py:552
  (30 other events, 186.4 us)

commit v4 on v3

--- a/solution.py
+++ b/solution.py
@@ -481,7 +481,7 @@
         ],
         out_shape=[jax.ShapeDtypeStruct((feat, width), F32)] * 5,
         scratch_shapes=[pltpu.VMEM((512, width), F32)],
-        compiler_params=pltpu.CompilerParams(vmem_limit_bytes=VMEM),
+        compiler_params=pltpu.CompilerParams(vmem_limit_bytes=16 * 2**20),
         name="unpack",
     )(place, near, far)
 

time: 214 us -> 212 us (level)
    unnamed x47 -> x43, local copies, waits for them, and re-layouts: 7.63 us -> 6.9 us
where the time goes in v4:
time: 212 us; the launch traced here: 211 us
  Pallas kernels  69.7 us (33%)
  starting transfers between devices  68.9 us (33%)
  waiting for transfers between devices  58.5 us (28%)
  local copies, waits for them, and re-layouts  10.6 us (5%)
    ppermute x25, waiting for transfers between devices, swap(): return lax.ppermute(x, axis, [(i, i ^ k) for i in range(count)])  39.3 us
    all_to_all x6, starting transfers between devices, exchange(): return lax.all_to_all(x, axes, 0, 0, tiled=True)  36.4 us
    ppermute x25, starting transfers between devices, swap(): return lax.ppermute(x, axis, [(i, i ^ k) for i in range(count)])  32.4 us
    pallas_call x1, Pallas kernels, attend(): pl.pallas_call(attend_kernel, grid=(heads,), in_specs=[pl.BlockSpec(memor...  20.5 us
    all_to_all x6, waiting for transfers between devices, exchange(): return lax.all_to_all(x, axes, 0, 0, tiled=True)  19.1 us
    pallas_call x1, Pallas kernels, pair_bias(): pl.pallas_call(bias_kernel, grid=(rows // step,), in_specs=[pl.BlockSpec(...  10.8 us
    pallas_call x1, Pallas kernels, wpair_part(): pl.pallas_call(wpair_kernel, grid=(rows // step,), in_specs=[pl.BlockSpec...  10 us
    unnamed x43, local copies, waits for them, and re-layouts  6.9 us
  transfers between devices with their start and end apart: 31, of which 14 were waited for; matrix products, arithmetic and copies ran while one was open for 3% of the time, Pallas kernels for 30%

profile of v4, /device:TPU:1, one launch (start us, length us, event | category | flops | bytes accessed | tf_op | source)
XLA Modules:
  0.0 210.7 jit_solution(4903864605603047554)
XLA Ops:
  0.6 2.7 %prepare.1 = bf16[8,176,768]{2,1,0:T(8,128)(2,1)} custom-call(s32[1]{0:T(128)} %bitcast.core_ref, bf16[4,32,768]{2,1,0:T(8,128)(2,1)} %act_ref.3, f32[768]{0:T(1024)} %gain_ref.1, bf16[96,768]{1,0:T(8,128)(2,1)} %w_ref.1), custom_call_target="tpu_custom_call" | custom-call | tf_op jit(solution)/shard_map/prepare/pallas_call | solution.py:102
  3.3 8.5 %all-to-all-start = ((bf16[8,176,768]{2,1,0:T(8,128)(2,1)}), bf16[8,176,768]{2,1,0:T(8,128)(2,1)S(1)}, u32[]{:S(2)}, u32[]{:S(2)}) async-start(bf16[8,176,768]{2,1,0:T(8,128)(2,1)} %prepare.1), calls=%async_computation | async-start | bytes 4325376 | tf_op jit(solution)/shard_map/all_to_all | solution.py:544
  13.2 10.8 %pair_bias.1 = (bf16[8,592,256]{2,1,0:T(8,128)(2,1)}, bf16[8,4,32,768]{3,2,1,0:T(8,128)(2,1)}) custom-call(bf16[256,2048]{1,0:T(8,128)(2,1)} %bitcast.39, bf16[256,256,128]{2,1,0:T(8,128)(2,1)} %pair_ref.3, bf16[4,32,768]{2,1,0:T(8,128)(2,1)} %cot_ref.3), custom_call_target="tpu_custom_call" | custom-call | flops 17179869184 | bytes 33554432 | tf_op jit(solution)/shard_map/pair_bias/pallas_call | solution.py:63
  24.0 16.0 %all-to-all-done.rows_ref = bf16[8,176,768]{2,1,0:T(8,128)(2,1)S(1)} async-done(((bf16[8,176,768]{2,1,0:T(8,128)(2,1)}), bf16[8,176,768]{2,1,0:T(8,128)(2,1)S(1)}, u32[]{:S(2)}, u32[]{:S(2)}) %all-to-all-start) | async-done | bytes 2162720 | tf_op jit(solution)/shard_map/all_to_all | solution.py:544
  44.5 2.6 %gated_grad.1 = bf16[8,592,256]{2,1,0:T(8,128)(2,1)} custom-call(s32[1]{0:T(128)} %bitcast.core_ref, bf16[128,768]{1,0:T(8,128)(2,1)} %bitcast.40, bf16[8,48,768]{2,1,0:T(8,128)(2,1)} %copy-done.3, bf16[8,48,768]{2,1,0:T(8,128)(2,1)} %copy-done.5, bf16[8,592,256]{2,1,0:T(8,128)(2,1)} %get-tuple-element.42._), custom_call_target="tpu_custom_call", output_to_operand_aliasing={{}: (4, {})} | custom-call | tf_op jit(solution)/shard_map/gated_grad/pallas_call | solution.py:160
  47.1 3.6 %all-to-all-start.1 = ((bf16[8,592,256]{2,1,0:T(8,128)(2,1)}), bf16[8,592,256]{2,1,0:T(8,128)(2,1)S(1)}, u32[]{:S(2)}, u32[]{:S(2)}) async-start(bf16[8,592,256]{2,1,0:T(8,128)(2,1)} %gated_grad.1), calls=%async_computation.1 | async-start | bytes 4849664 | tf_op jit(solution)/shard_map/all_to_all | solution.py:544
  50.7 4.9 %project.1 = (bf16[4,96,256]{2,1,0:T(8,128)(2,1)}, bf16[4,2,96,256]{3,2,1,0:T(8,128)(2,1)}, bf16[4,96,256]{2,1,0:T(8,128)(2,1)}) custom-call(bf16[8,176,768]{2,1,0:T(8,128)(2,1)} %copy-done, bf16[96,768]{1,0:T(8,128)(2,1)} %bitcast.41, bf16[96,768]{1,0:T(8,128)(2,1)} %bitcast.43, bf16[96,768]{1,0:T(8,128)(2,1)} %bitcast.45, bf16[96,768]{1,0:T(8,128)(2,1)} %bitcast.47), custom_call_target="tpu_custom_call" | custom-call | tf_op jit(solution)/shard_map/project/pallas_call | solution.py:129
  56.9 2.6 %collective-permute-start.2 = (bf16[4,2,96,256]{3,2,1,0:T(8,128)(2,1)}, bf16[4,2,96,256]{3,2,1,0:T(8,128)(2,1)S(1)}, u32[]{:S(2)}, u32[]{:S(2)}) collective-permute-start(bf16[4,2,96,256]{3,2,1,0:T(8,128)(2,1)} %get-tuple-element.45.refs_0_), channel_id=1, source_target_pairs={{0,64},{32,96},{64,0},{96,32},{1,65},{33,97},{65,1},{97,33},{2,66}... | collective-permute-start | bytes 1179656 | tf_op jit(solution)/shard_map/ppermute | solution.py:552
  60.7 5.6 %collective-permute-done.1.refs_1_ = bf16[4,2,96,256]{3,2,1,0:T(8,128)(2,1)S(1)} collective-permute-done((bf16[4,2,96,256]{3,2,1,0:T(8,128)(2,1)}, bf16[4,2,96,256]{3,2,1,0:T(8,128)(2,1)S(1)}, u32[]{:S(2)}, u32[]{:S(2)}) %collective-permute-start.1) | collective-permute-done | bytes 393248 | tf_op jit(solution)/shard_map/ppermute | solution.py:552
  68.2 8.9 %collective-permute-done.2.refs_2_ = bf16[4,2,96,256]{3,2,1,0:T(8,128)(2,1)S(1)} collective-permute-done((bf16[4,2,96,256]{3,2,1,0:T(8,128)(2,1)}, bf16[4,2,96,256]{3,2,1,0:T(8,128)(2,1)S(1)}, u32[]{:S(2)}, u32[]{:S(2)}) %collective-permute-start.2) | collective-permute-done | bytes 393248 | tf_op jit(solution)/shard_map/ppermute | solution.py:552
  83.8 5.2 %all-to-all-start.3 = ((bf16[8,4,32,768]{3,2,1,0:T(8,128)(2,1)}), bf16[8,4,32,768]{3,2,1,0:T(8,128)(2,1)S(1)}, u32[]{:S(2)}, u32[]{:S(2)}) async-start(bf16[8,4,32,768]{3,2,1,0:T(8,128)(2,1)} %get-tuple-element.52), calls=%async_computation.3 | async-start | bytes 3145728 | tf_op jit(solution)/shard_map/all_to_all | solution.py:544
  89.1 20.5 %attend.1 = (bf16[4,96,256]{2,1,0:T(8,128)(2,1)}, bf16[4,96,256]{2,1,0:T(8,128)(2,1)}, bf16[4,96,256]{2,1,0:T(8,128)(2,1)}, bf16[4,4,2,96,256]{4,3,2,1,0:T(8,128...) custom-call(s32[1]{0:T(128)} %bitcast.1.me_ref, bf16[8,592,256]{2,1,0:T(8,128)(2,1)} %copy-done.4, ...), custom_call_target="tpu_custom_call" | custom-call | flops 17179869184 | bytes 20971520 | tf_op jit(solution)/shard_map/attend/pallas_call | solution.py:268
  112.8 5.1 %all-to-all-start.2 = ((bf16[8,2,256,256]{3,2,1,0:T(8,128)(2,1)}), bf16[8,2,256,256]{3,2,1,0:T(8,128)(2,1)}, u32[]{:S(2)}, u32[]{:S(2)}) async-start(bf16[8,2,256,256]{3,2,1,0:T(8,128)(2,1)} %get-tuple-element.46), calls=%async_computation.2 | async-start | bytes 4194304 | tf_op jit(solution)/shard_map/all_to_all | solution.py:544
  119.2 3.2 %fold.1 = (bf16[4,2,96,256]{3,2,1,0:T(8,128)(2,1)}, bf16[4,2,96,256]{3,2,1,0:T(8,128)(2,1)}, bf16[4,2,96,256]{3,2,1,0:T(8,128)(2,1)}, bf16[4,2,96,256]{3,2,1,0:T(8,128)(2,1)}) custom-call(bf16[4,4,2,96,256]{4,3,2,1,0:T(8,128)(2,1)} %get-tuple-element.50.own_ref, bf16[4,4,2,96,256]{4,3,2,1,0:T(8,128)(2,1)} %copy-done.6, bf16[8,4,32,768]{3,2,1,0:T(8,128)(2,1)} %copy-done.1), custom_call_target="tpu_custom_call" | custom-call | tf_op jit(solution)/shard_map/fold/pallas_call | solution.py:303
  126.3 8.3 %collective-permute-done.10.refs_2_ = bf16[4,2,96,256]{3,2,1,0:T(8,128)(2,1)S(1)} collective-permute-done((bf16[4,2,96,256]{3,2,1,0:T(8,128)(2,1)}, bf16[4,2,96,256]{3,2,1,0:T(8,128)(2,1)S(1)}, u32[]{:S(2)}, u32[]{:S(2)}) %collective-permute-start.10) | collective-permute-done | bytes 393248 | tf_op jit(solution)/shard_map/ppermute | solution.py:552
  134.6 9.1 %collective-permute-done.11.refs_3_ = bf16[4,2,96,256]{3,2,1,0:T(8,128)(2,1)S(1)} collective-permute-done((bf16[4,2,96,256]{3,2,1,0:T(8,128)(2,1)}, bf16[4,2,96,256]{3,2,1,0:T(8,128)(2,1)S(1)}, u32[]{:S(2)}, u32[]{:S(2)}) %collective-permute-start.11) | collective-permute-done | bytes 393248 | tf_op jit(solution)/shard_map/ppermute | solution.py:552
  144.7 5.1 %norm_part.1 = (bf16[8,4,32,896]{3,2,1,0:T(8,128)(2,1)}, bf16[4,384,256]{2,1,0:T(8,128)(2,1)}) custom-call(bf16[4,96,256]{2,1,0:T(8,128)(2,1)} %get-tuple-element.47.gated_ref, bf16[4,96,256]{2,1,0:T(8,128)(2,1)} %get-tuple-element.48.dq_ref, bf16[4,96,256]{2,1,0:T(8,128)(2,1)} %get-tuple-element.49.dg_ref, ...), custom_call_target="tpu_custom_call" | custom-call | tf_op jit(solution)/shard_map/norm_part/pallas_call | solution.py:345
  149.8 6.6 %all-to-all-start.4 = ((bf16[8,4,32,896]{3,2,1,0:T(8,128)(2,1)}), bf16[8,4,32,896]{3,2,1,0:T(8,128)(2,1)S(1)}, u32[]{:S(2)}, u32[]{:S(2)}) async-start(bf16[8,4,32,896]{3,2,1,0:T(8,128)(2,1)} %get-tuple-element.60), calls=%async_computation.4 | async-start | bytes 3670016 | tf_op jit(solution)/shard_map/all_to_all | solution.py:544
  157.0 5.4 %weight_part.1 = (bf16[8,64,768]{2,1,0:T(8,128)(2,1)}, f32[1,768]{1,0:T(1,128)}) custom-call(s32[1]{0:T(128)} %bitcast.8.place_ref, bf16[4,384,256]{2,1,0:T(8,128)(2,1)} %get-tuple-element.57.dcat_ref, bf16[4,96,256]{2,1,0:T(8,128)(2,1)} %get-tuple-element.47.gated_ref, bf16[8,176,768]{2,1,0:T(8,128)(2,1)} %copy-done, bf16[8,4,32,768]{3,2,1,0:T(8,128)(2,1)} %copy-done.1, ...), custom_call_target="tpu_custom_call" | custom-call | tf_op jit(solution)/shard_map/weight_part/pallas_call | solution.py:400
  164.5 10.0 %wpair_part.1 = f32[16,128]{1,0:T(8,128)} custom-call(bf16[8,2,256,256]{3,2,1,0:T(8,128)(2,1)} %all-to-all-done.2.db_ref, bf16[256,256,128]{2,1,0:T(8,128)(2,1)} %pair_ref.3), custom_call_target="tpu_custom_call" | custom-call | flops 4294967296 | bytes 20971520 | tf_op jit(solution)/shard_map/wpair_part/pallas_call | solution.py:524
  175.9 2.6 %collective-permute-start.13 = (f32[22,128]{1,0:T(8,128)S(1)}, f32[22,128]{1,0:T(8,128)S(1)}, u32[]{:S(2)}, u32[]{:S(2)}) collective-permute-start(f32[22,128]{1,0:T(8,128)S(1)} %pad_maximum_fusion.2), channel_id=1, source_target_pairs={{0,64},{32,96},{64,0},{96,32},{1,65},{33,97},{65,1},{97,33},{2,66}... | collective-permute-start | bytes 33800 | tf_op jit(solution)/shard_map/ppermute | solution.py:552
  179.4 3.2 %collective-permute-start.18 = (bf16[64,768]{1,0:T(8,128)(2,1)S(1)}, bf16[64,768]{1,0:T(8,128)(2,1)S(1)}, u32[]{:S(2)}, u32[]{:S(2)}) collective-permute-start(bf16[64,768]{1,0:T(8,128)(2,1)S(1)} %get-tuple-element.73), channel_id=1, source_target_pairs={{0,64},{32,96},{64,0},{96,32},{1,65},{33,97},{65,1},{97,33},{2,66}... | collective-permute-start | bytes 294920 | tf_op jit(solution)/shard_map/ppermute | solution.py:552
  190.3 7.5 %all-to-all-start.5 = ((f32[16,22,128]{2,1,0:T(8,128)}), f32[16,22,128]{2,1,0:T(8,128)S(1)}, u32[]{:S(2)}, u32[]{:S(2)}) async-start(f32[16,22,128]{2,1,0:T(8,128)} %broadcast_in_dim.25), calls=%async_computation.5 | async-start | bytes 393216 | tf_op jit(solution)/shard_map/all_to_all | solution.py:544
  201.7 3.4 %finish.1 = (bf16[4,32,768]{2,1,0:T(8,128)(2,1)}, bf16[4,32,768]{2,1,0:T(8,128)(2,1)}) custom-call(s32[1]{0:T(128)} %bitcast.core_ref, bf16[8,4,32,896]{3,2,1,0:T(8,128)(2,1)} %copy-done.2, bf16[8,48,768]{2,1,0:T(8,128)(2,1)} %copy-done.3, bf16[8,48,768]{2,1,0:T(8,128)(2,1)} %copy-done.5, bf16[4,32,768]{2,1,0:T(8,128)(2,1)} %act_ref.3, ...), custom_call_target="tpu_custom_call" | custom-call | tf_op jit(solution)/shard_map/finish/pallas_call | solution.py:450
  (111 shorter events, 48.4 us)
Async XLA Ops:
  3.3 36.7 %all-to-all-start = ((bf16[8,176,768]{2,1,0:T(8,128)(2,1)}), bf16[8,176,768]{2,1,0:T(8,128)(2,1)S(1)}, u32[]{:S(2)}, u32[]{:S(2)}) async-start(bf16[8,176,768]{2,1,0:T(8,128)(2,1)} %prepare.1), calls=%async_computation | async-start | bytes 4325376 | tf_op jit(solution)/shard_map/all_to_all | solution.py:544
  47.1 35.3 %all-to-all-start.1 = ((bf16[8,592,256]{2,1,0:T(8,128)(2,1)}), bf16[8,592,256]{2,1,0:T(8,128)(2,1)S(1)}, u32[]{:S(2)}, u32[]{:S(2)}) async-start(bf16[8,592,256]{2,1,0:T(8,128)(2,1)} %gated_grad.1), calls=%async_computation.1 | async-start | bytes 4849664 | tf_op jit(solution)/shard_map/all_to_all | solution.py:544
  55.6 10.6 %collective-permute-start.1 = (bf16[4,2,96,256]{3,2,1,0:T(8,128)(2,1)}, bf16[4,2,96,256]{3,2,1,0:T(8,128)(2,1)S(1)}, u32[]{:S(2)}, u32[]{:S(2)}) collective-permute-start(bf16[4,2,96,256]{3,2,1,0:T(8,128)(2,1)} %get-tuple-element.45.refs_0_), channel_id=1, source_target_pairs={{0,32},{32,0},{64,96},{96,64},{1,33},{33,1},{65,97},{97,65},{2,34}... | collective-permute-start | bytes 1179656 | tf_op jit(solution)/shard_map/ppermute | solution.py:552
  56.9 20.1 %collective-permute-start.2 = (bf16[4,2,96,256]{3,2,1,0:T(8,128)(2,1)}, bf16[4,2,96,256]{3,2,1,0:T(8,128)(2,1)S(1)}, u32[]{:S(2)}, u32[]{:S(2)}) collective-permute-start(bf16[4,2,96,256]{3,2,1,0:T(8,128)(2,1)} %get-tuple-element.45.refs_0_), channel_id=1, source_target_pairs={{0,64},{32,96},{64,0},{96,32},{1,65},{33,97},{65,1},{97,33},{2,66}... | collective-permute-start | bytes 1179656 | tf_op jit(solution)/shard_map/ppermute | solution.py:552
  59.5 19.6 %collective-permute-start.3 = (bf16[4,2,96,256]{3,2,1,0:T(8,128)(2,1)}, bf16[4,2,96,256]{3,2,1,0:T(8,128)(2,1)}, u32[]{:S(2)}, u32[]{:S(2)}) collective-permute-start(bf16[4,2,96,256]{3,2,1,0:T(8,128)(2,1)} %get-tuple-element.45.refs_0_), channel_id=1, source_target_pairs={{0,96},{32,64},{64,32},{96,0},{1,97},{33,65},{65,33},{97,1},{2,98}... | collective-permute-start | bytes 1179656 | tf_op jit(solution)/shard_map/ppermute | solution.py:552
  59.5 29.5 %collective-permute-start.4 = (bf16[4,2,96,256]{3,2,1,0:T(8,128)(2,1)}, bf16[4,2,96,256]{3,2,1,0:T(8,128)(2,1)}, u32[]{:S(2)}, u32[]{:S(2)}) collective-permute-start(bf16[4,2,96,256]{3,2,1,0:T(8,128)(2,1)} %get-tuple-element.45.refs_0_), channel_id=1, source_target_pairs={{0,16},{16,0},{1,17},{17,1},{2,18},{18,2},{3,19},{19,3},{4,20},{20... | collective-permute-start | bytes 1179656 | tf_op jit(solution)/shard_map/ppermute | solution.py:552
  66.3 22.8 %collective-permute-start.5 = (bf16[4,2,96,256]{3,2,1,0:T(8,128)(2,1)S(1)}, bf16[4,2,96,256]{3,2,1,0:T(8,128)(2,1)}, u32[]{:S(2)}, u32[]{:S(2)}) collective-permute-start(bf16[4,2,96,256]{3,2,1,0:T(8,128)(2,1)S(1)} %collective-permute-done.1.refs_1_), channel_id=1, source_target_pairs={{0,16},{16,0},{1,17},{17,1},{2,18},{18,2},{3,19},{19,3},{4,20},{20... | collective-permute-start | bytes 1179656 | tf_op jit(solution)/shard_map/ppermute | solution.py:552
  77.0 12.0 %collective-permute-start.6 = (bf16[4,2,96,256]{3,2,1,0:T(8,128)(2,1)S(1)}, bf16[4,2,96,256]{3,2,1,0:T(8,128)(2,1)}, u32[]{:S(2)}, u32[]{:S(2)}) collective-permute-start(bf16[4,2,96,256]{3,2,1,0:T(8,128)(2,1)S(1)} %collective-permute-done.2.refs_2_), channel_id=1, source_target_pairs={{0,16},{16,0},{1,17},{17,1},{2,18},{18,2},{3,19},{19,3},{4,20},{20... | collective-permute-start | bytes 1179656 | tf_op jit(solution)/shard_map/ppermute | solution.py:552
  79.2 9.9 %collective-permute-start.7 = (bf16[4,2,96,256]{3,2,1,0:T(8,128)(2,1)}, bf16[4,2,96,256]{3,2,1,0:T(8,128)(2,1)}, u32[]{:S(2)}, u32[]{:S(2)}) collective-permute-start(bf16[4,2,96,256]{3,2,1,0:T(8,128)(2,1)} %collective-permute-done.3.refs_3_), channel_id=1, source_target_pairs={{0,16},{16,0},{1,17},{17,1},{2,18},{18,2},{3,19},{19,3},{4,20},{20... | collective-permute-start | bytes 1179656 | tf_op jit(solution)/shard_map/ppermute | solution.py:552
  83.8 27.9 %all-to-all-start.3 = ((bf16[8,4,32,768]{3,2,1,0:T(8,128)(2,1)}), bf16[8,4,32,768]{3,2,1,0:T(8,128)(2,1)S(1)}, u32[]{:S(2)}, u32[]{:S(2)}) async-start(bf16[8,4,32,768]{3,2,1,0:T(8,128)(2,1)} %get-tuple-element.52), calls=%async_computation.3 | async-start | bytes 3145728 | tf_op jit(solution)/shard_map/all_to_all | solution.py:544
  109.5 8.5 %collective-permute-start.8 = (bf16[4,4,2,96,256]{4,3,2,1,0:T(8,128)(2,1)}, bf16[4,4,2,96,256]{4,3,2,1,0:T(8,128)(2,1)S(1)}, u32[]{:S(2)}, u32[]{:S(2)}) collective-permute-start(bf16[4,4,2,96,256]{4,3,2,1,0:T(8,128)(2,1)} %get-tuple-element.51), channel_id=1, source_target_pairs={{0,16},{16,0},{1,17},{17,1},{2,18},{18,2},{3,19},{19,3},{4,20},{20... | collective-permute-start | bytes 4718600 | tf_op jit(solution)/shard_map/ppermute | solution.py:552
  112.8 37.0 %all-to-all-start.2 = ((bf16[8,2,256,256]{3,2,1,0:T(8,128)(2,1)}), bf16[8,2,256,256]{3,2,1,0:T(8,128)(2,1)}, u32[]{:S(2)}, u32[]{:S(2)}) async-start(bf16[8,2,256,256]{3,2,1,0:T(8,128)(2,1)} %get-tuple-element.46), calls=%async_computation.2 | async-start | bytes 4194304 | tf_op jit(solution)/shard_map/all_to_all | solution.py:544
  122.5 12.2 %collective-permute-start.10 = (bf16[4,2,96,256]{3,2,1,0:T(8,128)(2,1)}, bf16[4,2,96,256]{3,2,1,0:T(8,128)(2,1)S(1)}, u32[]{:S(2)}, u32[]{:S(2)}) collective-permute-start(bf16[4,2,96,256]{3,2,1,0:T(8,128)(2,1)} %get-tuple-element.55), channel_id=1, source_target_pairs={{0,64},{32,96},{64,0},{96,32},{1,65},{33,97},{65,1},{97,33},{2,66}... | collective-permute-start | bytes 1179656 | tf_op jit(solution)/shard_map/ppermute | solution.py:552
  124.6 19.1 %collective-permute-start.11 = (bf16[4,2,96,256]{3,2,1,0:T(8,128)(2,1)}, bf16[4,2,96,256]{3,2,1,0:T(8,128)(2,1)S(1)}, u32[]{:S(2)}, u32[]{:S(2)}) collective-permute-start(bf16[4,2,96,256]{3,2,1,0:T(8,128)(2,1)} %get-tuple-element.56), channel_id=1, source_target_pairs={{0,96},{32,64},{64,32},{96,0},{1,97},{33,65},{65,33},{97,1},{2,98}... | collective-permute-start | bytes 1179656 | tf_op jit(solution)/shard_map/ppermute | solution.py:552
  125.4 18.3 %collective-permute-start.9 = (bf16[4,2,96,256]{3,2,1,0:T(8,128)(2,1)}, bf16[4,2,96,256]{3,2,1,0:T(8,128)(2,1)S(1)}, u32[]{:S(2)}, u32[]{:S(2)}) collective-permute-start(bf16[4,2,96,256]{3,2,1,0:T(8,128)(2,1)} %get-tuple-element.54), channel_id=1, source_target_pairs={{0,32},{32,0},{64,96},{96,64},{1,33},{33,1},{65,97},{97,65},{2,34}... | collective-permute-start | bytes 1179656 | tf_op jit(solution)/shard_map/ppermute | solution.py:552
  149.8 39.1 %all-to-all-start.4 = ((bf16[8,4,32,896]{3,2,1,0:T(8,128)(2,1)}), bf16[8,4,32,896]{3,2,1,0:T(8,128)(2,1)S(1)}, u32[]{:S(2)}, u32[]{:S(2)}) async-start(bf16[8,4,32,896]{3,2,1,0:T(8,128)(2,1)} %get-tuple-element.60), calls=%async_computation.4 | async-start | bytes 3670016 | tf_op jit(solution)/shard_map/all_to_all | solution.py:544
  163.5 15.7 %collective-permute-start.16 = (bf16[4,64,768]{2,1,0:T(8,128)(2,1)S(1)}, bf16[4,64,768]{2,1,0:T(8,128)(2,1)S(1)}, u32[]{:S(2)}, u32[]{:S(2)}) collective-permute-start(bf16[4,64,768]{2,1,0:T(8,128)(2,1)S(1)} %slice.29), channel_id=1, source_target_pairs={{0,16},{16,0},{1,17},{17,1},{2,18},{18,2},{3,19},{19,3},{4,20},{20... | collective-permute-start | bytes 1179656 | tf_op jit(solution)/shard_map/ppermute | solution.py:552
  175.3 7.2 %collective-permute-start.12 = (f32[22,128]{1,0:T(8,128)S(1)}, f32[22,128]{1,0:T(8,128)S(1)}, u32[]{:S(2)}, u32[]{:S(2)}) collective-permute-start(f32[22,128]{1,0:T(8,128)S(1)} %pad_maximum_fusion.2), channel_id=1, source_target_pairs={{0,32},{32,0},{64,96},{96,64},{1,33},{33,1},{65,97},{97,65},{2,34}... | collective-permute-start | bytes 33800 | tf_op jit(solution)/shard_map/ppermute | solution.py:552
  175.9 7.4 %collective-permute-start.13 = (f32[22,128]{1,0:T(8,128)S(1)}, f32[22,128]{1,0:T(8,128)S(1)}, u32[]{:S(2)}, u32[]{:S(2)}) collective-permute-start(f32[22,128]{1,0:T(8,128)S(1)} %pad_maximum_fusion.2), channel_id=1, source_target_pairs={{0,64},{32,96},{64,0},{96,32},{1,65},{33,97},{65,1},{97,33},{2,66}... | collective-permute-start | bytes 33800 | tf_op jit(solution)/shard_map/ppermute | solution.py:552
  179.4 7.0 %collective-permute-start.18 = (bf16[64,768]{1,0:T(8,128)(2,1)S(1)}, bf16[64,768]{1,0:T(8,128)(2,1)S(1)}, u32[]{:S(2)}, u32[]{:S(2)}) collective-permute-start(bf16[64,768]{1,0:T(8,128)(2,1)S(1)} %get-tuple-element.73), channel_id=1, source_target_pairs={{0,64},{32,96},{64,0},{96,32},{1,65},{33,97},{65,1},{97,33},{2,66}... | collective-permute-start | bytes 294920 | tf_op jit(solution)/shard_map/ppermute | solution.py:552
  189.0 8.7 %collective-permute-start.20 = (bf16[64,768]{1,0:T(8,128)(2,1)S(1)}, bf16[64,768]{1,0:T(8,128)(2,1)S(1)}, u32[]{:S(2)}, u32[]{:S(2)}) collective-permute-start(bf16[64,768]{1,0:T(8,128)(2,1)S(1)} %fusion.2), channel_id=1, source_target_pairs={{0,1},{1,0},{2,3},{3,2},{4,5},{5,4},{6,7},{7,6},{8,9},{9,8},{10,11... | collective-permute-start | bytes 294920 | tf_op jit(solution)/shard_map/ppermute | solution.py:552
  190.3 14.8 %all-to-all-start.5 = ((f32[16,22,128]{2,1,0:T(8,128)}), f32[16,22,128]{2,1,0:T(8,128)S(1)}, u32[]{:S(2)}, u32[]{:S(2)}) async-start(f32[16,22,128]{2,1,0:T(8,128)} %broadcast_in_dim.25), calls=%async_computation.5 | async-start | bytes 393216 | tf_op jit(solution)/shard_map/all_to_all | solution.py:544
  197.8 7.3 %collective-permute-start.21 = (bf16[64,768]{1,0:T(8,128)(2,1)S(1)}, bf16[64,768]{1,0:T(8,128)(2,1)S(1)}, u32[]{:S(2)}, u32[]{:S(2)}) collective-permute-start(bf16[64,768]{1,0:T(8,128)(2,1)S(1)} %add_convert_fusion.1), channel_id=1, source_target_pairs={{0,32},{32,0},{64,96},{96,64},{1,33},{33,1},{65,97},{97,65},{2,34}... | collective-permute-start | bytes 294920 | tf_op jit(solution)/shard_map/ppermute | solution.py:552
  197.9 7.3 %collective-permute-start.22 = (bf16[64,768]{1,0:T(8,128)(2,1)S(1)}, bf16[64,768]{1,0:T(8,128)(2,1)S(1)}, u32[]{:S(2)}, u32[]{:S(2)}) collective-permute-start(bf16[64,768]{1,0:T(8,128)(2,1)S(1)} %add_convert_fusion.1), channel_id=1, source_target_pairs={{0,64},{32,96},{64,0},{96,32},{1,65},{33,97},{65,1},{97,33},{2,66}... | collective-permute-start | bytes 294920 | tf_op jit(solution)/shard_map/ppermute | solution.py:552
  (28 other events, 182.4 us)
